TPU v7x, 128 devices: a whole 4x4x4 slice. The times are simulated.
128 devices in a mesh: row: 16 (over y_lo, x, core), col: 8 (over z, y_hi).
Axes of the slice: x: 4, y: 4 (y_hi: 2, y_lo: 2; y = y_hi * 2 + y_lo), z: 4, core: 2. Of those that a mesh axis runs over, the one named last changes fastest.
Arguments:
- object_field: float32 [4, 2, 2048, 4096], P(None, None, 'row', 'col'), may hold values from -4 to 4
- probe_field: float32 [2, 128, 128], replicated, may hold values from -6 to 6
- propagator_phase: float32 [128, 128], replicated, may hold values from -3.140625 to 3.140625
- position_rows: int32 [16, 8, 4], P('row', 'col'), may hold values from 0 to 128
- position_cols: int32 [16, 8, 4], P('row', 'col'), may hold values from 0 to 512
- tile_counts: int32 [16, 8], P('row', 'col'), may hold values from 0 to 4, as said below
- intensities: float32 [16, 8, 4, 128, 128], P('row', 'col'), may hold values from 0.2 to 8
- conv_weight: float32 [3, 9, 32, 4], replicated, may hold values from -1 to 1
- conv_bias: float32 [3, 32], replicated, may hold values from -3 to 3
- output_weight: float32 [3, 4, 32], replicated, may hold values from -1 to 1
- output_bias: float32 [3, 4], replicated, may hold values from -2 to 2
Outputs:
- denoised: float32 [4, 2, 2048, 4096], P(None, None, 'row', 'col')
Inputs may be any that keep to these rules, and one draw needn't show every extreme that they name: For every column of tiles and every r < 8, tiles r and r + 8 hold 4 positions together; a tile uses its first tile_counts slots of position_rows, position_cols and intensities.
All inputs are finite; a program needn't handle non-finite values.
Results may differ from a plain program's by a relative error of at most 0.0003.
Values sent between devices are 32-bit elements; how exact they have to be, the bound alone decides.
No kernel may reach another device: no remote copies, remote signals or barrier semaphores. Data moves between devices by JAX's collectives and lax.ppermute only.
A program may use at most 128 MiB of HBM per device.

v0:
```python
import jax
import jax.numpy as jnp
from jax import lax
from jax.sharding import PartitionSpec as P

step_size = 0.02


def padded(cells, sides, width):
    for axis, dim in sides:
        count = lax.axis_size(axis)
        ends = count - 1
        head = lax.slice_in_dim(cells, 0, width, axis=dim)
        tail = lax.slice_in_dim(cells, cells.shape[dim] - width, cells.shape[dim], axis=dim)
        cells = jnp.concatenate(
            [
                lax.ppermute(tail, axis, [(i, (i + 1) % count) for i in range(ends)]),
                cells,
                lax.ppermute(head, axis, [((i + 1) % count, i) for i in range(ends)]),
            ],
            axis=dim,
        )
    return cells


def dft_tables(length):
    index = jnp.arange(length, dtype=jnp.int32)
    product = index[:, None] * index[None, :] % length
    angle = 2.0 * jnp.pi / length * product.astype(jnp.float32)
    scale_factor = 1.0 / jnp.sqrt(jnp.float32(length))
    return (jnp.cos(angle) * scale_factor, jnp.sin(angle) * scale_factor)


def matmul(left, right):
    return jnp.dot(left, right, precision=lax.Precision.HIGHEST)


def transform(real_part, imag_part, cosine, sine, direction):
    left_re = matmul(cosine, real_part) + direction * matmul(sine, imag_part)
    left_im = matmul(cosine, imag_part) - direction * matmul(sine, real_part)
    out_re = matmul(left_re, cosine) + direction * matmul(left_im, sine)
    out_im = matmul(left_im, cosine) - direction * matmul(left_re, sine)
    return (out_re, out_im)


def slot_loss(patch, measured, probe_field, phase_re, phase_im, cosine, sine):
    wave_re = probe_field[0]
    wave_im = probe_field[1]
    slices = patch.shape[0]
    for slice_index in range(slices):
        obj_re = patch[slice_index, 0]
        obj_im = patch[slice_index, 1]
        wave_re, wave_im = (
            wave_re * obj_re - wave_im * obj_im,
            wave_re * obj_im + wave_im * obj_re,
        )
        if slice_index + 1 < slices:
            spec_re, spec_im = transform(wave_re, wave_im, cosine, sine, 1.0)
            spec_re, spec_im = (
                spec_re * phase_re - spec_im * phase_im,
                spec_re * phase_im + spec_im * phase_re,
            )
            wave_re, wave_im = transform(spec_re, spec_im, cosine, sine, -1.0)
    far_re, far_im = transform(wave_re, wave_im, cosine, sine, 1.0)
    mismatch = far_re * far_re + far_im * far_im - measured
    return 0.5 * jnp.sum(mismatch * mismatch)


def batched_gradient(patches, measured, probe_field, phase_re, phase_im, cosine, sine):
    mapped = jax.vmap(jax.grad(slot_loss), in_axes=(0, 0, None, None, None, None, None))
    return mapped(patches, measured, probe_field, phase_re, phase_im, cosine, sine)


def coupling_term(cond_pad, kernel, hidden_bias, out_map, out_bias):
    extent_rows = cond_pad.shape[1] - 2
    extent_cols = cond_pad.shape[2] - 2
    tap_list = [
        cond_pad[:, shift_row : shift_row + extent_rows, shift_col : shift_col + extent_cols]
        for shift_row in range(3)
        for shift_col in range(3)
    ]
    stacked = jnp.concatenate(tap_list, axis=0)
    flat_kernel = jnp.transpose(kernel, (1, 0, 2)).reshape(kernel.shape[1], -1)
    hidden = (
        jnp.einsum("ok,khw->ohw", flat_kernel, stacked, precision=lax.Precision.HIGHEST)
        + hidden_bias[:, None, None]
    )
    hidden = jax.nn.silu(hidden)
    return (
        jnp.einsum("co,ohw->chw", out_map, hidden, precision=lax.Precision.HIGHEST)
        + out_bias[:, None, None]
    )


def per_device(
    object_field,
    probe_field,
    propagator_phase,
    position_rows,
    position_cols,
    tile_counts,
    intensities,
    conv_weight,
    conv_bias,
    output_weight,
    output_bias,
):
    slices = object_field.shape[0]
    tile_rows = object_field.shape[2]
    tile_cols = object_field.shape[3]
    probe_len = probe_field.shape[1]
    margin = probe_len // 2
    layer_total = conv_weight.shape[0]
    cosine, sine = dft_tables(probe_len)
    phase_re = jnp.cos(propagator_phase)
    phase_im = jnp.sin(propagator_phase)
    zero_index = jnp.int32(0)
    extended = padded(object_field, (("row", 2), ("col", 3)), margin)
    rows_here = position_rows.reshape(-1)
    cols_here = position_cols.reshape(-1)
    count_here = tile_counts.reshape(())
    measured = intensities.reshape((-1, probe_len, probe_len))
    slot_total = rows_here.shape[0]

    def cut_patch(row_offset, col_offset):
        return lax.dynamic_slice(
            extended,
            (zero_index, zero_index, row_offset, col_offset),
            (slices, 2, probe_len, probe_len),
        )

    patches = jax.vmap(cut_patch)(rows_here, cols_here)
    grads = batched_gradient(patches, measured, probe_field, phase_re, phase_im, cosine, sine)
    alive = jnp.arange(slot_total, dtype=jnp.int32) < count_here
    grads = jnp.where(alive[:, None, None, None, None], grads, 0.0)

    def add_slot(slot, accum):
        start = (zero_index, zero_index, rows_here[slot], cols_here[slot])
        current = lax.dynamic_slice(accum, start, (slices, 2, probe_len, probe_len))
        return lax.dynamic_update_slice(accum, current + grads[slot], start)

    accum = lax.fori_loop(0, slot_total, add_slot, jnp.zeros_like(extended))
    edges = jnp.concatenate([accum[:, :, :margin], accum[:, :, -margin:]], axis=2)
    framed = padded(edges, (("row", 2),), margin)
    inner = accum[:, :, margin:-margin]
    inner = inner.at[:, :, :margin].add(framed[:, :, :margin])
    inner = inner.at[:, :, -margin:].add(framed[:, :, -margin:])
    sides = jnp.concatenate([inner[:, :, :, :margin], inner[:, :, :, -margin:]], axis=3)
    framed_cols = padded(sides, (("col", 3),), margin)
    gradient = inner[:, :, :, margin:-margin]
    gradient = gradient.at[:, :, :, :margin].add(framed_cols[:, :, :, :margin])
    gradient = gradient.at[:, :, :, -margin:].add(framed_cols[:, :, :, -margin:])
    updated = object_field - step_size * gradient
    channels = updated.reshape(2 * slices, tile_rows, tile_cols)
    lower = channels[:slices]
    upper = channels[slices:]
    for layer_index in range(layer_total):
        cond = lower if layer_index % 2 == 0 else upper
        cond_pad = padded(cond, (("row", 1), ("col", 2)), 1)
        term = coupling_term(
            cond_pad,
            conv_weight[layer_index],
            conv_bias[layer_index],
            output_weight[layer_index],
            output_bias[layer_index],
        )
        if layer_index % 2 == 0:
            upper = upper + term
        else:
            lower = lower + term
    return jnp.concatenate([lower, upper], axis=0).reshape(slices, 2, tile_rows, tile_cols)


def solution(mesh):
    placed = (
        P(None, None, "row", "col"),
        P(),
        P(),
        P("row", "col", None),
        P("row", "col", None),
        P("row", "col"),
        P("row", "col", None, None, None),
        P(),
        P(),
        P(),
        P(),
    )
    return jax.shard_map(
        per_device,
        mesh=mesh,
        in_specs=placed,
        out_specs=P(None, None, "row", "col"),
        check_vma=False,
    )
```

profile of v0, /device:TPU:7, one launch (start us, length us, event | category | flops | bytes accessed | tf_op | source)
XLA Modules:
  0.0 525.3 jit_solution(8117811715718217090)
XLA Ops:
  12.2 6.8 %collective-permute-done = f32[4,2,64,512]{3,2,1,0:T(8,128)} collective-permute-done((f32[4,2,64,512]{3,2,1,0:T(8,128)}, f32[4,2,64,512]{3,2,1,0:T(8,128)}, u32[]{:S(2)}, u32[]{:S(2)}) %collective-permute-start) | collective-permute-done | bytes 1048608 | tf_op jit(solution)/shard_map/ppermute | solution.py:17
  35.7 9.0 %collective-permute-done.2 = f32[4,2,256,64]{2,3,1,0:T(8,128)S(1)} collective-permute-done((f32[4,2,256,64]{2,3,1,0:T(8,128)S(1)}, f32[4,2,256,64]{2,3,1,0:T(8,128)S(1)}, u32[]{:S(2)}, u32[]{:S(2)}) %collective-permute-start.2) | collective-permute-done | bytes 524320 | tf_op jit(solution)/shard_map/ppermute | solution.py:17
  44.6 13.1 %collective-permute-done.3 = f32[4,2,256,64]{2,3,1,0:T(8,128)S(1)} collective-permute-done((f32[4,2,256,64]{2,3,1,0:T(8,128)S(1)}, f32[4,2,256,64]{2,3,1,0:T(8,128)S(1)}, u32[]{:S(2)}, u32[]{:S(2)}) %collective-permute-start.3) | collective-permute-done | bytes 524320 | tf_op jit(solution)/shard_map/ppermute | solution.py:19
  61.4 18.1 %while.21 = (s32[]{:T(128)}, f32[4,2,256,640]{2,3,1,0:T(8,128)}, s32[4,4]{1,0:T(4,128)S(1)}, f32[4,4,2,128,128]{4,3,0,2,1:T(8,128)}) while((s32[]{:T(128)}, f32[4,2,256,640]{2,3,1,0:T(8,128)}, s32[4,4]{1,0:T(4,128)S(1)}, f32[4,4,2,128,128]{4,3,0,2,1:T(8,128)}) %tuple.132), condition=%wide.while_cond.4.clone, body=%wide.while_body.4.sunk.clone | while | flops 2 | bytes 3146353 | solution.py:126
  164.2 55.7 %while.20 = (s32[]{:T(128)}, f32[4,2,256,640]{3,2,1,0:T(8,128)}, s32[4]{0:T(128)S(1)}, s32[4]{0:T(128)S(1)}, f32[4,4,2,128,128]{4,3,0,2,1:T(8,128)}) while((s32[]{:T(128)}, f32[4,2,256,640]{3,2,1,0:T(8,128)}, s32[4]{0:T(128)S(1)}, s32[4]{0:T(128)S(1)}, f32[4,4,2,128,128]{4,3,0,2,1:T(8,128)}) %tuple.139), condition=%wide.region_1.2_spmd.clone, body=%wide.region_0.1_spmd.sunk.clone | while | flops 131080 | bytes 2621609 | solution.py:142
  171.2 7.5 %dynamic_update_slice.9 = f32[4,2,256,640]{3,2,1,0:T(8,128)} dynamic-update-slice(f32[4,2,256,640]{3,2,1,0:T(8,128)} %get-tuple-element.414, f32[4,2,128,128]{3,2,1,0:T(8,128)S(1)} %bitcast_add_fusion.3, s32[]{:T(128)} %constant.168.clone.1..sunk.1, s32[]{:T(128)} %constant.168.clone.1..sunk.1, s32[]{:T(128)S(6)} %select_n.646, s32[]{:T(128)S(6)} %select_n.647) | dynamic-update-slice | bytes 1048580 | tf_op jit(solution)/shard_map/while/body/eval_jaxpr/dynamic_update_slice | solution.py:140
  185.2 7.7 %dynamic_update_slice.9 = f32[4,2,256,640]{3,2,1,0:T(8,128)} dynamic-update-slice(f32[4,2,256,640]{3,2,1,0:T(8,128)} %get-tuple-element.414, f32[4,2,128,128]{3,2,1,0:T(8,128)S(1)} %bitcast_add_fusion.3, s32[]{:T(128)} %constant.168.clone.1..sunk.1, s32[]{:T(128)} %constant.168.clone.1..sunk.1, s32[]{:T(128)S(6)} %select_n.646, s32[]{:T(128)S(6)} %select_n.647) | dynamic-update-slice | bytes 1048580 | tf_op jit(solution)/shard_map/while/body/eval_jaxpr/dynamic_update_slice | solution.py:140
  199.5 6.9 %dynamic_update_slice.9 = f32[4,2,256,640]{3,2,1,0:T(8,128)} dynamic-update-slice(f32[4,2,256,640]{3,2,1,0:T(8,128)} %get-tuple-element.414, f32[4,2,128,128]{3,2,1,0:T(8,128)S(1)} %bitcast_add_fusion.3, s32[]{:T(128)} %constant.168.clone.1..sunk.1, s32[]{:T(128)} %constant.168.clone.1..sunk.1, s32[]{:T(128)S(6)} %select_n.646, s32[]{:T(128)S(6)} %select_n.647) | dynamic-update-slice | bytes 1048580 | tf_op jit(solution)/shard_map/while/body/eval_jaxpr/dynamic_update_slice | solution.py:140
  213.0 6.9 %dynamic_update_slice.9 = f32[4,2,256,640]{3,2,1,0:T(8,128)} dynamic-update-slice(f32[4,2,256,640]{3,2,1,0:T(8,128)} %get-tuple-element.414, f32[4,2,128,128]{3,2,1,0:T(8,128)S(1)} %bitcast_add_fusion.3, s32[]{:T(128)} %constant.168.clone.1..sunk.1, s32[]{:T(128)} %constant.168.clone.1..sunk.1, s32[]{:T(128)S(6)} %select_n.646, s32[]{:T(128)S(6)} %select_n.647) | dynamic-update-slice | bytes 1048580 | tf_op jit(solution)/shard_map/while/body/eval_jaxpr/dynamic_update_slice | solution.py:140
  228.7 12.4 %collective-permute-done.4 = f32[4,2,64,640]{3,2,1,0:T(8,128)S(1)} collective-permute-done((f32[4,2,64,640]{3,2,1,0:T(8,128)S(1)}, f32[4,2,64,640]{3,2,1,0:T(8,128)S(1)}, u32[]{:S(2)}, u32[]{:S(2)}) %collective-permute-start.4) | collective-permute-done | bytes 1310752 | tf_op jit(solution)/shard_map/ppermute | solution.py:17
  241.3 6.4 %collective-permute-done.5 = f32[4,2,64,640]{3,2,1,0:T(8,128)S(1)} collective-permute-done((f32[4,2,64,640]{3,2,1,0:T(8,128)S(1)}, f32[4,2,64,640]{3,2,1,0:T(8,128)S(1)}, u32[]{:S(2)}, u32[]{:S(2)}) %collective-permute-start.5) | collective-permute-done | bytes 1310752 | tf_op jit(solution)/shard_map/ppermute | solution.py:19
  265.0 10.0 %collective-permute-done.7 = f32[4,2,128,64]{3,2,1,0:T(8,128)} collective-permute-done((f32[4,2,128,64]{3,2,1,0:T(8,128)}, f32[4,2,128,64]{3,2,1,0:T(8,128)}, u32[]{:S(2)}, u32[]{:S(2)}) %collective-permute-start.7) | collective-permute-done | bytes 262176 | tf_op jit(solution)/shard_map/ppermute | solution.py:19
  304.3 7.0 %collective-permute-done.11 = f32[4,130,1]{2,0,1:T(4,128)S(1)} collective-permute-done((f32[4,130,1]{2,0,1:T(4,128)S(1)}, f32[4,130,1]{2,0,1:T(4,128)S(1)}, u32[]{:S(2)}, u32[]{:S(2)}) %collective-permute-start.11) | collective-permute-done | bytes 2112 | tf_op jit(solution)/shard_map/ppermute | solution.py:19
  311.3 6.2 %pad_maximum_fusion.8 = (f32[4,128,512]{2,0,1:T(4,128)}, f32[4,128,512]{2,0,1:T(4,128)}, f32[4,128,512]{2,0,1:T(4,128)}, f32[4,128,512]{2,0,1:T(4,128)}, f32[4,128,512]{2,0,1:T(4,128)}, /*index=5*/f32[4,128,512]{2,0,1:T(4,128)}) fusion(f32[4,130,1]{2,0,1:T(4,128)S(1)} %collective-permute-done.11, f32[4,130,512]{2,0,1:T(4,128)S(1)} %constant_dynamic-update-slice_fusion, ...), kind=kLoop, calls=%fused_computation.152 | loop fusion | flops 1572864 | bytes 7360576 | tf_op jit(solution)/shard_map/concatenate | solution.py:15
  317.5 29.0 %concatenate.97 = f32[36,128,512]{2,0,1:T(8,128)} concatenate(f32[4,128,512]{2,0,1:T(4,128)} %get-tuple-element.261, f32[4,128,512]{2,0,1:T(4,128)} %get-tuple-element.274, f32[4,128,512]{2,0,1:T(4,128)} %get-tuple-element.247, f32[4,128,512]{2,0,1:T(4,128)} %get-tuple-element.260, f32[4,128,512]{2,0,1:T(4,128)S(1)} %copy.383, f32[4,128,512]{2,0,1:T(4,128)} %get-tuple-element.248, ...), dimensions={0} | concatenate | bytes 18874368 | tf_op jit(solution)/shard_map/concatenate | solution.py:82
  346.5 13.0 %fusion.308 = f32[128,512,32]{1,2,0:T(8,128)S(1)} fusion(f32[36,128,512]{2,0,1:T(8,128)} %concatenate.97, f32[32,36]{0,1:T(8,128)S(1)} %reshape.242), kind=kOutput, calls=%fused_computation.469 | convolution fusion | flops 905969664 | bytes 17830400 | tf_op jit(solution)/shard_map/ok,khw->ohw/dot_general | solution.py:85
  359.5 6.7 %fusion.27 = f32[4,128,512]{2,0,1:T(4,128)S(1)} fusion(f32[128,512,32]{1,2,0:T(8,128)S(1)} %fusion.308, f32[32]{0:T(128)S(1)} %get-tuple-element.302, f32[4,128,512]{2,1,0:T(8,128)S(1)} %bitcast.704, f32[4]{0:T(128)S(1)} %get-tuple-element.299, f32[3,4,32]{2,1,0:T(4,128)S(1)} %copy-done.15), kind=kOutput, calls=%fused_computation.55 | convolution fusion | flops 111673344 | bytes 10488832 | tf_op jit(solution)/shard_map/co,ohw->chw/dot_general | solution.py:90
  396.1 29.4 %concatenate.103 = f32[36,128,512]{2,0,1:T(8,128)} concatenate(f32[4,128,512]{2,0,1:T(4,128)} %get-tuple-element.245, f32[4,128,512]{2,0,1:T(4,128)} %get-tuple-element.270, f32[4,128,512]{2,0,1:T(4,128)} %get-tuple-element.242, f32[4,128,512]{2,0,1:T(4,128)} %get-tuple-element.244, f32[4,128,512]{2,0,1:T(4,128)S(1)} %fusion.27, f32[4,128,512]{2,0,1:T(4,128)} %get-tuple-element.241, ...), dimensions={0} | concatenate | bytes 18874368 | tf_op jit(solution)/shard_map/concatenate | solution.py:82
  425.5 12.7 %fusion.306 = f32[128,512,32]{1,2,0:T(8,128)S(1)} fusion(f32[36,128,512]{2,0,1:T(8,128)} %concatenate.103, f32[32,36]{0,1:T(8,128)S(1)} %reshape.243), kind=kOutput, calls=%fused_computation.467 | convolution fusion | flops 905969664 | bytes 17830400 | tf_op jit(solution)/shard_map/ok,khw->ohw/dot_general | solution.py:85
  438.2 6.6 %fusion.24 = f32[4,128,512]{2,0,1:T(4,128)S(1)} fusion(f32[128,512,32]{1,2,0:T(8,128)S(1)} %fusion.306, f32[32]{0:T(128)S(1)} %get-tuple-element.303, f32[4]{0:T(128)S(1)} %get-tuple-element.300, f32[3,4,32]{2,1,0:T(4,128)S(1)} %copy-done.15, f32[4,128,512]{2,1,0:T(8,128)S(1)} %bitcast.703), kind=kOutput, calls=%fused_computation.52 | convolution fusion | flops 111673344 | bytes 10488832 | tf_op jit(solution)/shard_map/co,ohw->chw/dot_general | solution.py:90
  461.8 6.2 %collective-permute-done.19 = f32[4,130,1]{2,0,1:T(4,128)S(1)} collective-permute-done((f32[4,130,1]{2,0,1:T(4,128)S(1)}, f32[4,130,1]{2,0,1:T(4,128)S(1)}, u32[]{:S(2)}, u32[]{:S(2)}) %collective-permute-start.19) | collective-permute-done | bytes 2112 | tf_op jit(solution)/shard_map/ppermute | solution.py:19
  474.1 29.1 %concatenate.109 = f32[36,128,512]{2,0,1:T(8,128)} concatenate(f32[4,128,512]{2,0,1:T(4,128)} %get-tuple-element.239, f32[4,128,512]{2,0,1:T(4,128)} %get-tuple-element.266, f32[4,128,512]{2,0,1:T(4,128)} %get-tuple-element.236, f32[4,128,512]{2,0,1:T(4,128)} %get-tuple-element.238, f32[4,128,512]{2,0,1:T(4,128)S(1)} %fusion.24, f32[4,128,512]{2,0,1:T(4,128)} %get-tuple-element.235, ...), dimensions={0} | concatenate | bytes 18874368 | tf_op jit(solution)/shard_map/concatenate | solution.py:82
  503.2 12.7 %fusion.304 = f32[128,512,32]{1,2,0:T(8,128)S(1)} fusion(f32[36,128,512]{2,0,1:T(8,128)} %concatenate.109, f32[32,36]{0,1:T(8,128)S(1)} %reshape.244), kind=kOutput, calls=%fused_computation.465 | convolution fusion | flops 905969664 | bytes 17830400 | tf_op jit(solution)/shard_map/ok,khw->ohw/dot_general | solution.py:85
  515.8 6.3 %fusion.21 = f32[4,128,512]{2,0,1:T(4,128)S(1)} fusion(f32[4,128,512]{2,0,1:T(4,128)S(1)} %fusion.27, f32[128,512,32]{1,2,0:T(8,128)S(1)} %fusion.304, f32[32]{0:T(128)S(1)} %get-tuple-element.301, f32[4]{0:T(128)S(1)} %get-tuple-element.298, f32[3,4,32]{2,1,0:T(4,128)S(1)} %copy-done.15), kind=kOutput, calls=%fused_computation.49 | convolution fusion | flops 111673344 | bytes 10488832 | tf_op jit(solution)/shard_map/co,ohw->chw/dot_general | solution.py:90
  (267 shorter events, 255.8 us)
Async XLA Ops:
  3.3 15.7 %collective-permute-start = (f32[4,2,64,512]{3,2,1,0:T(8,128)}, f32[4,2,64,512]{3,2,1,0:T(8,128)}, u32[]{:S(2)}, u32[]{:S(2)}) collective-permute-start(f32[4,2,64,512]{3,2,1,0:T(8,128)} %get-tuple-element.232), channel_id=1, source_target_pairs={{0,8},{8,16},{16,24},{24,32},{32,40},{40,48},{48,56},{56,64},{64,7... | collective-permute-start | bytes 3145736 | tf_op jit(solution)/shard_map/ppermute | solution.py:17
  7.0 18.7 %collective-permute-start.1 = (f32[4,2,64,512]{3,2,1,0:T(8,128)}, f32[4,2,64,512]{3,2,1,0:T(8,128)S(1)}, u32[]{:S(2)}, u32[]{:S(2)}) collective-permute-start(f32[4,2,64,512]{3,2,1,0:T(8,128)} %get-tuple-element.233), channel_id=1, source_target_pairs={{8,0},{16,8},{24,16},{32,24},{40,32},{48,40},{56,48},{64,56},{72,6... | collective-permute-start | bytes 3145736 | tf_op jit(solution)/shard_map/ppermute | solution.py:19
  27.6 30.1 %copy-start.2 = (f32[4,2,128,512]{2,3,1,0:T(8,128)S(1)}, f32[4,2,128,512]{2,3,1,0:T(8,128)}, u32[]{:S(2)}) copy-start(f32[4,2,128,512]{2,3,1,0:T(8,128)} %copy.245) | copy-start | bytes 6291460
  27.6 30.1 %copy-start.3 = (f32[4,2,64,512]{2,3,1,0:T(8,128)S(1)}, f32[4,2,64,512]{2,3,1,0:T(8,128)}, u32[]{:S(2)}) copy-start(f32[4,2,64,512]{2,3,1,0:T(8,128)} %copy.244) | copy-start | bytes 3145732
  27.6 30.1 %copy-start.4 = (f32[4,2,64,512]{2,3,1,0:T(8,128)S(1)}, f32[4,2,64,512]{2,3,1,0:T(8,128)}, u32[]{:S(2)}) copy-start(f32[4,2,64,512]{2,3,1,0:T(8,128)} %copy.246) | copy-start | bytes 3145732
  29.6 15.0 %collective-permute-start.2 = (f32[4,2,256,64]{2,3,1,0:T(8,128)S(1)}, f32[4,2,256,64]{2,3,1,0:T(8,128)S(1)}, u32[]{:S(2)}, u32[]{:S(2)}) collective-permute-start(f32[4,2,256,64]{2,3,1,0:T(8,128)S(1)} %get-tuple-element.212), channel_id=1, source_target_pairs={{0,1},{1,2},{2,3},{3,4},{4,5},{5,6},{6,7},{8,9},{9,10},{10,11},{11... | collective-permute-start | bytes 1572872 | tf_op jit(solution)/shard_map/ppermute | solution.py:17
  34.3 23.5 %collective-permute-start.3 = (f32[4,2,256,64]{2,3,1,0:T(8,128)S(1)}, f32[4,2,256,64]{2,3,1,0:T(8,128)S(1)}, u32[]{:S(2)}, u32[]{:S(2)}) collective-permute-start(f32[4,2,256,64]{2,3,1,0:T(8,128)S(1)} %get-tuple-element.213), channel_id=1, source_target_pairs={{1,0},{2,1},{3,2},{4,3},{5,4},{6,5},{7,6},{9,8},{10,9},{11,10},{12... | collective-permute-start | bytes 1572872 | tf_op jit(solution)/shard_map/ppermute | solution.py:19
  222.0 19.2 %collective-permute-start.4 = (f32[4,2,64,640]{3,2,1,0:T(8,128)S(1)}, f32[4,2,64,640]{3,2,1,0:T(8,128)S(1)}, u32[]{:S(2)}, u32[]{:S(2)}) collective-permute-start(f32[4,2,64,640]{3,2,1,0:T(8,128)S(1)} %get-tuple-element.215), channel_id=1, source_target_pairs={{0,8},{8,16},{16,24},{24,32},{32,40},{40,48},{48,56},{56,64},{64,7... | collective-permute-start | bytes 3932168 | tf_op jit(solution)/shard_map/ppermute | solution.py:17
  226.6 21.1 %collective-permute-start.5 = (f32[4,2,64,640]{3,2,1,0:T(8,128)S(1)}, f32[4,2,64,640]{3,2,1,0:T(8,128)S(1)}, u32[]{:S(2)}, u32[]{:S(2)}) collective-permute-start(f32[4,2,64,640]{3,2,1,0:T(8,128)S(1)} %get-tuple-element.214), channel_id=1, source_target_pairs={{8,0},{16,8},{24,16},{32,24},{40,32},{48,40},{56,48},{64,56},{72,6... | collective-permute-start | bytes 3932168 | tf_op jit(solution)/shard_map/ppermute | solution.py:19
  249.0 12.3 %collective-permute-start.6 = (f32[4,2,128,64]{3,2,1,0:T(8,128)S(1)}, f32[4,2,128,64]{3,2,1,0:T(8,128)S(1)}, u32[]{:S(2)}, u32[]{:S(2)}) collective-permute-start(f32[4,2,128,64]{3,2,1,0:T(8,128)S(1)} %get-tuple-element.217), channel_id=1, source_target_pairs={{0,1},{1,2},{2,3},{3,4},{4,5},{5,6},{6,7},{8,9},{9,10},{10,11},{11... | collective-permute-start | bytes 786440 | tf_op jit(solution)/shard_map/ppermute | solution.py:17
  254.8 20.1 %collective-permute-start.7 = (f32[4,2,128,64]{3,2,1,0:T(8,128)}, f32[4,2,128,64]{3,2,1,0:T(8,128)}, u32[]{:S(2)}, u32[]{:S(2)}) collective-permute-start(f32[4,2,128,64]{3,2,1,0:T(8,128)} %get-tuple-element.216), channel_id=1, source_target_pairs={{1,0},{2,1},{3,2},{4,3},{5,4},{6,5},{7,6},{9,8},{10,9},{11,10},{12... | collective-permute-start | bytes 786440 | tf_op jit(solution)/shard_map/ppermute | solution.py:19
  283.9 7.5 %collective-permute-start.8 = (f32[4,1,512]{2,0,1:T(4,128)S(1)}, f32[4,1,512]{2,0,1:T(4,128)S(1)}, u32[]{:S(2)}, u32[]{:S(2)}) collective-permute-start(f32[4,1,512]{2,0,1:T(4,128)S(1)} %get-tuple-element.276), channel_id=1, source_target_pairs={{0,8},{8,16},{16,24},{24,32},{32,40},{40,48},{48,56},{56,64},{64,7... | collective-permute-start | bytes 24584 | tf_op jit(solution)/shard_map/ppermute | solution.py:17
  289.5 7.2 %collective-permute-start.9 = (f32[4,1,512]{2,0,1:T(4,128)S(1)}, f32[4,1,512]{2,0,1:T(4,128)S(1)}, u32[]{:S(2)}, u32[]{:S(2)}) collective-permute-start(f32[4,1,512]{2,0,1:T(4,128)S(1)} %get-tuple-element.275), channel_id=1, source_target_pairs={{8,0},{16,8},{24,16},{32,24},{40,32},{48,40},{56,48},{64,56},{72,6... | collective-permute-start | bytes 24584 | tf_op jit(solution)/shard_map/ppermute | solution.py:19
  296.9 7.4 %collective-permute-start.10 = (f32[4,130,1]{2,0,1:T(4,128)S(1)}, f32[4,130,1]{2,0,1:T(4,128)S(1)}, u32[]{:S(2)}, u32[]{:S(2)}) collective-permute-start(f32[4,130,1]{2,0,1:T(4,128)S(1)} %get-tuple-element.264), channel_id=1, source_target_pairs={{0,1},{1,2},{2,3},{3,4},{4,5},{5,6},{6,7},{8,9},{9,10},{10,11},{11... | collective-permute-start | bytes 6248 | tf_op jit(solution)/shard_map/ppermute | solution.py:17
  301.0 10.3 %collective-permute-start.11 = (f32[4,130,1]{2,0,1:T(4,128)S(1)}, f32[4,130,1]{2,0,1:T(4,128)S(1)}, u32[]{:S(2)}, u32[]{:S(2)}) collective-permute-start(f32[4,130,1]{2,0,1:T(4,128)S(1)} %get-tuple-element.263), channel_id=1, source_target_pairs={{1,0},{2,1},{3,2},{4,3},{5,4},{6,5},{7,6},{9,8},{10,9},{11,10},{12... | collective-permute-start | bytes 6248 | tf_op jit(solution)/shard_map/ppermute | solution.py:19
  346.5 13.0 %copy-start.15 = (f32[3,4,32]{2,1,0:T(4,128)S(1)}, f32[3,4,32]{2,1,0:T(4,128)}, u32[]{:S(2)}) copy-start(f32[3,4,32]{2,1,0:T(4,128)} %param.30) | copy-start | bytes 4612
  366.2 5.0 collective-permute-start.12
  369.2 7.2 %collective-permute-start.13 = (f32[4,1,512]{2,0,1:T(4,128)S(1)}, f32[4,1,512]{2,0,1:T(4,128)S(1)}, u32[]{:S(2)}, u32[]{:S(2)}) collective-permute-start(f32[4,1,512]{2,0,1:T(4,128)S(1)} %get-tuple-element.272), channel_id=1, source_target_pairs={{8,0},{16,8},{24,16},{32,24},{40,32},{48,40},{56,48},{64,56},{72,6... | collective-permute-start | bytes 24584 | tf_op jit(solution)/shard_map/ppermute | solution.py:19
  376.6 7.3 %collective-permute-start.14 = (f32[4,130,1]{2,0,1:T(4,128)S(1)}, f32[4,130,1]{2,0,1:T(4,128)S(1)}, u32[]{:S(2)}, u32[]{:S(2)}) collective-permute-start(f32[4,130,1]{2,0,1:T(4,128)S(1)} %get-tuple-element.259), channel_id=1, source_target_pairs={{0,1},{1,2},{2,3},{3,4},{4,5},{5,6},{6,7},{8,9},{9,10},{10,11},{11... | collective-permute-start | bytes 6248 | tf_op jit(solution)/shard_map/ppermute | solution.py:17
  380.5 9.5 %collective-permute-start.15 = (f32[4,130,1]{2,0,1:T(4,128)S(1)}, f32[4,130,1]{2,0,1:T(4,128)S(1)}, u32[]{:S(2)}, u32[]{:S(2)}) collective-permute-start(f32[4,130,1]{2,0,1:T(4,128)S(1)} %get-tuple-element.258), channel_id=1, source_target_pairs={{1,0},{2,1},{3,2},{4,3},{5,4},{6,5},{7,6},{9,8},{10,9},{11,10},{12... | collective-permute-start | bytes 6248 | tf_op jit(solution)/shard_map/ppermute | solution.py:19
  444.9 5.5 %collective-permute-start.16 = (f32[4,1,512]{2,0,1:T(4,128)S(1)}, f32[4,1,512]{2,0,1:T(4,128)S(1)}, u32[]{:S(2)}, u32[]{:S(2)}) collective-permute-start(f32[4,1,512]{2,0,1:T(4,128)S(1)} %get-tuple-element.267), channel_id=1, source_target_pairs={{0,8},{8,16},{16,24},{24,32},{32,40},{40,48},{48,56},{56,64},{64,7... | collective-permute-start | bytes 24584 | tf_op jit(solution)/shard_map/ppermute | solution.py:17
  448.5 7.1 %collective-permute-start.17 = (f32[4,1,512]{2,0,1:T(4,128)S(1)}, f32[4,1,512]{2,0,1:T(4,128)S(1)}, u32[]{:S(2)}, u32[]{:S(2)}) collective-permute-start(f32[4,1,512]{2,0,1:T(4,128)S(1)} %get-tuple-element.268), channel_id=1, source_target_pairs={{8,0},{16,8},{24,16},{32,24},{40,32},{48,40},{56,48},{64,56},{72,6... | collective-permute-start | bytes 24584 | tf_op jit(solution)/shard_map/ppermute | solution.py:19
  455.7 6.0 %collective-permute-start.18 = (f32[4,130,1]{2,0,1:T(4,128)S(1)}, f32[4,130,1]{2,0,1:T(4,128)S(1)}, u32[]{:S(2)}, u32[]{:S(2)}) collective-permute-start(f32[4,130,1]{2,0,1:T(4,128)S(1)} %get-tuple-element.255), channel_id=1, source_target_pairs={{0,1},{1,2},{2,3},{3,4},{4,5},{5,6},{6,7},{8,9},{9,10},{10,11},{11... | collective-permute-start | bytes 6248 | tf_op jit(solution)/shard_map/ppermute | solution.py:17
  458.5 9.5 %collective-permute-start.19 = (f32[4,130,1]{2,0,1:T(4,128)S(1)}, f32[4,130,1]{2,0,1:T(4,128)S(1)}, u32[]{:S(2)}, u32[]{:S(2)}) collective-permute-start(f32[4,130,1]{2,0,1:T(4,128)S(1)} %get-tuple-element.254), channel_id=1, source_target_pairs={{1,0},{2,1},{3,2},{4,3},{5,4},{6,5},{7,6},{9,8},{10,9},{11,10},{12... | collective-permute-start | bytes 6248 | tf_op jit(solution)/shard_map/ppermute | solution.py:19
  (12 other events, 89.7 us)
where the time goes:
time: 533 us; the launch traced here: 525 us
  local copies, waits for them, and re-layouts  181 us (34%)
  matrix products  137 us (26%)
  waiting for transfers between devices  103 us (19%)
  starting transfers between devices  55.8 us (10%)
  other arithmetic  31.1 us (6%)
  loops' own time  15.8 us (3%)
    concatenate x3, local copies, waits for them, and re-layouts, coupling_term(): stacked = jnp.concatenate(tap_list, axis=0)  87.5 us
    dot_general x112, matrix products, matmul(): return jnp.dot(left, right, precision=lax.Precision.HIGHEST)  79.4 us
    ppermute x10, waiting for transfers between devices, padded(): lax.ppermute(head, axis, [((i + 1) % count, i) for i in range(ends)])  67 us
    ppermute x10, starting transfers between devices, padded(): lax.ppermute(tail, axis, [(i, (i + 1) % count) for i in range(ends)])  39.6 us
    dot_general x3, matrix products, coupling_term(): jnp.einsum('ok,khw->ohw', flat_kernel, stacked, precision=lax.Precision.H...  38.3 us
    ppermute x10, waiting for transfers between devices, padded(): lax.ppermute(tail, axis, [(i, (i + 1) % count) for i in range(ends)])  35.6 us
    dynamic_update_slice x4, local copies, waits for them, and re-layouts, add_slot(): return lax.dynamic_update_slice(accum, current + grads[slot], start)  29 us
    dot_general x3, matrix products, coupling_term(): jnp.einsum('co,ohw->chw', out_map, hidden, precision=lax.Precision.HIGHEST)  19.6 us
  transfers between devices with their start and end apart: 20, of which 17 were waited for; matrix products, arithmetic and copies ran while one was open for 3% of the time, Pallas kernels for 0%

commit v1 on v0

v1 whole, which is shorter than its diff:
```python
import functools

import jax
import jax.numpy as jnp
import numpy as np
from jax import lax
from jax.experimental import pallas as pl
from jax.experimental.pallas import tpu as pltpu
from jax.sharding import PartitionSpec as P

step_size = 0.02
LANE = 128
HALF = 64
STRIP = 72
BAND = 144
TILES = 5
ROWS_KEPT = 140
KDX = 48
KTOT = 448

f32 = jnp.float32
bf16 = jnp.bfloat16


def params(mib):
    return pltpu.CompilerParams(vmem_limit_bytes=mib << 20)


def vmem():
    return pl.BlockSpec(memory_space=pltpu.VMEM)


def smem():
    return pl.BlockSpec(memory_space=pltpu.SMEM)


def lanes_of(shape):
    return lax.broadcasted_iota(jnp.int32, shape, len(shape) - 1)


def split(value):
    high = value.astype(bf16)
    low = (value - high.astype(f32)).astype(bf16)
    return high, low


def halves_swapped(value):
    return pltpu.roll(value, HALF, value.ndim - 1)


def pack_kernel(obj_ref, ce_ref, co_ref, ev_ref, od_ref):
    row_odd = lax.axis_index("row") % 2
    col_odd = lax.axis_index("col") % 2
    first = lanes_of((HALF, LANE)) < HALF
    ev_start = pl.multiple_of((1 - row_odd) * HALF, HALF)
    od_start = pl.multiple_of(row_odd * HALF, HALF)
    for c in range(8):
        left = obj_ref[c, :, 0:LANE]
        right = obj_ref[c, :, 3 * LANE : 4 * LANE]
        to_left = jnp.where(first, left[:HALF], halves_swapped(left[HALF:]))
        to_right = jnp.where(first, halves_swapped(right[HALF:]), right[:HALF])
        ce_ref[c] = jnp.where(col_odd == 1, to_left, to_right)
        co_ref[c] = jnp.where(col_odd == 1, to_right, to_left)
        for t in range(4):
            ev_ref[t, c] = obj_ref[c, pl.ds(ev_start, HALF), t * LANE : (t + 1) * LANE]
            od_ref[t, c] = obj_ref[c, pl.ds(od_start, HALF), t * LANE : (t + 1) * LANE]


def comb_kernel(ce_ref, co_ref, comb_ref, ev_ref, od_ref):
    row_odd = lax.axis_index("row") % 2
    col_odd = lax.axis_index("col") % 2
    first = lanes_of((HALF, LANE)) < HALF
    for c in range(8):
        ce = ce_ref[c]
        co = co_ref[c]
        from_right = jnp.where(col_odd == 1, co, ce)
        from_left = jnp.where(col_odd == 1, ce, co)
        top = jnp.where(first, from_right, from_left)
        bottom = halves_swapped(jnp.where(first, from_left, from_right))
        comb_ref[c, :HALF] = top
        comb_ref[c, HALF:] = bottom
        ev_ref[c] = jnp.where(row_odd == 1, top, bottom)
        od_ref[c] = jnp.where(row_odd == 1, bottom, top)


def slots_kernel(
    rows_ref,
    cols_ref,
    count_ref,
    obj_ref,
    comb_ref,
    evm_ref,
    odm_ref,
    evc_ref,
    odc_ref,
    meas_ref,
    probe_ref,
    phase_re_ref,
    phase_im_ref,
    left_f_ref,
    left_b_ref,
    right_f_ref,
    right_b_ref,
    u_ref,
    out_evm,
    out_odm,
    out_evc,
    out_odc,
    own_ref,
    frame,
    accum,
    win,
    waves,
    extra,
    sems,
):
    row_odd = lax.axis_index("row") % 2
    ev_at = pl.multiple_of((1 - row_odd) * 192, HALF)
    od_at = pl.multiple_of(row_odd * 192, HALF)
    copies = []
    for t in range(4):
        copies.append((obj_ref.at[:, :, t * LANE : (t + 1) * LANE], frame.at[t, :, HALF:192, :]))
    copies.append((comb_ref, frame.at[4, :, HALF:192, :]))
    copies.append((evm_ref, frame.at[0:4, :, pl.ds(ev_at, HALF), :]))
    copies.append((odm_ref, frame.at[0:4, :, pl.ds(od_at, HALF), :]))
    copies.append((evc_ref, frame.at[4, :, pl.ds(ev_at, HALF), :]))
    copies.append((odc_ref, frame.at[4, :, pl.ds(od_at, HALF), :]))
    started = [pltpu.make_async_copy(src, dst, sems.at[i]) for i, (src, dst) in enumerate(copies)]
    for item in started:
        item.start()
    accum[...] = jnp.zeros(accum.shape, f32)
    for item in started:
        item.wait()

    lane = lanes_of((LANE, LANE))
    spots = []
    for k in range(4):
        row = rows_ref[k]
        at = lax.rem(cols_ref[k] + (640 - HALF), 640)
        q = at // LANE
        s = at - q * LANE
        nxt = jnp.where(q == 4, 0, q + 1)
        spots.append((row, q, nxt, s))

    for k in range(4):
        row, q, nxt, s = spots[k]
        keep = lane >= s
        turn = jnp.where(s == 0, 0, LANE - s)

        def take(c, carry, k=k, row=row, q=q, nxt=nxt, keep=keep, turn=turn):
            here = frame[q, c, pl.ds(row, LANE), :]
            beyond = frame[nxt, c, pl.ds(row, LANE), :]
            win[c // 2, k, c % 2] = pltpu.roll(jnp.where(keep, here, beyond), turn, 1)
            return carry

        lax.fori_loop(0, 8, take, 0)

    h_re = phase_re_ref[...]
    h_im = phase_im_ref[...]

    def left(xs, mat_ref):
        stack = jnp.concatenate([jnp.concatenate([re, im], axis=0) for re, im in xs], axis=1)
        high, low = split(stack)
        out = jnp.dot(
            mat_ref[...], jnp.concatenate([high, low, high], axis=0), preferred_element_type=f32
        )
        return [
            (out[:LANE, k * LANE : (k + 1) * LANE], out[LANE:, k * LANE : (k + 1) * LANE])
            for k in range(4)
        ]

    def right(xs, mat_ref):
        stack = jnp.concatenate([jnp.concatenate([re, im], axis=1) for re, im in xs], axis=0)
        high, low = split(stack)
        out = jnp.dot(
            jnp.concatenate([high, low, high], axis=1), mat_ref[...], preferred_element_type=f32
        )
        return [
            (out[k * LANE : (k + 1) * LANE, :LANE], out[k * LANE : (k + 1) * LANE, LANE:])
            for k in range(4)
        ]

    def forth(xs):
        return right(left(xs, left_f_ref), right_f_ref)

    def back(xs):
        return left(right(xs, right_b_ref), left_b_ref)

    def times(xs, re, im):
        return [(a * re - b * im, a * im + b * re) for a, b in xs]

    for k in range(4):
        waves[0, k, 0] = probe_ref[0]
        waves[0, k, 1] = probe_ref[1]

    def exit_wave(s):
        xs = []
        for k in range(4):
            p_re, p_im = waves[s, k, 0], waves[s, k, 1]
            o_re, o_im = win[s, k, 0], win[s, k, 1]
            xs.append((p_re * o_re - p_im * o_im, p_re * o_im + p_im * o_re))
        return xs

    def forward(s, carry):
        xs = back(times(forth(exit_wave(s)), h_re, h_im))
        for k in range(4):
            waves[s + 1, k, 0] = xs[k][0]
            waves[s + 1, k, 1] = xs[k][1]
        return carry

    lax.fori_loop(0, 3, forward, 0)
    far = forth(exit_wave(3))
    count = count_ref[0]
    seeds = []
    for k in range(4):
        re, im = far[k]
        factor = (re * re + im * im - meas_ref[k]) * (-2.0 * step_size)
        factor = jnp.where(k < count, factor, 0.0)
        seeds.append((factor * re, factor * im))
    gs = back(seeds)
    grad = waves
    for k in range(4):
        grad[4, k, 0] = gs[k][0]
        grad[4, k, 1] = gs[k][1]

    def through(s):
        xs = []
        for k in range(4):
            g_re, g_im = waves[4, k, 0], waves[4, k, 1]
            p_re, p_im = waves[s, k, 0], waves[s, k, 1]
            o_re, o_im = win[s, k, 0], win[s, k, 1]
            win[s, k, 0] = p_re * g_re + p_im * g_im
            win[s, k, 1] = p_re * g_im - p_im * g_re
            xs.append((o_re * g_re + o_im * g_im, o_re * g_im - o_im * g_re))
        return xs

    def backward(i, carry):
        xs = back(times(forth(through(3 - i)), h_re, -h_im))
        for k in range(4):
            waves[4, k, 0] = xs[k][0]
            waves[4, k, 1] = xs[k][1]
        return carry

    lax.fori_loop(0, 3, backward, 0)
    for k in range(4):
        g_re, g_im = waves[4, k, 0], waves[4, k, 1]
        p_re, p_im = probe_ref[0], probe_ref[1]
        win[0, k, 0] = p_re * g_re + p_im * g_im
        win[0, k, 1] = p_re * g_im - p_im * g_re

    for k in range(4):
        row, q, nxt, s = spots[k]
        keep = lane >= s

        def give(c, carry, k=k, row=row, q=q, nxt=nxt, keep=keep, s=s):
            turned = pltpu.roll(win[c // 2, k, c % 2], s, 1)
            here = accum[q, c, pl.ds(row, LANE), :]
            accum[q, c, pl.ds(row, LANE), :] = here + jnp.where(keep, turned, 0.0)
            beyond = accum[nxt, c, pl.ds(row, LANE), :]
            accum[nxt, c, pl.ds(row, LANE), :] = beyond + jnp.where(keep, 0.0, turned)
            return carry

        lax.fori_loop(0, 8, give, 0)

    wide = lanes_of((256, LANE)) // 8
    gathered = jnp.zeros((256, LANE), f32)
    for c in range(8):
        tail = pltpu.roll(accum[3, c], (8 * c + 8) % LANE, 1)
        head = pltpu.roll(accum[0, c], HALF + 8 * c, 1)
        gathered = jnp.where(wide == c, tail, gathered)
        gathered = jnp.where(wide == 8 + c, head, gathered)
    extra[...] = gathered

    ev_from = pl.multiple_of((1 - row_odd) * 184, 8)
    od_from = pl.multiple_of(row_odd * 184, 8)
    for t in range(4):
        out_evm[t] = accum[t, :, pl.ds(ev_from, STRIP), :]
        out_odm[t] = accum[t, :, pl.ds(od_from, STRIP), :]
    out_evc[0:8] = accum[4, :, pl.ds(ev_from, STRIP), :]
    out_odc[0:8] = accum[4, :, pl.ds(od_from, STRIP), :]
    out_evc[8] = extra[pl.ds(ev_from, STRIP), :]
    out_odc[8] = extra[pl.ds(od_from, STRIP), :]
    own_ref[0:8] = accum[4, :, 56:200, :]
    own_ref[8] = extra[56:200, :]
    for t in range(TILES):
        u_ref[t] = frame[t, :, 56:200, :] + accum[t, :, 56:200, :]


def sides_kernel(own_ref, evc_ref, odc_ref, ce_ref, co_ref):
    row_odd = lax.axis_index("row") % 2
    col_odd = lax.axis_index("col") % 2
    first = lanes_of((STRIP, LANE)) < HALF
    for c in range(9):
        ev = evc_ref[c]
        od = odc_ref[c]
        top = own_ref[c, :STRIP] + jnp.where(row_odd == 1, ev, od)
        bottom = halves_swapped(own_ref[c, STRIP:] + jnp.where(row_odd == 1, od, ev))
        to_right = jnp.where(first, top, bottom)
        to_left = jnp.where(first, bottom, top)
        ce_ref[c] = jnp.where(col_odd == 1, to_left, to_right)
        co_ref[c] = jnp.where(col_odd == 1, to_right, to_left)


def denoise_kernel(
    u_ref,
    evm_ref,
    odm_ref,
    evc_ref,
    odc_ref,
    ce_ref,
    co_ref,
    conv_ref,
    map_ref,
    bias_ref,
    out_ref,
    low_st,
    up_st,
    cond_st,
    conv_sc,
    map_sc,
):
    row_id = lax.axis_index("row")
    col_id = lax.axis_index("col")
    row_odd = row_id % 2
    col_odd = col_id % 2
    lane = lanes_of((STRIP, LANE))
    first = lane < HALF

    for layer in range(3):
        high, low = split(conv_ref[layer])
        place = lanes_of(high.shape)
        use_low = ((place >= 288) & (place < 432)) | (place == 433)
        conv_sc[layer] = jnp.where(use_low, low.astype(f32), high.astype(f32)).astype(bf16)
        high, low = split(map_ref[layer])
        map_sc[layer, 0:32] = high
        map_sc[layer, 32:64] = low

    def combine(t, c):
        top = u_ref[t, c, :STRIP]
        bottom = u_ref[t, c, STRIP:]
        ev = evc_ref[c] if t == 4 else evm_ref[t, c]
        od = odc_ref[c] if t == 4 else odm_ref[t, c]
        top = top + jnp.where(row_odd == 1, ev, od)
        bottom = bottom + jnp.where(row_odd == 1, od, ev)
        if t in (0, 3):
            ce = ce_ref[c]
            co = co_ref[c]
            if t == 0:
                side = jnp.where(col_odd == 1, ce, co)
                top = top + jnp.where(first, side, 0.0)
                bottom = bottom + jnp.where(first, halves_swapped(side), 0.0)
            else:
                side = jnp.where(col_odd == 1, co, ce)
                top = top + jnp.where(first, 0.0, side)
                bottom = bottom + jnp.where(first, 0.0, halves_swapped(side))
        if t == 4:
            ce = ce_ref[8]
            co = co_ref[8]
            from_left = jnp.where(col_odd == 1, ce, co)
            from_right = jnp.where(col_odd == 1, co, ce)
            tail_top = pltpu.roll(from_left, (120 - 8 * c) % LANE, 1)
            tail_bottom = pltpu.roll(from_left, (HALF + 120 - 8 * c) % LANE, 1)
            head_top = pltpu.roll(from_right, (HALF - 8 * c) % LANE, 1)
            head_bottom = pltpu.roll(from_right, (LANE - 8 * c) % LANE, 1)
            at_tail = lane >= 120
            at_head = lane < 8
            top = top + jnp.where(at_tail, tail_top, jnp.where(at_head, head_top, 0.0))
            bottom = bottom + jnp.where(at_tail, tail_bottom, jnp.where(at_head, head_bottom, 0.0))
        return jnp.concatenate([top, bottom], axis=0)

    for t in range(TILES):
        for c in range(4):
            low_st[t, pl.ds(c, ROWS_KEPT, stride=4), :] = combine(t, c)[3:143]
            up_st[t, pl.ds(c, ROWS_KEPT, stride=4), :] = combine(t, 4 + c)[4:144]

    last_row = lax.axis_size("row") - 1
    last_col = lax.axis_size("col") - 1
    col_from = jnp.where(col_id == 0, 128, 640)
    right_off = jnp.where(col_id == last_col, 512, 576)
    left_off = jnp.where(col_id == 0, 640, 576)
    del col_from

    def prepare(store, first_row):
        row_low = jnp.where(row_id == 0, -first_row * 4, 0)
        row_high = jnp.where(row_id == last_row, (128 - first_row) * 4, 4 * ROWS_KEPT)

        def body(i, carry):
            at = pl.multiple_of(i * 16, 16)
            x = jnp.concatenate([store[t, pl.ds(at, 16), :] for t in range(TILES)], axis=1)
            column = lax.broadcasted_iota(jnp.int32, x.shape, 1)
            index = lax.broadcasted_iota(jnp.int32, x.shape, 0) + at
            inside = (index >= row_low) & (index < row_high)
            inside = inside & ((column < right_off) | (column >= left_off))
            x = jnp.where(inside, x, 0.0)
            for dx in range(3):
                y = x if dx == 1 else pltpu.roll(x, 1 if dx == 0 else 639, 1)
                high, low = split(y)
                cond_st[0, dx, pl.ds(at, 16), :] = high
                cond_st[1, dx, pl.ds(at, 16), :] = low
            return carry

        lax.fori_loop(0, 4 * ROWS_KEPT // 16, body, 0)

    ones = {w: jnp.ones((16, w), bf16) for w in (LANE, 2 * LANE)}

    def layer_pass(layer, groups, read_at, store, write_at, chunks):
        weights = conv_sc[layer]
        both = map_sc[layer]
        single = map_sc[layer, 0:32]
        bias = bias_ref[layer]

        def body(g, carry):
            src = pl.multiple_of(read_at + g * 32, 16)
            dst = pl.multiple_of(write_at + g * 32, 8)
            for begin, width in chunks:
                pieces = [cond_st[part, dx, pl.ds(src, KDX), begin : begin + width] for part in (0, 1) for dx in range(3)]
                pieces = pieces + pieces[:3] + [ones[width]]
                half = jnp.dot(weights, jnp.concatenate(pieces, axis=0), preferred_element_type=f32)
                hidden = half + half * jnp.tanh(half)
                high, low = split(hidden)
                out = jnp.dot(both, high, preferred_element_type=f32)
                term = out[:32] + out[32:] + jnp.dot(single, low, preferred_element_type=f32)
                for j in range(width // LANE):
                    t = begin // LANE + j
                    bit = term[:, j * LANE : (j + 1) * LANE]
                    store[t, pl.ds(dst, 32), :] = store[t, pl.ds(dst, 32), :] + (bit + bias)
            return carry

        lax.fori_loop(0, groups, body, 0)

    wide = ((0, 256), (256, 256), (512, 128))
    prepare(low_st, -5)
    layer_pass(0, 17, 0, up_st, 8, wide)
    prepare(up_st, -4)
    layer_pass(1, 17, 0, low_st, 16, wide)
    prepare(low_st, -5)
    layer_pass(2, 16, 16, up_st, 16, wide[:2])
    for t in range(4):
        for c in range(4):
            out_ref[c, :, t * LANE : (t + 1) * LANE] = low_st[t, pl.ds(20 + c, 128, stride=4), :]
            out_ref[4 + c, :, t * LANE : (t + 1) * LANE] = up_st[t, pl.ds(16 + c, 128, stride=4), :]


def dft_matrices():
    index = np.arange(LANE)
    angle = 2.0 * np.pi / LANE * (np.outer(index, index) % LANE)
    c = np.cos(angle) / np.sqrt(LANE)
    s = np.sin(angle) / np.sqrt(LANE)
    a = np.block([[c, s], [-s, c]]).astype(np.float32)
    b = np.block([[c, -s], [s, c]]).astype(np.float32)

    def parts(m):
        high = m.astype(jnp.bfloat16)
        low = (m - high.astype(np.float32)).astype(jnp.bfloat16)
        return high, low

    (ah, al), (bh, bl) = parts(a), parts(b)
    left_f = np.concatenate([ah, ah, al], axis=1)
    left_b = np.concatenate([bh, bh, bl], axis=1)
    right_f = np.concatenate([bh, bh, bl], axis=0)
    right_b = np.concatenate([ah, ah, al], axis=0)
    return left_f, left_b, right_f, right_b


def conv_matrices(conv_weight, conv_bias, output_weight, output_bias):
    layers = conv_weight.shape[0]
    w = conv_weight.reshape(layers, 3, 3, 32, 4) * 0.5
    blocks = []
    for layer, start in zip(range(layers), (2, 2, 0)):
        hot = np.zeros((8, 3, 12), np.float32)
        for j in range(8):
            for dy in range(3):
                hot[j, dy, j + dy + start] = 1.0
        m = sum(hot[:, dy][:, None, None, :, None] * jnp.transpose(w[layer, dy], (1, 0, 2))[None, :, :, None, :] for dy in range(3))
        blocks.append(m.reshape(256, 144))
    main = jnp.stack(blocks)
    bias = jnp.tile(conv_bias * 0.5, (1, 8))[:, :, None]
    packed = jnp.concatenate([main, main, main, bias, bias, jnp.zeros((layers, 256, 14), f32)], axis=2)
    eye = np.eye(8, dtype=np.float32)
    maps = (eye[None, :, None, :, None] * output_weight[:, None, :, None, :]).reshape(layers, 32, 256)
    out_bias = jnp.broadcast_to(jnp.tile(output_bias, (1, 8))[:, :, None], (layers, 32, LANE))
    return packed, maps, out_bias


def sds(*shape):
    return jax.ShapeDtypeStruct(shape, f32)


def per_device(
    object_field,
    probe_field,
    propagator_phase,
    position_rows,
    position_cols,
    tile_counts,
    intensities,
    conv_weight,
    conv_bias,
    output_weight,
    output_bias,
):
    rows = lax.axis_size("row")
    cols = lax.axis_size("col")

    def pairs(count, start):
        found = []
        for i in range(start, count - 1, 2):
            found += [(i, i + 1), (i + 1, i)]
        return found

    def row_ev(x):
        return lax.ppermute(x, "row", pairs(rows, 0))

    def row_od(x):
        return lax.ppermute(x, "row", pairs(rows, 1))

    def col_ev(x):
        return lax.ppermute(x, "col", pairs(cols, 0))

    def col_od(x):
        return lax.ppermute(x, "col", pairs(cols, 1))

    obj = object_field.reshape(8, 128, 512)
    ce, co, evm, odm = pl.pallas_call(
        pack_kernel,
        out_shape=[sds(8, HALF, LANE), sds(8, HALF, LANE), sds(4, 8, HALF, LANE), sds(4, 8, HALF, LANE)],
        in_specs=[vmem()],
        out_specs=[vmem()] * 4,
        compiler_params=params(32),
        name="pack",
    )(obj)
    odm = row_od(odm)
    ce = col_ev(ce)
    co = col_od(co)
    evm = row_ev(evm)
    comb, evc, odc = pl.pallas_call(
        comb_kernel,
        out_shape=[sds(8, 128, LANE), sds(8, HALF, LANE), sds(8, HALF, LANE)],
        in_specs=[vmem()] * 2,
        out_specs=[vmem()] * 3,
        compiler_params=params(32),
        name="comb",
    )(ce, co)
    odc = row_od(odc)
    evc = row_ev(evc)
    phase_re = jnp.cos(propagator_phase)
    phase_im = jnp.sin(propagator_phase)
    tables = [jnp.asarray(m) for m in dft_matrices()]
    anywhere = pl.BlockSpec(memory_space=pl.ANY)
    u, evm, odm, evc, odc, own = pl.pallas_call(
        slots_kernel,
        out_shape=[
            sds(TILES, 8, BAND, LANE),
            sds(4, 8, STRIP, LANE),
            sds(4, 8, STRIP, LANE),
            sds(9, STRIP, LANE),
            sds(9, STRIP, LANE),
            sds(9, BAND, LANE),
        ],
        in_specs=[smem()] * 3 + [anywhere] * 6 + [vmem()] * 8,
        out_specs=[vmem()] * 6,
        scratch_shapes=[
            pltpu.VMEM((TILES, 8, 256, LANE), f32),
            pltpu.VMEM((TILES, 8, 256, LANE), f32),
            pltpu.VMEM((4, 4, 2, LANE, LANE), f32),
            pltpu.VMEM((5, 4, 2, LANE, LANE), f32),
            pltpu.VMEM((256, LANE), f32),
            pltpu.SemaphoreType.DMA((9,)),
        ],
        compiler_params=params(56),
        name="slots",
    )(
        position_rows.reshape(-1),
        position_cols.reshape(-1),
        tile_counts.reshape(-1),
        obj,
        comb,
        evm,
        odm,
        evc,
        odc,
        intensities.reshape(4, LANE, LANE),
        probe_field,
        phase_re,
        phase_im,
        *tables,
    )
    odc = row_od(odc)
    evc = row_ev(evc)
    odm = row_od(odm)
    evm = row_ev(evm)
    ce, co = pl.pallas_call(
        sides_kernel,
        out_shape=[sds(9, STRIP, LANE)] * 2,
        in_specs=[vmem()] * 3,
        out_specs=[vmem()] * 2,
        compiler_params=params(32),
        name="sides",
    )(own, evc, odc)
    ce = col_ev(ce)
    co = col_od(co)
    packed, maps, out_bias = conv_matrices(conv_weight, conv_bias, output_weight, output_bias)
    out = pl.pallas_call(
        denoise_kernel,
        out_shape=sds(8, 128, 512),
        in_specs=[vmem()] * 10,
        out_specs=vmem(),
        scratch_shapes=[
            pltpu.VMEM((TILES, 4 * ROWS_KEPT, LANE), f32),
            pltpu.VMEM((TILES, 4 * ROWS_KEPT, LANE), f32),
            pltpu.VMEM((2, 3, 4 * ROWS_KEPT, 640), bf16),
            pltpu.VMEM((3, 256, KTOT), bf16),
            pltpu.VMEM((3, 64, 256), bf16),
        ],
        compiler_params=params(56),
        name="denoise",
    )(u, evm, odm, evc, odc, ce, co, packed, maps, out_bias)
    return out.reshape(4, 2, 128, 512)


def solution(mesh):
    placed = (
        P(None, None, "row", "col"),
        P(),
        P(),
        P("row", "col", None),
        P("row", "col", None),
        P("row", "col"),
        P("row", "col", None, None, None),
        P(),
        P(),
        P(),
        P(),
    )
    return jax.shard_map(
        per_device,
        mesh=mesh,
        in_specs=placed,
        out_specs=P(None, None, "row", "col"),
        check_vma=False,
    )
```

time: 533 us -> 175 us (0.33)
  the two profiles are of different devices: /device:TPU:7 before, /device:TPU:28 now
where the time goes in v1:
time: 175 us
  Pallas kernels  89.4 us (51%)
  starting transfers between devices  36.7 us (21%)
  waiting for transfers between devices  33.7 us (19%)
  local copies, waits for them, and re-layouts  11.7 us (7%)
  other arithmetic  2.12 us (1%)
    pallas_call x1, Pallas kernels, per_device(): pl.pallas_call(denoise_kernel, out_shape=sds(8, 128, 512), in_specs=[vmem...  63.4 us
    pallas_call x1, Pallas kernels, per_device(): pl.pallas_call(slots_kernel, out_shape=[sds(TILES, 8, BAND, LANE), sds(4,...  25.3 us
    ppermute x2, waiting for transfers between devices, col_od(): return lax.ppermute(x, 'col', pairs(cols, 1))  15.4 us
    ppermute x4, waiting for transfers between devices, row_od(): return lax.ppermute(x, 'row', pairs(rows, 1))  14.4 us
    ppermute x4, starting transfers between devices, row_ev(): return lax.ppermute(x, 'row', pairs(rows, 0))  13.6 us
    ppermute x2, starting transfers between devices, col_od(): return lax.ppermute(x, 'col', pairs(cols, 1))  12.5 us
    ppermute x4, starting transfers between devices, row_od(): return lax.ppermute(x, 'row', pairs(rows, 1))  9.16 us
    ppermute x2, waiting for transfers between devices, col_ev(): return lax.ppermute(x, 'col', pairs(cols, 0))  3.87 us
  transfers between devices with their start and end apart: 12, of which 6 were waited for; matrix products, arithmetic and copies ran while one was open for 5% of the time, Pallas kernels for 0%

profile of v1, /device:TPU:28, one launch (start us, length us, event | category | flops | bytes accessed | tf_op | source)
XLA Modules:
  0.0 174.6 jit_solution(2166643061208347981)
XLA Ops:
  0.0 1.6 copy-done
  2.0 2.5 %collective-permute-start.3 = (f32[4,8,64,128]{3,2,1,0:T(8,128)S(1)}, f32[4,8,64,128]{3,2,1,0:T(8,128)S(1)}, u32[]{:S(2)}, u32[]{:S(2)}) collective-permute-start(f32[4,8,64,128]{3,2,1,0:T(8,128)S(1)} %get-tuple-element.24), channel_id=1, source_target_pairs={{8,16},{16,8},{24,32},{32,24},{40,48},{48,40},{56,64},{64,56},{72,... | collective-permute-start | bytes 3145736 | tf_op jit(solution)/shard_map/ppermute | solution.py:515
  4.5 1.3 collective-permute-start
  5.8 5.5 %collective-permute-start.1 = (f32[8,64,128]{2,1,0:T(8,128)S(1)}, f32[8,64,128]{2,1,0:T(8,128)S(1)}, u32[]{:S(2)}, u32[]{:S(2)}) collective-permute-start(f32[8,64,128]{2,1,0:T(8,128)S(1)} %get-tuple-element.21), channel_id=1, source_target_pairs={{1,2},{2,1},{3,4},{4,3},{5,6},{6,5},{9,10},{10,9},{11,12},{12,11},... | collective-permute-start | bytes 786440 | tf_op jit(solution)/shard_map/ppermute | solution.py:521
  11.4 3.6 %collective-permute-done.ce_ref = f32[8,64,128]{2,1,0:T(8,128)S(1)} collective-permute-done((f32[8,64,128]{2,1,0:T(8,128)S(1)}, f32[8,64,128]{2,1,0:T(8,128)S(1)}, u32[]{:S(2)}, u32[]{:S(2)}) %collective-permute-start) | collective-permute-done | bytes 262176 | tf_op jit(solution)/shard_map/ppermute | solution.py:518
  15.0 7.0 %collective-permute-done.1.co_ref = f32[8,64,128]{2,1,0:T(8,128)S(1)} collective-permute-done((f32[8,64,128]{2,1,0:T(8,128)S(1)}, f32[8,64,128]{2,1,0:T(8,128)S(1)}, u32[]{:S(2)}, u32[]{:S(2)}) %collective-permute-start.1) | collective-permute-done | bytes 262176 | tf_op jit(solution)/shard_map/ppermute | solution.py:521
  22.1 0.8 copy-done.4
  22.9 2.8 %collective-permute-start.5 = (f32[8,64,128]{2,1,0:T(8,128)S(1)}, f32[8,64,128]{2,1,0:T(8,128)S(1)}, u32[]{:S(2)}, u32[]{:S(2)}) collective-permute-start(f32[8,64,128]{2,1,0:T(8,128)S(1)} %get-tuple-element.26), channel_id=1, source_target_pairs={{8,16},{16,8},{24,32},{32,24},{40,48},{48,40},{56,64},{64,56},{72,... | collective-permute-start | bytes 786440 | tf_op jit(solution)/shard_map/ppermute | solution.py:515
  26.4 0.9 fusion
  27.3 3.3 %collective-permute-done.5.odc_ref = f32[8,64,128]{2,1,0:T(8,128)S(1)} collective-permute-done((f32[8,64,128]{2,1,0:T(8,128)S(1)}, f32[8,64,128]{2,1,0:T(8,128)S(1)}, u32[]{:S(2)}, u32[]{:S(2)}) %collective-permute-start.5) | collective-permute-done | bytes 262176 | tf_op jit(solution)/shard_map/ppermute | solution.py:515
  32.0 25.3 %slots.1 = (f32[5,8,144,128]{3,2,1,0:T(8,128)}, f32[4,8,72,128]{3,2,1,0:T(8,128)}, f32[4,8,72,128]{3,2,1,0:T(8,128)}, f32[9,72,128]{2,1,0:T(8,128)}, f32[9,72,128]{2,1,0:T(8,128)}, /*index=5*/f32[9,144,128]{2,1,0:T(8,128)}) custom-call(s32[4]{0:T(128)} %bitcast.64, s32[4]{0:T(128)} %bitcast.65, s32[1]{0:T(128)} %bitcast.59.count_ref, ...), custom_call_target="tpu_custom_call" | custom-call | tf_op jit(solution)/shard_map/slots/pallas_call | solution.py:550
  57.4 11.7 %collective-permute-start.6 = (f32[4,8,72,128]{3,2,1,0:T(8,128)}, f32[4,8,72,128]{3,2,1,0:T(8,128)}, u32[]{:S(2)}, u32[]{:S(2)}) collective-permute-start(f32[4,8,72,128]{3,2,1,0:T(8,128)} %get-tuple-element.28), channel_id=1, source_target_pairs={{0,8},{8,0},{16,24},{24,16},{32,40},{40,32},{48,56},{56,48},{64,72... | collective-permute-start | bytes 3538952 | tf_op jit(solution)/shard_map/ppermute | solution.py:512
  69.0 1.9 %collective-permute-start.7 = (f32[4,8,72,128]{3,2,1,0:T(8,128)}, f32[4,8,72,128]{3,2,1,0:T(8,128)}, u32[]{:S(2)}, u32[]{:S(2)}) collective-permute-start(f32[4,8,72,128]{3,2,1,0:T(8,128)} %get-tuple-element.29), channel_id=1, source_target_pairs={{8,16},{16,8},{24,32},{32,24},{40,48},{48,40},{56,64},{64,56},{72,... | collective-permute-start | bytes 3538952 | tf_op jit(solution)/shard_map/ppermute | solution.py:515
  71.0 1.9 %collective-permute-start.8 = (f32[9,72,128]{2,1,0:T(8,128)}, f32[9,72,128]{2,1,0:T(8,128)S(1)}, u32[]{:S(2)}, u32[]{:S(2)}) collective-permute-start(f32[9,72,128]{2,1,0:T(8,128)} %get-tuple-element.30), channel_id=1, source_target_pairs={{0,8},{8,0},{16,24},{24,16},{32,40},{40,32},{48,56},{56,48},{64,72... | collective-permute-start | bytes 995336 | tf_op jit(solution)/shard_map/ppermute | solution.py:512
  72.9 1.9 %collective-permute-start.9 = (f32[9,72,128]{2,1,0:T(8,128)}, f32[9,72,128]{2,1,0:T(8,128)S(1)}, u32[]{:S(2)}, u32[]{:S(2)}) collective-permute-start(f32[9,72,128]{2,1,0:T(8,128)} %get-tuple-element.31), channel_id=1, source_target_pairs={{8,16},{16,8},{24,32},{32,24},{40,48},{48,40},{56,64},{64,56},{72,... | collective-permute-start | bytes 995336 | tf_op jit(solution)/shard_map/ppermute | solution.py:515
  75.8 0.8 copy.36
  76.9 0.9 copy.37
  78.4 0.7 mul.287
  79.2 11.1 %collective-permute-done.9.odc_ref = f32[9,72,128]{2,1,0:T(8,128)S(1)} collective-permute-done((f32[9,72,128]{2,1,0:T(8,128)}, f32[9,72,128]{2,1,0:T(8,128)S(1)}, u32[]{:S(2)}, u32[]{:S(2)}) %collective-permute-start.9) | collective-permute-done | bytes 331808 | tf_op jit(solution)/shard_map/ppermute | solution.py:515
  90.6 6.9 %collective-permute-start.11 = (f32[9,72,128]{2,1,0:T(8,128)S(1)}, f32[9,72,128]{2,1,0:T(8,128)}, u32[]{:S(2)}, u32[]{:S(2)}) collective-permute-start(f32[9,72,128]{2,1,0:T(8,128)S(1)} %get-tuple-element.34), channel_id=1, source_target_pairs={{1,2},{2,1},{3,4},{4,3},{5,6},{6,5},{9,10},{10,9},{11,12},{12,11},... | collective-permute-start | bytes 995336 | tf_op jit(solution)/shard_map/ppermute | solution.py:521
  97.6 1.1 pad_maximum_fusion
  98.7 2.4 %concatenate.3.conv_ref = f32[3,256,448]{2,1,0:T(8,128)} concatenate(f32[3,256,144]{2,1,0:T(8,128)S(1)} %pad_maximum_fusion, f32[3,256,144]{2,1,0:T(8,128)S(1)} %pad_maximum_fusion, f32[3,256,144]{2,1,0:T(8,128)S(1)} %pad_maximum_fusion, f32[3,256,1]{2,1,0:T(8,128)S(1)} %tile.20, f32[3,256,1]{2,1,0:T(8,128)S(1)} %tile.20, f32[3,256,14]{2,1,0:T(8,128)S(1)} %broadcast_in_dim.4), dimensions={2} | concatenate | bytes 2752512 | tf_op jit(solution)/shard_map/concatenate | solution.py:478
  102.0 8.5 %collective-permute-done.11.co_ref = f32[9,72,128]{2,1,0:T(8,128)} collective-permute-done((f32[9,72,128]{2,1,0:T(8,128)S(1)}, f32[9,72,128]{2,1,0:T(8,128)}, u32[]{:S(2)}, u32[]{:S(2)}) %collective-permute-start.11) | collective-permute-done | bytes 331808 | tf_op jit(solution)/shard_map/ppermute | solution.py:521
  111.2 63.4 %denoise.1 = f32[8,128,512]{2,1,0:T(8,128)} custom-call(f32[5,8,144,128]{3,2,1,0:T(8,128)} %get-tuple-element.27.u_ref, f32[4,8,72,128]{3,2,1,0:T(8,128)} %collective-permute-done.6.evm_ref, f32[4,8,72,128]{3,2,1,0:T(8,128)} %collective-permute-done.7.odm_ref, f32[9,72,128]{2,1,0:T(8,128)} %copy-done.1, f32[9,72,128]{2,1,0:T(8,128)} %copy-done.2, ...), custom_call_target="tpu_custom_call" | custom-call | tf_op jit(solution)/shard_map/denoise/pallas_call | solution.py:603
  (71 shorter events, 5.8 us)
Async XLA Ops:
  1.6 24.8 %copy-start.10 = (f32[128,128]{1,0:T(8,128)S(1)}, f32[128,128]{1,0:T(8,128)}, u32[]{:S(2)}) copy-start(f32[128,128]{1,0:T(8,128)} %param.27) | copy-start | bytes 196612
  1.9 28.7 %collective-permute-start.2 = (f32[4,8,64,128]{3,2,1,0:T(8,128)S(1)}, f32[4,8,64,128]{3,2,1,0:T(8,128)S(1)}, u32[]{:S(2)}, u32[]{:S(2)}) collective-permute-start(f32[4,8,64,128]{3,2,1,0:T(8,128)S(1)} %get-tuple-element.23), channel_id=1, source_target_pairs={{0,8},{8,0},{16,24},{24,16},{32,40},{40,32},{48,56},{56,48},{64,72... | collective-permute-start | bytes 3145736 | tf_op jit(solution)/shard_map/ppermute | solution.py:512
  2.0 28.6 %collective-permute-start.3 = (f32[4,8,64,128]{3,2,1,0:T(8,128)S(1)}, f32[4,8,64,128]{3,2,1,0:T(8,128)S(1)}, u32[]{:S(2)}, u32[]{:S(2)}) collective-permute-start(f32[4,8,64,128]{3,2,1,0:T(8,128)S(1)} %get-tuple-element.24), channel_id=1, source_target_pairs={{8,16},{16,8},{24,32},{32,24},{40,48},{48,40},{56,64},{64,56},{72,... | collective-permute-start | bytes 3145736 | tf_op jit(solution)/shard_map/ppermute | solution.py:515
  4.5 10.5 %collective-permute-start = (f32[8,64,128]{2,1,0:T(8,128)S(1)}, f32[8,64,128]{2,1,0:T(8,128)S(1)}, u32[]{:S(2)}, u32[]{:S(2)}) collective-permute-start(f32[8,64,128]{2,1,0:T(8,128)S(1)} %get-tuple-element.20), channel_id=1, source_target_pairs={{0,1},{1,0},{2,3},{3,2},{4,5},{5,4},{6,7},{7,6},{8,9},{9,8},{10,11... | collective-permute-start | bytes 786440 | tf_op jit(solution)/shard_map/ppermute | solution.py:518
  5.8 16.1 %collective-permute-start.1 = (f32[8,64,128]{2,1,0:T(8,128)S(1)}, f32[8,64,128]{2,1,0:T(8,128)S(1)}, u32[]{:S(2)}, u32[]{:S(2)}) collective-permute-start(f32[8,64,128]{2,1,0:T(8,128)S(1)} %get-tuple-element.21), channel_id=1, source_target_pairs={{1,2},{2,1},{3,4},{4,3},{5,6},{6,5},{9,10},{10,9},{11,12},{12,11},... | collective-permute-start | bytes 786440 | tf_op jit(solution)/shard_map/ppermute | solution.py:521
  22.9 4.4 %collective-permute-start.4 = (f32[8,64,128]{2,1,0:T(8,128)S(1)}, f32[8,64,128]{2,1,0:T(8,128)S(1)}, u32[]{:S(2)}, u32[]{:S(2)}) collective-permute-start(f32[8,64,128]{2,1,0:T(8,128)S(1)} %get-tuple-element.25), channel_id=1, source_target_pairs={{0,8},{8,0},{16,24},{24,16},{32,40},{40,32},{48,56},{56,48},{64,72... | collective-permute-start | bytes 786440 | tf_op jit(solution)/shard_map/ppermute | solution.py:512
  22.9 7.7 %collective-permute-start.5 = (f32[8,64,128]{2,1,0:T(8,128)S(1)}, f32[8,64,128]{2,1,0:T(8,128)S(1)}, u32[]{:S(2)}, u32[]{:S(2)}) collective-permute-start(f32[8,64,128]{2,1,0:T(8,128)S(1)} %get-tuple-element.26), channel_id=1, source_target_pairs={{8,16},{16,8},{24,32},{32,24},{40,48},{48,40},{56,64},{64,56},{72,... | collective-permute-start | bytes 786440 | tf_op jit(solution)/shard_map/ppermute | solution.py:515
  27.3 3.3 %copy-start.7 = (f32[8,64,128]{2,1,0:T(8,128)}, f32[8,64,128]{2,1,0:T(8,128)S(1)}, u32[]{:S(2)}) copy-start(f32[8,64,128]{2,1,0:T(8,128)S(1)} %collective-permute-done.4.evc_ref) | copy-start | bytes 786436
  32.0 39.0 %copy-start.11 = (f32[3,9,32,4]{2,3,1,0:T(4,128)S(1)}, f32[3,9,32,4]{2,3,1,0:T(4,128)}, u32[]{:S(2)}) copy-start(f32[3,9,32,4]{2,3,1,0:T(4,128)} %param.32) | copy-start | bytes 41476
  32.0 42.8 %copy-start.12 = (f32[8,12]{0,1:T(8,128)S(1)}, f32[8,12]{0,1:T(8,128)}, u32[]{:S(2)}) copy-start(f32[8,12]{0,1:T(8,128)} %constant.39) | copy-start | bytes 1156
  32.0 42.8 %copy-start.13 = (f32[8,12]{0,1:T(8,128)S(1)}, f32[8,12]{0,1:T(8,128)}, u32[]{:S(2)}) copy-start(f32[8,12]{0,1:T(8,128)} %constant.40) | copy-start | bytes 1156
  32.0 42.8 %copy-start.14 = (f32[8,12]{0,1:T(8,128)S(1)}, f32[8,12]{0,1:T(8,128)}, u32[]{:S(2)}) copy-start(f32[8,12]{0,1:T(8,128)} %constant.41) | copy-start | bytes 1156
  32.0 42.8 %copy-start.15 = (f32[8,12]{0,1:T(8,128)S(1)}, f32[8,12]{0,1:T(8,128)}, u32[]{:S(2)}) copy-start(f32[8,12]{0,1:T(8,128)} %constant.42) | copy-start | bytes 1156
  32.0 42.8 %copy-start.16 = (f32[8,12]{0,1:T(8,128)S(1)}, f32[8,12]{0,1:T(8,128)}, u32[]{:S(2)}) copy-start(f32[8,12]{0,1:T(8,128)} %constant.43) | copy-start | bytes 1156
  57.4 53.1 %collective-permute-start.6 = (f32[4,8,72,128]{3,2,1,0:T(8,128)}, f32[4,8,72,128]{3,2,1,0:T(8,128)}, u32[]{:S(2)}, u32[]{:S(2)}) collective-permute-start(f32[4,8,72,128]{3,2,1,0:T(8,128)} %get-tuple-element.28), channel_id=1, source_target_pairs={{0,8},{8,0},{16,24},{24,16},{32,40},{40,32},{48,56},{56,48},{64,72... | collective-permute-start | bytes 3538952 | tf_op jit(solution)/shard_map/ppermute | solution.py:512
  69.0 41.5 %collective-permute-start.7 = (f32[4,8,72,128]{3,2,1,0:T(8,128)}, f32[4,8,72,128]{3,2,1,0:T(8,128)}, u32[]{:S(2)}, u32[]{:S(2)}) collective-permute-start(f32[4,8,72,128]{3,2,1,0:T(8,128)} %get-tuple-element.29), channel_id=1, source_target_pairs={{8,16},{16,8},{24,32},{32,24},{40,48},{48,40},{56,64},{64,56},{72,... | collective-permute-start | bytes 3538952 | tf_op jit(solution)/shard_map/ppermute | solution.py:515
  71.0 8.2 %collective-permute-start.8 = (f32[9,72,128]{2,1,0:T(8,128)}, f32[9,72,128]{2,1,0:T(8,128)S(1)}, u32[]{:S(2)}, u32[]{:S(2)}) collective-permute-start(f32[9,72,128]{2,1,0:T(8,128)} %get-tuple-element.30), channel_id=1, source_target_pairs={{0,8},{8,0},{16,24},{24,16},{32,40},{40,32},{48,56},{56,48},{64,72... | collective-permute-start | bytes 995336 | tf_op jit(solution)/shard_map/ppermute | solution.py:512
  72.9 17.4 %collective-permute-start.9 = (f32[9,72,128]{2,1,0:T(8,128)}, f32[9,72,128]{2,1,0:T(8,128)S(1)}, u32[]{:S(2)}, u32[]{:S(2)}) collective-permute-start(f32[9,72,128]{2,1,0:T(8,128)} %get-tuple-element.31), channel_id=1, source_target_pairs={{8,16},{16,8},{24,32},{32,24},{40,48},{48,40},{56,64},{64,56},{72,... | collective-permute-start | bytes 995336 | tf_op jit(solution)/shard_map/ppermute | solution.py:515
  75.8 3.3 %copy-start.19 = (f32[3,4]{1,0:T(4,128)S(1)}, f32[3,4]{1,0:T(4,128)}, u32[]{:S(2)}) copy-start(f32[3,4]{1,0:T(4,128)} %param.35) | copy-start | bytes 148
  75.8 14.5 %copy-start.3 = (f32[9,144,128]{2,1,0:T(8,128)S(1)}, f32[9,144,128]{2,1,0:T(8,128)}, u32[]{:S(2)}) copy-start(f32[9,144,128]{2,1,0:T(8,128)} %get-tuple-element.32.own_ref) | copy-start | bytes 1990660
  79.2 19.5 %copy-start.1 = (f32[9,72,128]{2,1,0:T(8,128)}, f32[9,72,128]{2,1,0:T(8,128)S(1)}, u32[]{:S(2)}) copy-start(f32[9,72,128]{2,1,0:T(8,128)S(1)} %collective-permute-done.8.evc_ref) | copy-start | bytes 995332
  90.3 8.4 %copy-start.2 = (f32[9,72,128]{2,1,0:T(8,128)}, f32[9,72,128]{2,1,0:T(8,128)S(1)}, u32[]{:S(2)}) copy-start(f32[9,72,128]{2,1,0:T(8,128)S(1)} %collective-permute-done.9.odc_ref) | copy-start | bytes 995332
  90.5 11.5 %collective-permute-start.10 = (f32[9,72,128]{2,1,0:T(8,128)S(1)}, f32[9,72,128]{2,1,0:T(8,128)}, u32[]{:S(2)}, u32[]{:S(2)}) collective-permute-start(f32[9,72,128]{2,1,0:T(8,128)S(1)} %get-tuple-element.33), channel_id=1, source_target_pairs={{0,1},{1,0},{2,3},{3,2},{4,5},{5,4},{6,7},{7,6},{8,9},{9,8},{10,11... | collective-permute-start | bytes 995336 | tf_op jit(solution)/shard_map/ppermute | solution.py:518
  90.6 19.9 %collective-permute-start.11 = (f32[9,72,128]{2,1,0:T(8,128)S(1)}, f32[9,72,128]{2,1,0:T(8,128)}, u32[]{:S(2)}, u32[]{:S(2)}) collective-permute-start(f32[9,72,128]{2,1,0:T(8,128)S(1)} %get-tuple-element.34), channel_id=1, source_target_pairs={{1,2},{2,1},{3,4},{4,3},{5,6},{6,5},{9,10},{10,9},{11,12},{12,11},... | collective-permute-start | bytes 995336 | tf_op jit(solution)/shard_map/ppermute | solution.py:521
  (9 other events, 15.7 us)

commit v2 on v1

--- a/solution.py
+++ b/solution.py
@@ -48,28 +48,24 @@
     return pltpu.roll(value, HALF, value.ndim - 1)
 
 
-def pack_kernel(obj_ref, ce_ref, co_ref, ev_ref, od_ref):
+def pack_kernel(first_ref, last_ref, ce_ref, co_ref):
+    col_odd = lax.axis_index("col") % 2
+    first = lanes_of((HALF, LANE)) < HALF
+    for c in range(8):
+        left = first_ref[c]
+        right = last_ref[c]
+        to_left = jnp.where(first, left[:HALF], halves_swapped(left[HALF:]))
+        to_right = jnp.where(first, halves_swapped(right[HALF:]), right[:HALF])
+        ce_ref[c] = jnp.where(col_odd == 1, to_left, to_right)
+        co_ref[c] = jnp.where(col_odd == 1, to_right, to_left)
+
+
+def comb_kernel(obj_ref, ce_ref, co_ref, comb_ref, ev_ref, od_ref):
     row_odd = lax.axis_index("row") % 2
     col_odd = lax.axis_index("col") % 2
     first = lanes_of((HALF, LANE)) < HALF
     ev_start = pl.multiple_of((1 - row_odd) * HALF, HALF)
     od_start = pl.multiple_of(row_odd * HALF, HALF)
-    for c in range(8):
-        left = obj_ref[c, :, 0:LANE]
-        right = obj_ref[c, :, 3 * LANE : 4 * LANE]
-        to_left = jnp.where(first, left[:HALF], halves_swapped(left[HALF:]))
-        to_right = jnp.where(first, halves_swapped(right[HALF:]), right[:HALF])
-        ce_ref[c] = jnp.where(col_odd == 1, to_left, to_right)
-        co_ref[c] = jnp.where(col_odd == 1, to_right, to_left)
-        for t in range(4):
-            ev_ref[t, c] = obj_ref[c, pl.ds(ev_start, HALF), t * LANE : (t + 1) * LANE]
-            od_ref[t, c] = obj_ref[c, pl.ds(od_start, HALF), t * LANE : (t + 1) * LANE]
-
-
-def comb_kernel(ce_ref, co_ref, comb_ref, ev_ref, od_ref):
-    row_odd = lax.axis_index("row") % 2
-    col_odd = lax.axis_index("col") % 2
-    first = lanes_of((HALF, LANE)) < HALF
     for c in range(8):
         ce = ce_ref[c]
         co = co_ref[c]
@@ -79,8 +75,11 @@
         bottom = halves_swapped(jnp.where(first, from_left, from_right))
         comb_ref[c, :HALF] = top
         comb_ref[c, HALF:] = bottom
-        ev_ref[c] = jnp.where(row_odd == 1, top, bottom)
-        od_ref[c] = jnp.where(row_odd == 1, bottom, top)
+        ev_ref[4, c] = jnp.where(row_odd == 1, top, bottom)
+        od_ref[4, c] = jnp.where(row_odd == 1, bottom, top)
+        for t in range(4):
+            ev_ref[t, c] = obj_ref[c, pl.ds(ev_start, HALF), t * LANE : (t + 1) * LANE]
+            od_ref[t, c] = obj_ref[c, pl.ds(od_start, HALF), t * LANE : (t + 1) * LANE]
 
 
 def slots_kernel(
@@ -89,10 +88,8 @@
     count_ref,
     obj_ref,
     comb_ref,
-    evm_ref,
-    odm_ref,
-    evc_ref,
-    odc_ref,
+    ev_ref,
+    od_ref,
     meas_ref,
     probe_ref,
     phase_re_ref,
@@ -102,10 +99,8 @@
     right_f_ref,
     right_b_ref,
     u_ref,
-    out_evm,
-    out_odm,
-    out_evc,
-    out_odc,
+    out_ev,
+    out_od,
     own_ref,
     frame,
     accum,
@@ -121,10 +116,8 @@
     for t in range(4):
         copies.append((obj_ref.at[:, :, t * LANE : (t + 1) * LANE], frame.at[t, :, HALF:192, :]))
     copies.append((comb_ref, frame.at[4, :, HALF:192, :]))
-    copies.append((evm_ref, frame.at[0:4, :, pl.ds(ev_at, HALF), :]))
-    copies.append((odm_ref, frame.at[0:4, :, pl.ds(od_at, HALF), :]))
-    copies.append((evc_ref, frame.at[4, :, pl.ds(ev_at, HALF), :]))
-    copies.append((odc_ref, frame.at[4, :, pl.ds(od_at, HALF), :]))
+    copies.append((ev_ref, frame.at[:, :, pl.ds(ev_at, HALF), :]))
+    copies.append((od_ref, frame.at[:, :, pl.ds(od_at, HALF), :]))
     started = [pltpu.make_async_copy(src, dst, sems.at[i]) for i, (src, dst) in enumerate(copies)]
     for item in started:
         item.start()
@@ -274,12 +267,12 @@
     ev_from = pl.multiple_of((1 - row_odd) * 184, 8)
     od_from = pl.multiple_of(row_odd * 184, 8)
     for t in range(4):
-        out_evm[t] = accum[t, :, pl.ds(ev_from, STRIP), :]
-        out_odm[t] = accum[t, :, pl.ds(od_from, STRIP), :]
-    out_evc[0:8] = accum[4, :, pl.ds(ev_from, STRIP), :]
-    out_odc[0:8] = accum[4, :, pl.ds(od_from, STRIP), :]
-    out_evc[8] = extra[pl.ds(ev_from, STRIP), :]
-    out_odc[8] = extra[pl.ds(od_from, STRIP), :]
+        out_ev[9 + 8 * t : 17 + 8 * t] = accum[t, :, pl.ds(ev_from, STRIP), :]
+        out_od[9 + 8 * t : 17 + 8 * t] = accum[t, :, pl.ds(od_from, STRIP), :]
+    out_ev[0:8] = accum[4, :, pl.ds(ev_from, STRIP), :]
+    out_od[0:8] = accum[4, :, pl.ds(od_from, STRIP), :]
+    out_ev[8] = extra[pl.ds(ev_from, STRIP), :]
+    out_od[8] = extra[pl.ds(od_from, STRIP), :]
     own_ref[0:8] = accum[4, :, 56:200, :]
     own_ref[8] = extra[56:200, :]
     for t in range(TILES):
@@ -303,10 +296,8 @@
 
 def denoise_kernel(
     u_ref,
-    evm_ref,
-    odm_ref,
-    evc_ref,
-    odc_ref,
+    ev_ref,
+    od_ref,
     ce_ref,
     co_ref,
     conv_ref,
@@ -318,6 +309,7 @@
     cond_st,
     conv_sc,
     map_sc,
+    half_sc,
 ):
     row_id = lax.axis_index("row")
     col_id = lax.axis_index("col")
@@ -338,8 +330,9 @@
     def combine(t, c):
         top = u_ref[t, c, :STRIP]
         bottom = u_ref[t, c, STRIP:]
-        ev = evc_ref[c] if t == 4 else evm_ref[t, c]
-        od = odc_ref[c] if t == 4 else odm_ref[t, c]
+        plane = c if t == 4 else 9 + 8 * t + c
+        ev = ev_ref[plane]
+        od = od_ref[plane]
         top = top + jnp.where(row_odd == 1, ev, od)
         bottom = bottom + jnp.where(row_odd == 1, od, ev)
         if t in (0, 3):
@@ -399,42 +392,58 @@
                 cond_st[1, dx, pl.ds(at, 16), :] = low
             return carry
 
-        lax.fori_loop(0, 4 * ROWS_KEPT // 16, body, 0)
-
-    ones = {w: jnp.ones((16, w), bf16) for w in (LANE, 2 * LANE)}
-
-    def layer_pass(layer, groups, read_at, store, write_at, chunks):
-        weights = conv_sc[layer]
-        both = map_sc[layer]
-        single = map_sc[layer, 0:32]
+        lax.fori_loop(0, 4 * ROWS_KEPT // 16, body, 0, unroll=5)
+
+    ones = jnp.ones((16, 640), bf16)
+
+    def layer_pass(layer, groups, read_at, store, write_at, width):
         bias = bias_ref[layer]
 
-        def body(g, carry):
+        def first_map(g, slot):
             src = pl.multiple_of(read_at + g * 32, 16)
+            pieces = [cond_st[part, dx, pl.ds(src, KDX), :width] for part in (0, 1) for dx in range(3)]
+            pieces = pieces + pieces[:3] + [ones[:, :width]]
+            half_sc[slot, :, :width] = jnp.dot(
+                conv_sc[layer], jnp.concatenate(pieces, axis=0), preferred_element_type=f32
+            )
+
+        def second_map(g, slot):
             dst = pl.multiple_of(write_at + g * 32, 8)
-            for begin, width in chunks:
-                pieces = [cond_st[part, dx, pl.ds(src, KDX), begin : begin + width] for part in (0, 1) for dx in range(3)]
-                pieces = pieces + pieces[:3] + [ones[width]]
-                half = jnp.dot(weights, jnp.concatenate(pieces, axis=0), preferred_element_type=f32)
-                hidden = half + half * jnp.tanh(half)
-                high, low = split(hidden)
-                out = jnp.dot(both, high, preferred_element_type=f32)
-                term = out[:32] + out[32:] + jnp.dot(single, low, preferred_element_type=f32)
-                for j in range(width // LANE):
-                    t = begin // LANE + j
-                    bit = term[:, j * LANE : (j + 1) * LANE]
-                    store[t, pl.ds(dst, 32), :] = store[t, pl.ds(dst, 32), :] + (bit + bias)
+            half = half_sc[slot, :, :width]
+            hidden = half + half * jnp.tanh(half)
+            high, low = split(hidden)
+            out = jnp.dot(map_sc[layer], high, preferred_element_type=f32)
+            low_out = jnp.dot(map_sc[layer, 0:32], low, preferred_element_type=f32)
+            term = out[:32] + out[32:] + low_out
+            for t in range(width // LANE):
+                bit = term[:, t * LANE : (t + 1) * LANE]
+                store[t, pl.ds(dst, 32), :] = store[t, pl.ds(dst, 32), :] + (bit + bias)
+
+        first_map(0, 0)
+        pairs_whole = (groups - 1) // 2
+
+        def body(i, carry):
+            first_map(2 * i + 1, 1)
+            second_map(2 * i, 0)
+            first_map(2 * i + 2, 0)
+            second_map(2 * i + 1, 1)
             return carry
 
-        lax.fori_loop(0, groups, body, 0)
-
-    wide = ((0, 256), (256, 256), (512, 128))
+        lax.fori_loop(0, pairs_whole, body, 0)
+        done = 2 * pairs_whole
+        if groups - done == 2:
+            first_map(done + 1, 1)
+            second_map(done, 0)
+            second_map(done + 1, 1)
+        else:
+            second_map(done, 0)
+
     prepare(low_st, -5)
-    layer_pass(0, 17, 0, up_st, 8, wide)
+    layer_pass(0, 17, 0, up_st, 8, 640)
     prepare(up_st, -4)
-    layer_pass(1, 17, 0, low_st, 16, wide)
+    layer_pass(1, 17, 0, low_st, 16, 640)
     prepare(low_st, -5)
-    layer_pass(2, 16, 16, up_st, 16, wide[:2])
+    layer_pass(2, 16, 16, up_st, 16, 512)
     for t in range(4):
         for c in range(4):
             out_ref[c, :, t * LANE : (t + 1) * LANE] = low_st[t, pl.ds(20 + c, 128, stride=4), :]
@@ -486,6 +495,25 @@
     return jax.ShapeDtypeStruct(shape, f32)
 
 
+def denoise_call(*operands):
+    return pl.pallas_call(
+        denoise_kernel,
+        out_shape=sds(8, 128, 512),
+        in_specs=[vmem()] * 8,
+        out_specs=vmem(),
+        scratch_shapes=[
+            pltpu.VMEM((TILES, 4 * ROWS_KEPT, LANE), f32),
+            pltpu.VMEM((TILES, 4 * ROWS_KEPT, LANE), f32),
+            pltpu.VMEM((2, 3, 4 * ROWS_KEPT, 640), bf16),
+            pltpu.VMEM((3, 256, KTOT), bf16),
+            pltpu.VMEM((3, 64, 256), bf16),
+            pltpu.VMEM((2, 256, 640), f32),
+        ],
+        compiler_params=params(56),
+        name="denoise",
+    )(*operands)
+
+
 def per_device(
     object_field,
     probe_field,
@@ -521,51 +549,54 @@
         return lax.ppermute(x, "col", pairs(cols, 1))
 
     obj = object_field.reshape(8, 128, 512)
-    ce, co, evm, odm = pl.pallas_call(
+    def edge(index):
+        return pl.BlockSpec((8, 128, LANE), lambda i: (0, 0, index))
+
+    def whole(*shape):
+        return pl.BlockSpec(shape, lambda i: (0,) * len(shape))
+
+    ce, co = pl.pallas_call(
         pack_kernel,
-        out_shape=[sds(8, HALF, LANE), sds(8, HALF, LANE), sds(4, 8, HALF, LANE), sds(4, 8, HALF, LANE)],
-        in_specs=[vmem()],
-        out_specs=[vmem()] * 4,
+        out_shape=[sds(8, HALF, LANE)] * 2,
+        grid=(1,),
+        in_specs=[edge(0), edge(3)],
+        out_specs=[whole(8, HALF, LANE)] * 2,
         compiler_params=params(32),
         name="pack",
-    )(obj)
-    odm = row_od(odm)
+    )(obj, obj)
     ce = col_ev(ce)
     co = col_od(co)
-    evm = row_ev(evm)
-    comb, evc, odc = pl.pallas_call(
+    comb, ev, od = pl.pallas_call(
         comb_kernel,
-        out_shape=[sds(8, 128, LANE), sds(8, HALF, LANE), sds(8, HALF, LANE)],
-        in_specs=[vmem()] * 2,
+        out_shape=[sds(8, 128, LANE), sds(TILES, 8, HALF, LANE), sds(TILES, 8, HALF, LANE)],
+        in_specs=[vmem()] * 3,
         out_specs=[vmem()] * 3,
         compiler_params=params(32),
         name="comb",
-    )(ce, co)
-    odc = row_od(odc)
-    evc = row_ev(evc)
+    )(obj, ce, co)
+    od = row_od(od)
+    ev = row_ev(ev)
     phase_re = jnp.cos(propagator_phase)
     phase_im = jnp.sin(propagator_phase)
     tables = [jnp.asarray(m) for m in dft_matrices()]
     anywhere = pl.BlockSpec(memory_space=pl.ANY)
-    u, evm, odm, evc, odc, own = pl.pallas_call(
+    u, ev, od, own = pl.pallas_call(
         slots_kernel,
         out_shape=[
             sds(TILES, 8, BAND, LANE),
-            sds(4, 8, STRIP, LANE),
-            sds(4, 8, STRIP, LANE),
-            sds(9, STRIP, LANE),
-            sds(9, STRIP, LANE),
+            sds(41, STRIP, LANE),
+            sds(41, STRIP, LANE),
             sds(9, BAND, LANE),
         ],
-        in_specs=[smem()] * 3 + [anywhere] * 6 + [vmem()] * 8,
-        out_specs=[vmem()] * 6,
+        in_specs=[smem()] * 3 + [anywhere] * 4 + [vmem()] * 8,
+        out_specs=[vmem()] * 4,
         scratch_shapes=[
             pltpu.VMEM((TILES, 8, 256, LANE), f32),
             pltpu.VMEM((TILES, 8, 256, LANE), f32),
             pltpu.VMEM((4, 4, 2, LANE, LANE), f32),
             pltpu.VMEM((5, 4, 2, LANE, LANE), f32),
             pltpu.VMEM((256, LANE), f32),
-            pltpu.SemaphoreType.DMA((9,)),
+            pltpu.SemaphoreType.DMA((7,)),
         ],
         compiler_params=params(56),
         name="slots",
@@ -575,46 +606,29 @@
         tile_counts.reshape(-1),
         obj,
         comb,
-        evm,
-        odm,
-        evc,
-        odc,
+        ev,
+        od,
         intensities.reshape(4, LANE, LANE),
         probe_field,
         phase_re,
         phase_im,
         *tables,
     )
-    odc = row_od(odc)
-    evc = row_ev(evc)
-    odm = row_od(odm)
-    evm = row_ev(evm)
+    od = row_od(od)
+    ev = row_ev(ev)
     ce, co = pl.pallas_call(
         sides_kernel,
         out_shape=[sds(9, STRIP, LANE)] * 2,
-        in_specs=[vmem()] * 3,
-        out_specs=[vmem()] * 2,
+        grid=(1,),
+        in_specs=[whole(9, BAND, LANE), whole(9, STRIP, LANE), whole(9, STRIP, LANE)],
+        out_specs=[whole(9, STRIP, LANE)] * 2,
         compiler_params=params(32),
         name="sides",
-    )(own, evc, odc)
+    )(own, ev, od)
     ce = col_ev(ce)
     co = col_od(co)
     packed, maps, out_bias = conv_matrices(conv_weight, conv_bias, output_weight, output_bias)
-    out = pl.pallas_call(
-        denoise_kernel,
-        out_shape=sds(8, 128, 512),
-        in_specs=[vmem()] * 10,
-        out_specs=vmem(),
-        scratch_shapes=[
-            pltpu.VMEM((TILES, 4 * ROWS_KEPT, LANE), f32),
-            pltpu.VMEM((TILES, 4 * ROWS_KEPT, LANE), f32),
-            pltpu.VMEM((2, 3, 4 * ROWS_KEPT, 640), bf16),
-            pltpu.VMEM((3, 256, KTOT), bf16),
-            pltpu.VMEM((3, 64, 256), bf16),
-        ],
-        compiler_params=params(56),
-        name="denoise",
-    )(u, evm, odm, evc, odc, ce, co, packed, maps, out_bias)
+    out = denoise_call(u, ev, od, ce, co, packed, maps, out_bias)
     return out.reshape(4, 2, 128, 512)
 
 

time: 175 us -> 142 us (0.81)
  the two profiles are of different devices: /device:TPU:28 before, /device:TPU:23 now
where the time goes in v2:
time: 142 us
  Pallas kernels  55.5 us (39%)
  waiting for transfers between devices  46 us (32%)
  starting transfers between devices  19.8 us (14%)
  local copies, waits for them, and re-layouts  17.2 us (12%)
  other arithmetic  2.23 us (2%)
    pallas_call x1, Pallas kernels, denoise_call(): pl.pallas_call(denoise_kernel, out_shape=sds(8, 128, 512), in_specs=[vmem...  28.8 us
    ppermute x2, waiting for transfers between devices, row_od(): return lax.ppermute(x, 'row', pairs(rows, 1))  27.8 us
    pallas_call x1, Pallas kernels, per_device(): pl.pallas_call(slots_kernel, out_shape=[sds(TILES, 8, BAND, LANE), sds(41...  25.3 us
    ppermute x2, waiting for transfers between devices, col_od(): return lax.ppermute(x, 'col', pairs(cols, 1))  15.4 us
    ppermute x2, starting transfers between devices, col_od(): return lax.ppermute(x, 'col', pairs(cols, 1))  12.6 us
    add x6, local copies, waits for them, and re-layouts, conv_matrices(): sum((hot[:, dy][:, None, None, :, None] * jnp.transpose(w[layer, dy], (1,...  6.33 us
    ppermute x2, starting transfers between devices, row_od(): return lax.ppermute(x, 'row', pairs(rows, 1))  5.47 us
    unnamed x48, local copies, waits for them, and re-layouts  5.13 us
  transfers between devices with their start and end apart: 8, of which 6 were waited for; matrix products, arithmetic and copies ran while one was open for 10% of the time, Pallas kernels for 0%

profile of v2, /device:TPU:23, one launch (start us, length us, event | category | flops | bytes accessed | tf_op | source)
XLA Modules:
  0.0 141.7 jit_solution(5347837234289138102)
XLA Ops:
  0.0 1.6 %copy-done = f32[4,2,128,512]{3,2,1,0:T(8,128)S(1)} copy-done((f32[4,2,128,512]{3,2,1,0:T(8,128)S(1)}, f32[4,2,128,512]{3,2,1,0:T(8,128)}, u32[]{:S(2)}) %copy-start) | copy-done | bytes 2097176
  1.9 6.2 %collective-permute-start.1 = (f32[8,64,128]{2,1,0:T(8,128)S(1)}, f32[8,64,128]{2,1,0:T(8,128)S(1)}, u32[]{:S(2)}, u32[]{:S(2)}) collective-permute-start(f32[8,64,128]{2,1,0:T(8,128)S(1)} %get-tuple-element.17), channel_id=1, source_target_pairs={{1,2},{2,1},{3,4},{4,3},{5,6},{6,5},{9,10},{10,9},{11,12},{12,11},... | collective-permute-start | bytes 786440 | tf_op jit(solution)/shard_map/ppermute | solution.py:549
  8.1 2.4 %collective-permute-done.ce_ref = f32[8,64,128]{2,1,0:T(8,128)S(1)} collective-permute-done((f32[8,64,128]{2,1,0:T(8,128)S(1)}, f32[8,64,128]{2,1,0:T(8,128)S(1)}, u32[]{:S(2)}, u32[]{:S(2)}) %collective-permute-start) | collective-permute-done | bytes 262176 | tf_op jit(solution)/shard_map/ppermute | solution.py:546
  10.6 7.0 %collective-permute-done.1.co_ref = f32[8,64,128]{2,1,0:T(8,128)S(1)} collective-permute-done((f32[8,64,128]{2,1,0:T(8,128)S(1)}, f32[8,64,128]{2,1,0:T(8,128)S(1)}, u32[]{:S(2)}, u32[]{:S(2)}) %collective-permute-start.1) | collective-permute-done | bytes 262176 | tf_op jit(solution)/shard_map/ppermute | solution.py:549
  18.6 1.5 %collective-permute-start.2 = (f32[5,8,64,128]{3,2,1,0:T(8,128)S(1)}, f32[5,8,64,128]{3,2,1,0:T(8,128)S(1)}, u32[]{:S(2)}, u32[]{:S(2)}) collective-permute-start(f32[5,8,64,128]{3,2,1,0:T(8,128)S(1)} %get-tuple-element.19), channel_id=1, source_target_pairs={{0,8},{8,0},{16,24},{24,16},{32,40},{40,32},{48,56},{56,48},{64,72... | collective-permute-start | bytes 3932168 | tf_op jit(solution)/shard_map/ppermute | solution.py:540
  20.2 2.7 %collective-permute-start.3 = (f32[5,8,64,128]{3,2,1,0:T(8,128)S(1)}, f32[5,8,64,128]{3,2,1,0:T(8,128)S(1)}, u32[]{:S(2)}, u32[]{:S(2)}) collective-permute-start(f32[5,8,64,128]{3,2,1,0:T(8,128)S(1)} %get-tuple-element.20), channel_id=1, source_target_pairs={{8,16},{16,8},{24,32},{32,24},{40,48},{48,40},{56,64},{64,56},{72,... | collective-permute-start | bytes 3932168 | tf_op jit(solution)/shard_map/ppermute | solution.py:543
  23.6 0.9 fusion
  24.5 16.8 %collective-permute-done.3.od_ref = f32[5,8,64,128]{3,2,1,0:T(8,128)S(1)} collective-permute-done((f32[5,8,64,128]{3,2,1,0:T(8,128)S(1)}, f32[5,8,64,128]{3,2,1,0:T(8,128)S(1)}, u32[]{:S(2)}, u32[]{:S(2)}) %collective-permute-start.3) | collective-permute-done | bytes 1310752 | tf_op jit(solution)/shard_map/ppermute | solution.py:543
  41.2 1.1 copy-done.7
  42.3 25.3 %slots.1 = (f32[5,8,144,128]{3,2,1,0:T(8,128)}, f32[41,72,128]{2,1,0:T(8,128)}, f32[41,72,128]{2,1,0:T(8,128)}, f32[9,144,128]{2,1,0:T(8,128)}) custom-call(s32[4]{0:T(128)} %bitcast.66, s32[4]{0:T(128)} %bitcast.67, s32[1]{0:T(128)} %bitcast.59.count_ref, f32[8,128,512]{2,1,0:T(8,128)} %bitcast.60, f32[8,128,128]{2,1,0:T(8,128)} %copy-done.4, ...), custom_call_target="tpu_custom_call" | custom-call | tf_op jit(solution)/shard_map/slots/pallas_call | solution.py:583
  67.7 2.8 %collective-permute-start.5 = (f32[41,72,128]{2,1,0:T(8,128)}, f32[41,72,128]{2,1,0:T(8,128)S(1)}, u32[]{:S(2)}, u32[]{:S(2)}) collective-permute-start(f32[41,72,128]{2,1,0:T(8,128)} %get-tuple-element.23), channel_id=1, source_target_pairs={{8,16},{16,8},{24,32},{32,24},{40,48},{48,40},{56,64},{64,56},{72,... | collective-permute-start | bytes 4534280 | tf_op jit(solution)/shard_map/ppermute | solution.py:543
  70.6 1.5 %multiply_add_fusion.2 = (f32[8,32,3,12,4]{1,0,4,3,2:T(8,128)}, f32[8,32,3,12,4]{1,0,4,3,2:T(8,128)}, f32[8,32,3,12,4]{1,0,4,3,2:T(8,128)}) fusion(f32[32,3,4]{0,2,1:T(4,128)S(1)} %get-tuple-element.36, f32[8,12]{0,1:T(8,128)S(1)} %copy-done.17, f32[32,3,4]{0,2,1:T(4,128)S(1)} %get-tuple-element.37, f32[8,12]{0,1:T(8,128)S(1)} %copy-done.16, ...), kind=kLoop, calls=%fused_computation.3 | loop fusion | flops 552960 | bytes 458112 | tf_op jit(solution)/shard_map/add | solution.py:483
  72.1 1.3 add.74
  74.2 1.3 add.77
  76.3 1.3 add.80
  77.6 0.9 copy.37
  78.5 1.2 tile.20
  80.2 11.1 %collective-permute-done.5.odc_ref.od_ref = f32[41,72,128]{2,1,0:T(8,128)S(1)} collective-permute-done((f32[41,72,128]{2,1,0:T(8,128)}, f32[41,72,128]{2,1,0:T(8,128)S(1)}, u32[]{:S(2)}, u32[]{:S(2)}) %collective-permute-start.5) | collective-permute-done | bytes 1511456 | tf_op jit(solution)/shard_map/ppermute | solution.py:543
  91.2 1.5 %copy-done.3 = f32[9,144,128]{2,1,0:T(8,128)S(1)} copy-done((f32[9,144,128]{2,1,0:T(8,128)S(1)}, f32[9,144,128]{2,1,0:T(8,128)}, u32[]{:S(2)}) %copy-start.3) | copy-done | bytes 663576
  92.8 0.9 sides.1
  93.7 6.4 %collective-permute-start.7 = (f32[9,72,128]{2,1,0:T(8,128)S(1)}, f32[9,72,128]{2,1,0:T(8,128)S(1)}, u32[]{:S(2)}, u32[]{:S(2)}) collective-permute-start(f32[9,72,128]{2,1,0:T(8,128)S(1)} %get-tuple-element.26), channel_id=1, source_target_pairs={{1,2},{2,1},{3,4},{4,3},{5,6},{6,5},{9,10},{10,9},{11,12},{12,11},... | collective-permute-start | bytes 995336 | tf_op jit(solution)/shard_map/ppermute | solution.py:549
  100.2 2.4 %concatenate.3.conv_ref = f32[3,256,448]{2,1,0:T(8,128)} concatenate(f32[3,256,144]{2,1,0:T(8,128)S(1)} %pad_maximum_fusion, f32[3,256,144]{2,1,0:T(8,128)S(1)} %pad_maximum_fusion, f32[3,256,144]{2,1,0:T(8,128)S(1)} %pad_maximum_fusion, f32[3,256,1]{2,1,0:T(8,128)S(1)} %copy-done.5, f32[3,256,1]{2,1,0:T(8,128)S(1)} %copy-done.5, f32[3,256,14]{2,1,0:T(8,128)S(1)} %broadcast_in_dim.4), dimensions={2} | concatenate | bytes 2752512 | tf_op jit(solution)/shard_map/concatenate | solution.py:487
  103.7 8.5 %collective-permute-done.7.co_ref = f32[9,72,128]{2,1,0:T(8,128)S(1)} collective-permute-done((f32[9,72,128]{2,1,0:T(8,128)S(1)}, f32[9,72,128]{2,1,0:T(8,128)S(1)}, u32[]{:S(2)}, u32[]{:S(2)}) %collective-permute-start.7) | collective-permute-done | bytes 331808 | tf_op jit(solution)/shard_map/ppermute | solution.py:549
  112.9 28.8 %denoise.1 = f32[8,128,512]{2,1,0:T(8,128)} custom-call(f32[5,8,144,128]{3,2,1,0:T(8,128)} %get-tuple-element.21.u_ref, f32[41,72,128]{2,1,0:T(8,128)} %copy-done.1, f32[41,72,128]{2,1,0:T(8,128)} %copy-done.2, f32[9,72,128]{2,1,0:T(8,128)} %copy-done.11, f32[9,72,128]{2,1,0:T(8,128)} %copy-done.12, f32[3,256,448]{2,1,0:T(8,128)} %concatenate.3.conv_ref, ...), custom_call_target="tpu_custom_call" | custom-call | tf_op jit(solution)/shard_map/denoise/pallas_call | solution.py:499
  (69 shorter events, 5.6 us)
Async XLA Ops:
  1.8 21.8 %copy-start.13 = (f32[128,128]{1,0:T(8,128)S(1)}, f32[128,128]{1,0:T(8,128)}, u32[]{:S(2)}) copy-start(f32[128,128]{1,0:T(8,128)} %param.27) | copy-start | bytes 196612
  1.8 8.8 %collective-permute-start = (f32[8,64,128]{2,1,0:T(8,128)S(1)}, f32[8,64,128]{2,1,0:T(8,128)S(1)}, u32[]{:S(2)}, u32[]{:S(2)}) collective-permute-start(f32[8,64,128]{2,1,0:T(8,128)S(1)} %get-tuple-element.16), channel_id=1, source_target_pairs={{0,1},{1,0},{2,3},{3,2},{4,5},{5,4},{6,7},{7,6},{8,9},{9,8},{10,11... | collective-permute-start | bytes 786440 | tf_op jit(solution)/shard_map/ppermute | solution.py:546
  1.9 15.6 %collective-permute-start.1 = (f32[8,64,128]{2,1,0:T(8,128)S(1)}, f32[8,64,128]{2,1,0:T(8,128)S(1)}, u32[]{:S(2)}, u32[]{:S(2)}) collective-permute-start(f32[8,64,128]{2,1,0:T(8,128)S(1)} %get-tuple-element.17), channel_id=1, source_target_pairs={{1,2},{2,1},{3,4},{4,3},{5,6},{6,5},{9,10},{10,9},{11,12},{12,11},... | collective-permute-start | bytes 786440 | tf_op jit(solution)/shard_map/ppermute | solution.py:549
  18.6 5.8 %collective-permute-start.2 = (f32[5,8,64,128]{3,2,1,0:T(8,128)S(1)}, f32[5,8,64,128]{3,2,1,0:T(8,128)S(1)}, u32[]{:S(2)}, u32[]{:S(2)}) collective-permute-start(f32[5,8,64,128]{3,2,1,0:T(8,128)S(1)} %get-tuple-element.19), channel_id=1, source_target_pairs={{0,8},{8,0},{16,24},{24,16},{32,40},{40,32},{48,56},{56,48},{64,72... | collective-permute-start | bytes 3932168 | tf_op jit(solution)/shard_map/ppermute | solution.py:540
  20.2 21.0 %collective-permute-start.3 = (f32[5,8,64,128]{3,2,1,0:T(8,128)S(1)}, f32[5,8,64,128]{3,2,1,0:T(8,128)S(1)}, u32[]{:S(2)}, u32[]{:S(2)}) collective-permute-start(f32[5,8,64,128]{3,2,1,0:T(8,128)S(1)} %get-tuple-element.20), channel_id=1, source_target_pairs={{8,16},{16,8},{24,32},{32,24},{40,48},{48,40},{56,64},{64,56},{72,... | collective-permute-start | bytes 3932168 | tf_op jit(solution)/shard_map/ppermute | solution.py:543
  24.5 16.8 %copy-start.6 = (f32[5,8,64,128]{3,2,1,0:T(8,128)}, f32[5,8,64,128]{3,2,1,0:T(8,128)S(1)}, u32[]{:S(2)}) copy-start(f32[5,8,64,128]{3,2,1,0:T(8,128)S(1)} %collective-permute-done.2.ev_ref) | copy-start | bytes 3932164
  42.3 28.2 %copy-start.14 = (f32[3,9,32,4]{2,3,1,0:T(4,128)S(1)}, f32[3,9,32,4]{2,3,1,0:T(4,128)}, u32[]{:S(2)}) copy-start(f32[3,9,32,4]{2,3,1,0:T(4,128)} %param.32) | copy-start | bytes 41476
  42.3 28.3 %copy-start.15 = (f32[8,12]{0,1:T(8,128)S(1)}, f32[8,12]{0,1:T(8,128)}, u32[]{:S(2)}) copy-start(f32[8,12]{0,1:T(8,128)} %constant.39) | copy-start | bytes 1156
  42.3 28.3 %copy-start.16 = (f32[8,12]{0,1:T(8,128)S(1)}, f32[8,12]{0,1:T(8,128)}, u32[]{:S(2)}) copy-start(f32[8,12]{0,1:T(8,128)} %constant.40) | copy-start | bytes 1156
  42.3 28.3 %copy-start.17 = (f32[8,12]{0,1:T(8,128)S(1)}, f32[8,12]{0,1:T(8,128)}, u32[]{:S(2)}) copy-start(f32[8,12]{0,1:T(8,128)} %constant.41) | copy-start | bytes 1156
  42.3 28.3 %copy-start.18 = (f32[8,12]{0,1:T(8,128)S(1)}, f32[8,12]{0,1:T(8,128)}, u32[]{:S(2)}) copy-start(f32[8,12]{0,1:T(8,128)} %constant.42) | copy-start | bytes 1156
  42.3 28.3 %copy-start.19 = (f32[8,12]{0,1:T(8,128)S(1)}, f32[8,12]{0,1:T(8,128)}, u32[]{:S(2)}) copy-start(f32[8,12]{0,1:T(8,128)} %constant.43) | copy-start | bytes 1156
  67.6 12.5 %collective-permute-start.4 = (f32[41,72,128]{2,1,0:T(8,128)}, f32[41,72,128]{2,1,0:T(8,128)S(1)}, u32[]{:S(2)}, u32[]{:S(2)}) collective-permute-start(f32[41,72,128]{2,1,0:T(8,128)} %get-tuple-element.22), channel_id=1, source_target_pairs={{0,8},{8,0},{16,24},{24,16},{32,40},{40,32},{48,56},{56,48},{64,72... | collective-permute-start | bytes 4534280 | tf_op jit(solution)/shard_map/ppermute | solution.py:540
  67.7 23.5 %collective-permute-start.5 = (f32[41,72,128]{2,1,0:T(8,128)}, f32[41,72,128]{2,1,0:T(8,128)S(1)}, u32[]{:S(2)}, u32[]{:S(2)}) collective-permute-start(f32[41,72,128]{2,1,0:T(8,128)} %get-tuple-element.23), channel_id=1, source_target_pairs={{8,16},{16,8},{24,32},{32,24},{40,48},{48,40},{56,64},{64,56},{72,... | collective-permute-start | bytes 4534280 | tf_op jit(solution)/shard_map/ppermute | solution.py:543
  73.4 5.1 %copy-start.23 = (f32[3,32]{1,0:T(4,128)S(1)}, f32[3,32]{1,0:T(4,128)}, u32[]{:S(2)}) copy-start(f32[3,32]{1,0:T(4,128)} %param.33) | copy-start | bytes 1156
  73.4 6.3 %copy-start.20 = (f32[3,4,32]{2,1,0:T(4,128)S(1)}, f32[3,4,32]{2,1,0:T(4,128)}, u32[]{:S(2)}) copy-start(f32[3,4,32]{2,1,0:T(4,128)} %param.34) | copy-start | bytes 4612
  80.2 13.5 %copy-start.1 = (f32[41,72,128]{2,1,0:T(8,128)}, f32[41,72,128]{2,1,0:T(8,128)S(1)}, u32[]{:S(2)}) copy-start(f32[41,72,128]{2,1,0:T(8,128)S(1)} %collective-permute-done.4.evc_ref.ev_ref) | copy-start | bytes 4534276
  92.8 7.3 %copy-start.8 = (f32[1,256,144]{2,1,0:T(8,128)S(1)}, f32[1,256,144]{2,1,0:T(8,128)}, u32[]{:S(2)}) copy-start(f32[1,256,144]{2,1,0:T(8,128)} %copy.35) | copy-start | bytes 442372
  92.8 7.3 %copy-start.9 = (f32[1,256,144]{2,1,0:T(8,128)S(1)}, f32[1,256,144]{2,1,0:T(8,128)}, u32[]{:S(2)}) copy-start(f32[1,256,144]{2,1,0:T(8,128)} %copy.36) | copy-start | bytes 442372
  92.8 7.4 %copy-start.10 = (f32[1,256,144]{2,1,0:T(8,128)S(1)}, f32[1,256,144]{2,1,0:T(8,128)}, u32[]{:S(2)}) copy-start(f32[1,256,144]{2,1,0:T(8,128)} %copy.37) | copy-start | bytes 442372
  93.7 6.5 %copy-start.5 = (f32[3,256,1]{2,1,0:T(8,128)S(1)}, f32[3,256,1]{2,1,0:T(8,128)}, u32[]{:S(2)}) copy-start(f32[3,256,1]{2,1,0:T(8,128)} %tile.20) | copy-start | bytes 9220
  93.7 10.0 %collective-permute-start.6 = (f32[9,72,128]{2,1,0:T(8,128)}, f32[9,72,128]{2,1,0:T(8,128)S(1)}, u32[]{:S(2)}, u32[]{:S(2)}) collective-permute-start(f32[9,72,128]{2,1,0:T(8,128)} %get-tuple-element.25), channel_id=1, source_target_pairs={{0,1},{1,0},{2,3},{3,2},{4,5},{5,4},{6,7},{7,6},{8,9},{9,8},{10,11... | collective-permute-start | bytes 995336 | tf_op jit(solution)/shard_map/ppermute | solution.py:546
  93.7 18.4 %collective-permute-start.7 = (f32[9,72,128]{2,1,0:T(8,128)S(1)}, f32[9,72,128]{2,1,0:T(8,128)S(1)}, u32[]{:S(2)}, u32[]{:S(2)}) collective-permute-start(f32[9,72,128]{2,1,0:T(8,128)S(1)} %get-tuple-element.26), channel_id=1, source_target_pairs={{1,2},{2,1},{3,4},{4,3},{5,6},{6,5},{9,10},{10,9},{11,12},{12,11},... | collective-permute-start | bytes 995336 | tf_op jit(solution)/shard_map/ppermute | solution.py:549
  103.7 9.3 %copy-start.11 = (f32[9,72,128]{2,1,0:T(8,128)}, f32[9,72,128]{2,1,0:T(8,128)S(1)}, u32[]{:S(2)}) copy-start(f32[9,72,128]{2,1,0:T(8,128)S(1)} %collective-permute-done.6.ce_ref) | copy-start | bytes 995332
  (8 other events, 17.2 us)

commit v3 on v2

--- a/solution.py
+++ b/solution.py
@@ -60,26 +60,39 @@
         co_ref[c] = jnp.where(col_odd == 1, to_right, to_left)
 
 
-def comb_kernel(obj_ref, ce_ref, co_ref, comb_ref, ev_ref, od_ref):
+def strips_kernel(obj_ref, ev_ref, od_ref):
+    row_odd = lax.axis_index("row") % 2
+    ev_start = pl.multiple_of((1 - row_odd) * HALF, HALF)
+    od_start = pl.multiple_of(row_odd * HALF, HALF)
+    for c in range(8):
+        for t in range(4):
+            ev_ref[t, c] = obj_ref[c, pl.ds(ev_start, HALF), t * LANE : (t + 1) * LANE]
+            od_ref[t, c] = obj_ref[c, pl.ds(od_start, HALF), t * LANE : (t + 1) * LANE]
+
+
+def comb_kernel(ce_ref, co_ref, ev_in, od_in, comb_ref, ev_ref, od_ref, comb_sc, sems):
+    del ev_in, od_in
     row_odd = lax.axis_index("row") % 2
     col_odd = lax.axis_index("col") % 2
     first = lanes_of((HALF, LANE)) < HALF
-    ev_start = pl.multiple_of((1 - row_odd) * HALF, HALF)
-    od_start = pl.multiple_of(row_odd * HALF, HALF)
     for c in range(8):
         ce = ce_ref[c]
         co = co_ref[c]
         from_right = jnp.where(col_odd == 1, co, ce)
         from_left = jnp.where(col_odd == 1, ce, co)
-        top = jnp.where(first, from_right, from_left)
-        bottom = halves_swapped(jnp.where(first, from_left, from_right))
-        comb_ref[c, :HALF] = top
-        comb_ref[c, HALF:] = bottom
-        ev_ref[4, c] = jnp.where(row_odd == 1, top, bottom)
-        od_ref[4, c] = jnp.where(row_odd == 1, bottom, top)
-        for t in range(4):
-            ev_ref[t, c] = obj_ref[c, pl.ds(ev_start, HALF), t * LANE : (t + 1) * LANE]
-            od_ref[t, c] = obj_ref[c, pl.ds(od_start, HALF), t * LANE : (t + 1) * LANE]
+        comb_sc[c, :HALF] = jnp.where(first, from_right, from_left)
+        comb_sc[c, HALF:] = halves_swapped(jnp.where(first, from_left, from_right))
+    ev_start = pl.multiple_of((1 - row_odd) * HALF, HALF)
+    od_start = pl.multiple_of(row_odd * HALF, HALF)
+    started = [
+        pltpu.make_async_copy(comb_sc.at[:, pl.ds(od_start, HALF), :], od_ref.at[4], sems.at[0]),
+        pltpu.make_async_copy(comb_sc.at[:, pl.ds(ev_start, HALF), :], ev_ref.at[4], sems.at[1]),
+        pltpu.make_async_copy(comb_sc, comb_ref, sems.at[2]),
+    ]
+    for item in started:
+        item.start()
+    for item in started:
+        item.wait()
 
 
 def slots_kernel(
@@ -90,14 +103,14 @@
     comb_ref,
     ev_ref,
     od_ref,
-    meas_ref,
+    meas_any,
     probe_ref,
     phase_re_ref,
     phase_im_ref,
-    left_f_ref,
-    left_b_ref,
-    right_f_ref,
-    right_b_ref,
+    left_f_any,
+    left_b_any,
+    right_f_any,
+    right_b_any,
     u_ref,
     out_ev,
     out_od,
@@ -107,6 +120,11 @@
     win,
     waves,
     extra,
+    left_f_ref,
+    left_b_ref,
+    right_f_ref,
+    right_b_ref,
+    meas_ref,
     sems,
 ):
     row_odd = lax.axis_index("row") % 2
@@ -119,7 +137,15 @@
     copies.append((ev_ref, frame.at[:, :, pl.ds(ev_at, HALF), :]))
     copies.append((od_ref, frame.at[:, :, pl.ds(od_at, HALF), :]))
     started = [pltpu.make_async_copy(src, dst, sems.at[i]) for i, (src, dst) in enumerate(copies)]
-    for item in started:
+    late = [
+        (left_f_any, left_f_ref),
+        (right_f_any, right_f_ref),
+        (right_b_any, right_b_ref),
+        (left_b_any, left_b_ref),
+        (meas_any, meas_ref),
+    ]
+    later = [pltpu.make_async_copy(src, dst, sems.at[7 + i]) for i, (src, dst) in enumerate(late)]
+    for item in started + later:
         item.start()
     accum[...] = jnp.zeros(accum.shape, f32)
     for item in started:
@@ -146,32 +172,32 @@
             win[c // 2, k, c % 2] = pltpu.roll(jnp.where(keep, here, beyond), turn, 1)
             return carry
 
-        lax.fori_loop(0, 8, take, 0)
+        lax.fori_loop(0, 8, take, 0, unroll=8)
 
     h_re = phase_re_ref[...]
     h_im = phase_im_ref[...]
 
     def left(xs, mat_ref):
-        stack = jnp.concatenate([jnp.concatenate([re, im], axis=0) for re, im in xs], axis=1)
-        high, low = split(stack)
-        out = jnp.dot(
-            mat_ref[...], jnp.concatenate([high, low, high], axis=0), preferred_element_type=f32
-        )
-        return [
-            (out[:LANE, k * LANE : (k + 1) * LANE], out[LANE:, k * LANE : (k + 1) * LANE])
-            for k in range(4)
-        ]
+        outs = []
+        for g in range(0, 4, 2):
+            stack = jnp.concatenate([jnp.concatenate(xs[k], axis=0) for k in (g, g + 1)], axis=1)
+            high, low = split(stack)
+            out = jnp.dot(
+                mat_ref[...], jnp.concatenate([high, low, high], axis=0), preferred_element_type=f32
+            )
+            outs += [(out[:LANE, at : at + LANE], out[LANE:, at : at + LANE]) for at in (0, LANE)]
+        return outs
 
     def right(xs, mat_ref):
-        stack = jnp.concatenate([jnp.concatenate([re, im], axis=1) for re, im in xs], axis=0)
-        high, low = split(stack)
-        out = jnp.dot(
-            jnp.concatenate([high, low, high], axis=1), mat_ref[...], preferred_element_type=f32
-        )
-        return [
-            (out[k * LANE : (k + 1) * LANE, :LANE], out[k * LANE : (k + 1) * LANE, LANE:])
-            for k in range(4)
-        ]
+        outs = []
+        for g in range(0, 4, 2):
+            stack = jnp.concatenate([jnp.concatenate(xs[k], axis=1) for k in (g, g + 1)], axis=0)
+            high, low = split(stack)
+            out = jnp.dot(
+                jnp.concatenate([high, low, high], axis=1), mat_ref[...], preferred_element_type=f32
+            )
+            outs += [(out[at : at + LANE, :LANE], out[at : at + LANE, LANE:]) for at in (0, LANE)]
+        return outs
 
     def forth(xs):
         return right(left(xs, left_f_ref), right_f_ref)
@@ -201,6 +227,8 @@
             waves[s + 1, k, 1] = xs[k][1]
         return carry
 
+    for item in later:
+        item.wait()
     lax.fori_loop(0, 3, forward, 0)
     far = forth(exit_wave(3))
     count = count_ref[0]
@@ -253,7 +281,7 @@
             accum[nxt, c, pl.ds(row, LANE), :] = beyond + jnp.where(keep, 0.0, turned)
             return carry
 
-        lax.fori_loop(0, 8, give, 0)
+        lax.fori_loop(0, 8, give, 0, unroll=8)
 
     wide = lanes_of((256, LANE)) // 8
     gathered = jnp.zeros((256, LANE), f32)
@@ -266,20 +294,40 @@
 
     ev_from = pl.multiple_of((1 - row_odd) * 184, 8)
     od_from = pl.multiple_of(row_odd * 184, 8)
+    moves = [
+        (accum.at[4, :, pl.ds(od_from, STRIP), :], out_od.at[0:8]),
+        (extra.at[pl.ds(od_from, STRIP), :], out_od.at[8]),
+    ]
     for t in range(4):
-        out_ev[9 + 8 * t : 17 + 8 * t] = accum[t, :, pl.ds(ev_from, STRIP), :]
-        out_od[9 + 8 * t : 17 + 8 * t] = accum[t, :, pl.ds(od_from, STRIP), :]
-    out_ev[0:8] = accum[4, :, pl.ds(ev_from, STRIP), :]
-    out_od[0:8] = accum[4, :, pl.ds(od_from, STRIP), :]
-    out_ev[8] = extra[pl.ds(ev_from, STRIP), :]
-    out_od[8] = extra[pl.ds(od_from, STRIP), :]
-    own_ref[0:8] = accum[4, :, 56:200, :]
-    own_ref[8] = extra[56:200, :]
+        moves.append((accum.at[t, :, pl.ds(od_from, STRIP), :], out_od.at[9 + 8 * t : 17 + 8 * t]))
+    moves.append((accum.at[4, :, pl.ds(ev_from, STRIP), :], out_ev.at[0:8]))
+    moves.append((extra.at[pl.ds(ev_from, STRIP), :], out_ev.at[8]))
+    for t in range(4):
+        moves.append((accum.at[t, :, pl.ds(ev_from, STRIP), :], out_ev.at[9 + 8 * t : 17 + 8 * t]))
+    moves.append((accum.at[4, :, 56:200, :], own_ref.at[0:8]))
+    moves.append((extra.at[56:200, :], own_ref.at[8]))
+    sent = [pltpu.make_async_copy(src, dst, sems.at[12 + i]) for i, (src, dst) in enumerate(moves)]
+    for item in sent:
+        item.start()
     for t in range(TILES):
-        u_ref[t] = frame[t, :, 56:200, :] + accum[t, :, 56:200, :]
-
-
-def sides_kernel(own_ref, evc_ref, odc_ref, ce_ref, co_ref):
+        frame[t, :, 56:200, :] = frame[t, :, 56:200, :] + accum[t, :, 56:200, :]
+        item = pltpu.make_async_copy(frame.at[t, :, 56:200, :], u_ref.at[t], sems.at[26 + t])
+        item.start()
+        sent.append(item)
+    for item in sent:
+        item.wait()
+
+
+def sides_kernel(own_any, ev_any, od_any, ce_ref, co_ref, own_ref, evc_ref, odc_ref, sems):
+    started = [
+        pltpu.make_async_copy(own_any, own_ref, sems.at[0]),
+        pltpu.make_async_copy(ev_any.at[0:9], evc_ref, sems.at[1]),
+        pltpu.make_async_copy(od_any.at[0:9], odc_ref, sems.at[2]),
+    ]
+    for item in started:
+        item.start()
+    for item in started:
+        item.wait()
     row_odd = lax.axis_index("row") % 2
     col_odd = lax.axis_index("col") % 2
     first = lanes_of((STRIP, LANE)) < HALF
@@ -294,84 +342,133 @@
         co_ref[c] = jnp.where(col_odd == 1, to_right, to_left)
 
 
+def weights_kernel(taps_ref, bias_ref, map_ref, map_bias_ref, conv_out, map_out, bias_out):
+    def hot(rows, cols, test):
+        a = lax.broadcasted_iota(jnp.int32, (rows, cols), 0)
+        b = lax.broadcasted_iota(jnp.int32, (rows, cols), 1)
+        return jnp.where(test(a, b), 1.0, 0.0).astype(f32)
+
+    def exact(a, b):
+        return jnp.dot(a, b, precision=lax.Precision.HIGHEST, preferred_element_type=f32)
+
+    place = hot(12, KTOT, lambda a, b: (b < 432) & (a == (b % 144) // 48 * 4 + b % 4))
+    row = lax.broadcasted_iota(jnp.int32, (256, KTOT), 0)
+    col = lax.broadcasted_iota(jnp.int32, (256, KTOT), 1)
+    shift = (col % 48) // 4 - row // 32
+    is_bias = (col == 432) | (col == 433)
+    use_low = ((col >= 288) & (col < 432)) | (col == 433)
+    hidden_hot = hot(256, 32, lambda a, b: a % 32 == b)
+    channel_hot = hot(32, 4, lambda a, b: a % 4 == b)
+    spread = hot(32, 256, lambda a, b: a == b % 32)
+    same_row = hot(32, 256, lambda a, b: a // 4 == b // 32)
+    for layer, start in zip(range(3), (2, 2, 0)):
+        bias = jnp.sum(hidden_hot * bias_ref[layer : layer + 1, :], axis=1, keepdims=True)
+        total = jnp.where(is_bias, bias, 0.0)
+        for dy in range(3):
+            part = exact(taps_ref[layer, dy], place)
+            whole = jnp.concatenate([part] * 8, axis=0)
+            total = total + jnp.where((shift == dy + start) & (col < 432), whole, 0.0)
+        high, low = split(total * 0.5)
+        conv_out[layer] = jnp.where(use_low, low.astype(f32), high.astype(f32)).astype(bf16)
+        wide = exact(exact(channel_hot, map_ref[layer]), spread) * same_row
+        high, low = split(wide)
+        map_out[layer, 0:32] = high
+        map_out[layer, 32:64] = low
+        out_bias = jnp.sum(channel_hot * map_bias_ref[layer : layer + 1, :], axis=1, keepdims=True)
+        bias_out[layer] = jnp.broadcast_to(out_bias, (32, LANE))
+
+
+def merge_kernel(u_any, ev_any, od_any, low_st, up_st, u_ref, ev_ref, od_ref, sems):
+    pairs = ((u_any, u_ref), (ev_any, ev_ref), (od_any, od_ref))
+    started = [pltpu.make_async_copy(a, b, sems.at[i]) for i, (a, b) in enumerate(pairs)]
+    for item in started:
+        item.start()
+    for item in started:
+        item.wait()
+    row_odd = lax.axis_index("row") % 2
+
+    def combine(t, c):
+        plane = c if t == 4 else 9 + 8 * t + c
+        ev = ev_ref[plane]
+        od = od_ref[plane]
+        top = u_ref[t, c, :STRIP] + jnp.where(row_odd == 1, ev, od)
+        bottom = u_ref[t, c, STRIP:] + jnp.where(row_odd == 1, od, ev)
+        return jnp.concatenate([top, bottom], axis=0)
+
+    for t in range(TILES):
+        for c in range(4):
+            low_st[t, pl.ds(c, ROWS_KEPT, stride=4), :] = combine(t, c)[3:143]
+            up_st[t, pl.ds(c, ROWS_KEPT, stride=4), :] = combine(t, 4 + c)[4:144]
+
+
 def denoise_kernel(
-    u_ref,
-    ev_ref,
-    od_ref,
+    low_any,
+    up_any,
     ce_ref,
     co_ref,
-    conv_ref,
-    map_ref,
+    conv_sc,
+    map_sc,
     bias_ref,
     out_ref,
     low_st,
     up_st,
     cond_st,
-    conv_sc,
-    map_sc,
     half_sc,
+    sems,
 ):
     row_id = lax.axis_index("row")
     col_id = lax.axis_index("col")
-    row_odd = row_id % 2
     col_odd = col_id % 2
     lane = lanes_of((STRIP, LANE))
     first = lane < HALF
-
-    for layer in range(3):
-        high, low = split(conv_ref[layer])
-        place = lanes_of(high.shape)
-        use_low = ((place >= 288) & (place < 432)) | (place == 433)
-        conv_sc[layer] = jnp.where(use_low, low.astype(f32), high.astype(f32)).astype(bf16)
-        high, low = split(map_ref[layer])
-        map_sc[layer, 0:32] = high
-        map_sc[layer, 32:64] = low
-
-    def combine(t, c):
-        top = u_ref[t, c, :STRIP]
-        bottom = u_ref[t, c, STRIP:]
-        plane = c if t == 4 else 9 + 8 * t + c
-        ev = ev_ref[plane]
-        od = od_ref[plane]
-        top = top + jnp.where(row_odd == 1, ev, od)
-        bottom = bottom + jnp.where(row_odd == 1, od, ev)
-        if t in (0, 3):
-            ce = ce_ref[c]
-            co = co_ref[c]
-            if t == 0:
-                side = jnp.where(col_odd == 1, ce, co)
-                top = top + jnp.where(first, side, 0.0)
-                bottom = bottom + jnp.where(first, halves_swapped(side), 0.0)
-            else:
-                side = jnp.where(col_odd == 1, co, ce)
-                top = top + jnp.where(first, 0.0, side)
-                bottom = bottom + jnp.where(first, 0.0, halves_swapped(side))
-        if t == 4:
-            ce = ce_ref[8]
-            co = co_ref[8]
-            from_left = jnp.where(col_odd == 1, ce, co)
-            from_right = jnp.where(col_odd == 1, co, ce)
-            tail_top = pltpu.roll(from_left, (120 - 8 * c) % LANE, 1)
-            tail_bottom = pltpu.roll(from_left, (HALF + 120 - 8 * c) % LANE, 1)
-            head_top = pltpu.roll(from_right, (HALF - 8 * c) % LANE, 1)
-            head_bottom = pltpu.roll(from_right, (LANE - 8 * c) % LANE, 1)
-            at_tail = lane >= 120
-            at_head = lane < 8
-            top = top + jnp.where(at_tail, tail_top, jnp.where(at_head, head_top, 0.0))
-            bottom = bottom + jnp.where(at_tail, tail_bottom, jnp.where(at_head, head_bottom, 0.0))
-        return jnp.concatenate([top, bottom], axis=0)
-
-    for t in range(TILES):
-        for c in range(4):
-            low_st[t, pl.ds(c, ROWS_KEPT, stride=4), :] = combine(t, c)[3:143]
-            up_st[t, pl.ds(c, ROWS_KEPT, stride=4), :] = combine(t, 4 + c)[4:144]
+    low_copy = pltpu.make_async_copy(low_any, low_st, sems.at[0])
+    up_copy = pltpu.make_async_copy(up_any, up_st, sems.at[1])
+    low_copy.start()
+    up_copy.start()
+
+    def add_sides(c):
+        store = low_st if c < 4 else up_st
+        skip = 3 if c < 4 else 4
+        ce = ce_ref[c]
+        co = co_ref[c]
+        from_left = jnp.where(col_odd == 1, ce, co)
+        from_right = jnp.where(col_odd == 1, co, ce)
+        swapped_left = halves_swapped(from_left)
+        swapped_right = halves_swapped(from_right)
+        ce = ce_ref[8]
+        co = co_ref[8]
+        tail = jnp.where(col_odd == 1, ce, co)
+        head = jnp.where(col_odd == 1, co, ce)
+        tail_top = pltpu.roll(tail, (120 - 8 * c) % LANE, 1)
+        tail_bottom = pltpu.roll(tail, (HALF + 120 - 8 * c) % LANE, 1)
+        head_top = pltpu.roll(head, (HALF - 8 * c) % LANE, 1)
+        head_bottom = pltpu.roll(head, (LANE - 8 * c) % LANE, 1)
+        at_tail = lane >= 120
+        at_head = lane < 8
+        pieces = {
+            0: (jnp.where(first, from_left, 0.0), jnp.where(first, swapped_left, 0.0)),
+            3: (jnp.where(first, 0.0, from_right), jnp.where(first, 0.0, swapped_right)),
+            4: (
+                jnp.where(at_tail, tail_top, jnp.where(at_head, head_top, 0.0)),
+                jnp.where(at_tail, tail_bottom, jnp.where(at_head, head_bottom, 0.0)),
+            ),
+        }
+        for t, both in pieces.items():
+            at = pl.ds(c % 4, ROWS_KEPT, stride=4)
+            whole = jnp.concatenate(both, axis=0)[skip : skip + ROWS_KEPT]
+            store[t, at, :] = store[t, at, :] + whole
+
+    low_copy.wait()
+    for c in range(4):
+        add_sides(c)
+    up_copy.wait()
+    for c in range(4, 8):
+        add_sides(c)
 
     last_row = lax.axis_size("row") - 1
     last_col = lax.axis_size("col") - 1
-    col_from = jnp.where(col_id == 0, 128, 640)
     right_off = jnp.where(col_id == last_col, 512, 576)
     left_off = jnp.where(col_id == 0, 640, 576)
-    del col_from
 
     def prepare(store, first_row):
         row_low = jnp.where(row_id == 0, -first_row * 4, 0)
@@ -471,47 +568,86 @@
     return left_f, left_b, right_f, right_b
 
 
-def conv_matrices(conv_weight, conv_bias, output_weight, output_bias):
-    layers = conv_weight.shape[0]
-    w = conv_weight.reshape(layers, 3, 3, 32, 4) * 0.5
-    blocks = []
-    for layer, start in zip(range(layers), (2, 2, 0)):
-        hot = np.zeros((8, 3, 12), np.float32)
-        for j in range(8):
-            for dy in range(3):
-                hot[j, dy, j + dy + start] = 1.0
-        m = sum(hot[:, dy][:, None, None, :, None] * jnp.transpose(w[layer, dy], (1, 0, 2))[None, :, :, None, :] for dy in range(3))
-        blocks.append(m.reshape(256, 144))
-    main = jnp.stack(blocks)
-    bias = jnp.tile(conv_bias * 0.5, (1, 8))[:, :, None]
-    packed = jnp.concatenate([main, main, main, bias, bias, jnp.zeros((layers, 256, 14), f32)], axis=2)
-    eye = np.eye(8, dtype=np.float32)
-    maps = (eye[None, :, None, :, None] * output_weight[:, None, :, None, :]).reshape(layers, 32, 256)
-    out_bias = jnp.broadcast_to(jnp.tile(output_bias, (1, 8))[:, :, None], (layers, 32, LANE))
-    return packed, maps, out_bias
-
-
 def sds(*shape):
     return jax.ShapeDtypeStruct(shape, f32)
 
 
-def denoise_call(*operands):
+def slots_call(*operands):
+    anywhere = pl.BlockSpec(memory_space=pl.ANY)
+    return pl.pallas_call(
+        slots_kernel,
+        out_shape=[
+            sds(TILES, 8, BAND, LANE),
+            sds(41, STRIP, LANE),
+            sds(41, STRIP, LANE),
+            sds(9, BAND, LANE),
+        ],
+        in_specs=[smem()] * 3 + [anywhere] * 5 + [vmem()] * 3 + [anywhere] * 4,
+        out_specs=[anywhere] * 4,
+        scratch_shapes=[
+            pltpu.VMEM((TILES, 8, 256, LANE), f32),
+            pltpu.VMEM((TILES, 8, 256, LANE), f32),
+            pltpu.VMEM((4, 4, 2, LANE, LANE), f32),
+            pltpu.VMEM((5, 4, 2, LANE, LANE), f32),
+            pltpu.VMEM((256, LANE), f32),
+            pltpu.VMEM((256, 768), bf16),
+            pltpu.VMEM((256, 768), bf16),
+            pltpu.VMEM((768, 256), bf16),
+            pltpu.VMEM((768, 256), bf16),
+            pltpu.VMEM((4, LANE, LANE), f32),
+            pltpu.SemaphoreType.DMA((31,)),
+        ],
+        compiler_params=params(62),
+        name="slots",
+    )(*operands)
+
+
+def denoise_call(u, ev, od, ce, co, taps, conv_bias, output_weight, output_bias):
+    anywhere = pl.BlockSpec(memory_space=pl.ANY)
+    lines = sds(TILES, 4 * ROWS_KEPT, LANE)
+    conv_parts, map_parts, out_bias = pl.pallas_call(
+        weights_kernel,
+        out_shape=[
+            jax.ShapeDtypeStruct((3, 256, KTOT), bf16),
+            jax.ShapeDtypeStruct((3, 64, 256), bf16),
+            sds(3, 32, LANE),
+        ],
+        in_specs=[vmem()] * 4,
+        out_specs=[vmem()] * 3,
+        compiler_params=params(62),
+        cost_estimate=pl.CostEstimate(flops=1 << 20, bytes_accessed=3 << 20, transcendentals=0),
+        name="weights",
+    )(taps, conv_bias, output_weight, output_bias)
+    low, up = pl.pallas_call(
+        merge_kernel,
+        out_shape=[lines] * 2,
+        in_specs=[anywhere] * 3,
+        out_specs=[vmem()] * 2,
+        scratch_shapes=[
+            pltpu.VMEM((TILES, 8, BAND, LANE), f32),
+            pltpu.VMEM((41, STRIP, LANE), f32),
+            pltpu.VMEM((41, STRIP, LANE), f32),
+            pltpu.SemaphoreType.DMA((3,)),
+        ],
+        compiler_params=params(62),
+        cost_estimate=pl.CostEstimate(flops=1 << 20, bytes_accessed=9 << 20, transcendentals=0),
+        name="merge",
+    )(u, ev, od)
     return pl.pallas_call(
         denoise_kernel,
         out_shape=sds(8, 128, 512),
-        in_specs=[vmem()] * 8,
+        in_specs=[anywhere] * 2 + [vmem()] * 5,
         out_specs=vmem(),
         scratch_shapes=[
             pltpu.VMEM((TILES, 4 * ROWS_KEPT, LANE), f32),
             pltpu.VMEM((TILES, 4 * ROWS_KEPT, LANE), f32),
             pltpu.VMEM((2, 3, 4 * ROWS_KEPT, 640), bf16),
-            pltpu.VMEM((3, 256, KTOT), bf16),
-            pltpu.VMEM((3, 64, 256), bf16),
             pltpu.VMEM((2, 256, 640), f32),
+            pltpu.SemaphoreType.DMA((2,)),
         ],
-        compiler_params=params(56),
+        compiler_params=params(62),
         name="denoise",
-    )(*operands)
+    )(low, up, ce, co, conv_parts, map_parts, out_bias)
 
 
 def per_device(
@@ -561,46 +697,38 @@
         grid=(1,),
         in_specs=[edge(0), edge(3)],
         out_specs=[whole(8, HALF, LANE)] * 2,
-        compiler_params=params(32),
+        compiler_params=params(62),
         name="pack",
     )(obj, obj)
     ce = col_ev(ce)
     co = col_od(co)
+    anywhere = pl.BlockSpec(memory_space=pl.ANY)
+    strip = sds(TILES, 8, HALF, LANE)
+    ev, od = pl.pallas_call(
+        strips_kernel,
+        out_shape=[strip] * 2,
+        in_specs=[vmem()],
+        out_specs=[vmem()] * 2,
+        compiler_params=params(62),
+        cost_estimate=pl.CostEstimate(flops=0, bytes_accessed=4 << 20, transcendentals=0),
+        name="strips",
+    )(obj)
     comb, ev, od = pl.pallas_call(
         comb_kernel,
-        out_shape=[sds(8, 128, LANE), sds(TILES, 8, HALF, LANE), sds(TILES, 8, HALF, LANE)],
-        in_specs=[vmem()] * 3,
-        out_specs=[vmem()] * 3,
-        compiler_params=params(32),
+        out_shape=[sds(8, 128, LANE), strip, strip],
+        in_specs=[vmem()] * 2 + [anywhere] * 2,
+        out_specs=[anywhere] * 3,
+        scratch_shapes=[pltpu.VMEM((8, 128, LANE), f32), pltpu.SemaphoreType.DMA((3,))],
+        input_output_aliases={2: 1, 3: 2},
+        compiler_params=params(62),
         name="comb",
-    )(obj, ce, co)
+    )(ce, co, ev, od)
     od = row_od(od)
     ev = row_ev(ev)
     phase_re = jnp.cos(propagator_phase)
     phase_im = jnp.sin(propagator_phase)
     tables = [jnp.asarray(m) for m in dft_matrices()]
-    anywhere = pl.BlockSpec(memory_space=pl.ANY)
-    u, ev, od, own = pl.pallas_call(
-        slots_kernel,
-        out_shape=[
-            sds(TILES, 8, BAND, LANE),
-            sds(41, STRIP, LANE),
-            sds(41, STRIP, LANE),
-            sds(9, BAND, LANE),
-        ],
-        in_specs=[smem()] * 3 + [anywhere] * 4 + [vmem()] * 8,
-        out_specs=[vmem()] * 4,
-        scratch_shapes=[
-            pltpu.VMEM((TILES, 8, 256, LANE), f32),
-            pltpu.VMEM((TILES, 8, 256, LANE), f32),
-            pltpu.VMEM((4, 4, 2, LANE, LANE), f32),
-            pltpu.VMEM((5, 4, 2, LANE, LANE), f32),
-            pltpu.VMEM((256, LANE), f32),
-            pltpu.SemaphoreType.DMA((7,)),
-        ],
-        compiler_params=params(56),
-        name="slots",
-    )(
+    u, ev, od, own = slots_call(
         position_rows.reshape(-1),
         position_cols.reshape(-1),
         tile_counts.reshape(-1),
@@ -619,16 +747,21 @@
     ce, co = pl.pallas_call(
         sides_kernel,
         out_shape=[sds(9, STRIP, LANE)] * 2,
-        grid=(1,),
-        in_specs=[whole(9, BAND, LANE), whole(9, STRIP, LANE), whole(9, STRIP, LANE)],
-        out_specs=[whole(9, STRIP, LANE)] * 2,
-        compiler_params=params(32),
+        in_specs=[anywhere] * 3,
+        out_specs=[vmem()] * 2,
+        scratch_shapes=[
+            pltpu.VMEM((9, BAND, LANE), f32),
+            pltpu.VMEM((9, STRIP, LANE), f32),
+            pltpu.VMEM((9, STRIP, LANE), f32),
+            pltpu.SemaphoreType.DMA((3,)),
+        ],
+        compiler_params=params(62),
         name="sides",
     )(own, ev, od)
     ce = col_ev(ce)
     co = col_od(co)
-    packed, maps, out_bias = conv_matrices(conv_weight, conv_bias, output_weight, output_bias)
-    out = denoise_call(u, ev, od, ce, co, packed, maps, out_bias)
+    taps = conv_weight.reshape(3, 3, 3, 32, 4).transpose(0, 1, 3, 2, 4).reshape(3, 3, 32, 12)
+    out = denoise_call(u, ev, od, ce, co, taps, conv_bias, output_weight, output_bias)
     return out.reshape(4, 2, 128, 512)
 
 

time: 142 us -> 136 us (0.958)
  local copies, waits for them, and re-layouts: 17.2 us -> 3.13 us
  Pallas kernels: 55.5 us -> 64.5 us
  other arithmetic: 2.23 us -> 0 us
  waiting for transfers between devices: 46 us -> 47.6 us
    ppermute x2, waiting for transfers between devices: 27.8 us -> 37.1 us  [row_od(): return lax.ppermute(x, 'row', pairs(rows, 1))]
    pallas_call x4 -> x7, Pallas kernels: 55.3 us -> 62.3 us  [the longest x1 28 us: denoise_call(): pl.pallas_call(denoise_kernel, out_shape=sds(8, 128, 512), in_specs=[anyw...]
    add x6 -> x0, local copies, waits for them, and re-layouts: 6.33 us -> none  [conv_matrices(): sum((hot[:, dy][:, None, None, :, None] * jnp.transpose(w[layer, dy], (1,...]
    ppermute x2, waiting for transfers between devices: 15.4 us -> 9.66 us  [col_od(): return lax.ppermute(x, 'col', pairs(cols, 1))]
    unnamed x48 -> x16, local copies, waits for them, and re-layouts: 5.13 us -> 1.43 us
    ppermute x2, waiting for transfers between devices: 2.79 us -> 0.01 us  [col_ev(): return lax.ppermute(x, 'col', pairs(cols, 0))]
    concatenate x1 -> x0, local copies, waits for them, and re-layouts: 2.44 us -> none  [conv_matrices(): jnp.concatenate([main, main, main, bias, bias, jnp.zeros((layers, 256, 14...]
    pallas_call x1, Pallas kernels: 0.2 us -> 2.21 us  [per_device(): pl.pallas_call(pack_kernel, out_shape=[sds(8, HALF, LANE)] * 2, grid=(1,)...]
  transfers between devices with their start and end apart: 8 -> 8, of which waited for: 6 -> 5; matrix products, arithmetic and copies ran while one was open for 10% -> 1% of each run, Pallas kernels for 0% -> 8%
where the time goes in v3:
time: 136 us
  Pallas kernels  64.5 us (47%)
  waiting for transfers between devices  47.6 us (35%)
  starting transfers between devices  19.8 us (15%)
  local copies, waits for them, and re-layouts  3.13 us (2%)
    ppermute x2, waiting for transfers between devices, row_od(): return lax.ppermute(x, 'row', pairs(rows, 1))  37.1 us
    pallas_call x1, Pallas kernels, denoise_call(): pl.pallas_call(denoise_kernel, out_shape=sds(8, 128, 512), in_specs=[anyw...  28 us
    pallas_call x1, Pallas kernels, slots_call(): pl.pallas_call(slots_kernel, out_shape=[sds(TILES, 8, BAND, LANE), sds(41...  18.6 us
    ppermute x2, starting transfers between devices, col_od(): return lax.ppermute(x, 'col', pairs(cols, 1))  12.6 us
    ppermute x2, waiting for transfers between devices, col_od(): return lax.ppermute(x, 'col', pairs(cols, 1))  9.66 us
    ppermute x2, starting transfers between devices, row_od(): return lax.ppermute(x, 'row', pairs(rows, 1))  5.44 us
    pallas_call x1, Pallas kernels, denoise_call(): pl.pallas_call(merge_kernel, out_shape=[lines] * 2, in_specs=[anywhere] *...  4.8 us
    pallas_call x1, Pallas kernels, per_device(): pl.pallas_call(strips_kernel, out_shape=[strip] * 2, in_specs=[vmem()], o...  3.23 us
  transfers between devices with their start and end apart: 8, of which 5 were waited for; matrix products, arithmetic and copies ran while one was open for 1% of the time, Pallas kernels for 8%

profile of v3, /device:TPU:23, one launch (start us, length us, event | category | flops | bytes accessed | tf_op | source)
XLA Modules:
  0.0 136.0 jit_solution(14427282474466083495)
XLA Ops:
  0.0 2.2 %pack.1 = (f32[8,64,128]{2,1,0:T(8,128)}, f32[8,64,128]{2,1,0:T(8,128)}) custom-call(f32[8,128,512]{2,1,0:T(8,128)} %bitcast.12, f32[8,128,512]{2,1,0:T(8,128)} %bitcast.13), custom_call_target="tpu_custom_call" | custom-call | tf_op jit(solution)/shard_map/pack/pallas_call | solution.py:694
  2.3 6.2 %collective-permute-start.1 = (f32[8,64,128]{2,1,0:T(8,128)}, f32[8,64,128]{2,1,0:T(8,128)S(1)}, u32[]{:S(2)}, u32[]{:S(2)}) collective-permute-start(f32[8,64,128]{2,1,0:T(8,128)} %get-tuple-element.24), channel_id=1, source_target_pairs={{1,2},{2,1},{3,4},{4,3},{5,6},{6,5},{9,10},{10,9},{11,12},{12,11},... | collective-permute-start | bytes 786440 | tf_op jit(solution)/shard_map/ppermute | solution.py:685
  8.4 3.2 %strips.1 = (f32[5,8,64,128]{3,2,1,0:T(8,128)}, f32[5,8,64,128]{3,2,1,0:T(8,128)}) custom-call(f32[8,128,512]{2,1,0:T(8,128)} %bitcast.14), custom_call_target="tpu_custom_call" | custom-call | bytes 4194304 | tf_op jit(solution)/shard_map/strips/pallas_call | solution.py:707
  11.7 6.4 %collective-permute-done.1.co_ref = f32[8,64,128]{2,1,0:T(8,128)S(1)} collective-permute-done((f32[8,64,128]{2,1,0:T(8,128)}, f32[8,64,128]{2,1,0:T(8,128)S(1)}, u32[]{:S(2)}, u32[]{:S(2)}) %collective-permute-start.1) | collective-permute-done | bytes 262176 | tf_op jit(solution)/shard_map/ppermute | solution.py:685
  18.1 0.7 copy-done.5
  18.8 2.2 %comb.1 = (f32[8,128,128]{2,1,0:T(8,128)}, f32[5,8,64,128]{3,2,1,0:T(8,128)}, f32[5,8,64,128]{3,2,1,0:T(8,128)}) custom-call(f32[8,64,128]{2,1,0:T(8,128)} %copy-done.4, f32[8,64,128]{2,1,0:T(8,128)} %copy-done.5, f32[5,8,64,128]{3,2,1,0:T(8,128)} %get-tuple-element.25.ev_in, ...), custom_call_target="tpu_custom_call", output_to_operand_aliasing={{1}: (2, {}), {2}: (3, {})} | custom-call | tf_op jit(solution)/shard_map/comb/pallas_call | solution.py:716
  21.0 1.6 %collective-permute-start.2 = (f32[5,8,64,128]{3,2,1,0:T(8,128)}, f32[5,8,64,128]{3,2,1,0:T(8,128)S(1)}, u32[]{:S(2)}, u32[]{:S(2)}) collective-permute-start(f32[5,8,64,128]{3,2,1,0:T(8,128)} %get-tuple-element.28), channel_id=1, source_target_pairs={{0,8},{8,0},{16,24},{24,16},{32,40},{40,32},{48,56},{56,48},{64,72... | collective-permute-start | bytes 3932168 | tf_op jit(solution)/shard_map/ppermute | solution.py:676
  22.6 2.7 %collective-permute-start.3 = (f32[5,8,64,128]{3,2,1,0:T(8,128)}, f32[5,8,64,128]{3,2,1,0:T(8,128)}, u32[]{:S(2)}, u32[]{:S(2)}) collective-permute-start(f32[5,8,64,128]{3,2,1,0:T(8,128)} %get-tuple-element.29), channel_id=1, source_target_pairs={{8,16},{16,8},{24,32},{32,24},{40,48},{48,40},{56,64},{64,56},{72,... | collective-permute-start | bytes 3932168 | tf_op jit(solution)/shard_map/ppermute | solution.py:679
  26.0 0.9 fusion
  26.9 17.1 %collective-permute-done.3.od_ref = f32[5,8,64,128]{3,2,1,0:T(8,128)} collective-permute-done((f32[5,8,64,128]{3,2,1,0:T(8,128)}, f32[5,8,64,128]{3,2,1,0:T(8,128)}, u32[]{:S(2)}, u32[]{:S(2)}) %collective-permute-start.3) | collective-permute-done | bytes 1310752 | tf_op jit(solution)/shard_map/ppermute | solution.py:679
  44.0 18.6 %slots.1 = (f32[5,8,144,128]{3,2,1,0:T(8,128)}, f32[41,72,128]{2,1,0:T(8,128)}, f32[41,72,128]{2,1,0:T(8,128)}, f32[9,144,128]{2,1,0:T(8,128)}) custom-call(s32[4]{0:T(128)} %bitcast.18, s32[4]{0:T(128)} %bitcast.19, s32[1]{0:T(128)} %bitcast.11.count_ref, f32[8,128,512]{2,1,0:T(8,128)} %bitcast.15, f32[8,128,128]{2,1,0:T(8,128)} %get-tuple-element.27.comb_ref, ...), custom_call_target="tpu_custom_call" | custom-call | tf_op jit(solution)/shard_map/slots/pallas_call | solution.py:577
  62.5 0.1 collective-permute-start.4
  62.6 2.7 %collective-permute-start.5 = (f32[41,72,128]{2,1,0:T(8,128)}, f32[41,72,128]{2,1,0:T(8,128)}, u32[]{:S(2)}, u32[]{:S(2)}) collective-permute-start(f32[41,72,128]{2,1,0:T(8,128)} %get-tuple-element.32), channel_id=1, source_target_pairs={{8,16},{16,8},{24,32},{32,24},{40,48},{48,40},{56,64},{64,56},{72,... | collective-permute-start | bytes 4534280 | tf_op jit(solution)/shard_map/ppermute | solution.py:679
  65.3 0.8 collective-permute-done.4.ev_any
  66.2 20.1 %collective-permute-done.5.od_any = f32[41,72,128]{2,1,0:T(8,128)} collective-permute-done((f32[41,72,128]{2,1,0:T(8,128)}, f32[41,72,128]{2,1,0:T(8,128)}, u32[]{:S(2)}, u32[]{:S(2)}) %collective-permute-start.5) | collective-permute-done | bytes 1511456 | tf_op jit(solution)/shard_map/ppermute | solution.py:679
  86.2 2.3 %sides.1 = (f32[9,72,128]{2,1,0:T(8,128)}, f32[9,72,128]{2,1,0:T(8,128)}) custom-call(f32[9,144,128]{2,1,0:T(8,128)} %get-tuple-element.35.own_any, f32[41,72,128]{2,1,0:T(8,128)} %copy-done, f32[41,72,128]{2,1,0:T(8,128)} %collective-permute-done.5.od_any), custom_call_target="tpu_custom_call" | custom-call | tf_op jit(solution)/shard_map/sides/pallas_call | solution.py:747
  88.6 0.1 collective-permute-start.6
  88.7 6.4 %collective-permute-start.7 = (f32[9,72,128]{2,1,0:T(8,128)}, f32[9,72,128]{2,1,0:T(8,128)S(1)}, u32[]{:S(2)}, u32[]{:S(2)}) collective-permute-start(f32[9,72,128]{2,1,0:T(8,128)} %get-tuple-element.37), channel_id=1, source_target_pairs={{1,2},{2,1},{3,4},{4,3},{5,6},{6,5},{9,10},{10,9},{11,12},{12,11},... | collective-permute-start | bytes 995336 | tf_op jit(solution)/shard_map/ppermute | solution.py:685
  95.1 0.8 copy.19.taps_ref
  95.9 3.1 %weights.1 = (bf16[3,256,448]{2,1,0:T(8,128)(2,1)}, bf16[3,64,256]{2,1,0:T(8,128)(2,1)}, f32[3,32,128]{2,1,0:T(8,128)}) custom-call(f32[3,3,32,12]{3,2,1,0:T(8,128)} %copy.19.taps_ref, f32[3,32]{1,0:T(4,128)} %bias_ref.1, f32[3,4,32]{2,1,0:T(4,128)} %map_ref.1, f32[3,4]{1,0:T(4,128)} %map_bias_ref.1), custom_call_target="tpu_custom_call" | custom-call | flops 1048576 | bytes 3145728 | tf_op jit(solution)/shard_map/weights/pallas_call | solution.py:608
  99.0 4.8 %merge.1 = (f32[5,560,128]{2,1,0:T(8,128)}, f32[5,560,128]{2,1,0:T(8,128)}) custom-call(f32[5,8,144,128]{3,2,1,0:T(8,128)} %get-tuple-element.30.u_any, f32[41,72,128]{2,1,0:T(8,128)} %copy-done, f32[41,72,128]{2,1,0:T(8,128)} %collective-permute-done.5.od_any), custom_call_target="tpu_custom_call" | custom-call | flops 1048576 | bytes 9437184 | tf_op jit(solution)/shard_map/merge/pallas_call | solution.py:621
  103.8 3.3 %collective-permute-done.7.co_ref = f32[9,72,128]{2,1,0:T(8,128)S(1)} collective-permute-done((f32[9,72,128]{2,1,0:T(8,128)}, f32[9,72,128]{2,1,0:T(8,128)S(1)}, u32[]{:S(2)}, u32[]{:S(2)}) %collective-permute-start.7) | collective-permute-done | bytes 331808 | tf_op jit(solution)/shard_map/ppermute | solution.py:685
  107.1 0.7 copy-done.3
  107.8 28.0 %denoise.1 = f32[8,128,512]{2,1,0:T(8,128)} custom-call(f32[5,560,128]{2,1,0:T(8,128)} %get-tuple-element.33.low_any, f32[5,560,128]{2,1,0:T(8,128)} %get-tuple-element.34.up_any, f32[9,72,128]{2,1,0:T(8,128)} %copy-done.2, f32[9,72,128]{2,1,0:T(8,128)} %copy-done.3, bf16[3,256,448]{2,1,0:T(8,128)(2,1)} %get-tuple-element.38.conv_sc, ...), custom_call_target="tpu_custom_call" | custom-call | tf_op jit(solution)/shard_map/denoise/pallas_call | solution.py:636
  (19 shorter events, 0.1 us)
Async XLA Ops:
  2.2 9.5 %collective-permute-start = (f32[8,64,128]{2,1,0:T(8,128)}, f32[8,64,128]{2,1,0:T(8,128)S(1)}, u32[]{:S(2)}, u32[]{:S(2)}) collective-permute-start(f32[8,64,128]{2,1,0:T(8,128)} %get-tuple-element.23), channel_id=1, source_target_pairs={{0,1},{1,0},{2,3},{3,2},{4,5},{5,4},{6,7},{7,6},{8,9},{9,8},{10,11... | collective-permute-start | bytes 786440 | tf_op jit(solution)/shard_map/ppermute | solution.py:682
  2.3 15.8 %collective-permute-start.1 = (f32[8,64,128]{2,1,0:T(8,128)}, f32[8,64,128]{2,1,0:T(8,128)S(1)}, u32[]{:S(2)}, u32[]{:S(2)}) collective-permute-start(f32[8,64,128]{2,1,0:T(8,128)} %get-tuple-element.24), channel_id=1, source_target_pairs={{1,2},{2,1},{3,4},{4,3},{5,6},{6,5},{9,10},{10,9},{11,12},{12,11},... | collective-permute-start | bytes 786440 | tf_op jit(solution)/shard_map/ppermute | solution.py:685
  11.7 6.4 %copy-start.4 = (f32[8,64,128]{2,1,0:T(8,128)}, f32[8,64,128]{2,1,0:T(8,128)S(1)}, u32[]{:S(2)}) copy-start(f32[8,64,128]{2,1,0:T(8,128)S(1)} %collective-permute-done.ce_ref) | copy-start | bytes 786436
  18.1 0.7 copy-start.5
  18.8 7.2 %copy-start.6 = (f32[128,128]{1,0:T(8,128)S(1)}, f32[128,128]{1,0:T(8,128)}, u32[]{:S(2)}) copy-start(f32[128,128]{1,0:T(8,128)} %param.17) | copy-start | bytes 196612
  21.0 5.9 %collective-permute-start.2 = (f32[5,8,64,128]{3,2,1,0:T(8,128)}, f32[5,8,64,128]{3,2,1,0:T(8,128)S(1)}, u32[]{:S(2)}, u32[]{:S(2)}) collective-permute-start(f32[5,8,64,128]{3,2,1,0:T(8,128)} %get-tuple-element.28), channel_id=1, source_target_pairs={{0,8},{8,0},{16,24},{24,16},{32,40},{40,32},{48,56},{56,48},{64,72... | collective-permute-start | bytes 3932168 | tf_op jit(solution)/shard_map/ppermute | solution.py:676
  22.6 21.3 %collective-permute-start.3 = (f32[5,8,64,128]{3,2,1,0:T(8,128)}, f32[5,8,64,128]{3,2,1,0:T(8,128)}, u32[]{:S(2)}, u32[]{:S(2)}) collective-permute-start(f32[5,8,64,128]{3,2,1,0:T(8,128)} %get-tuple-element.29), channel_id=1, source_target_pairs={{8,16},{16,8},{24,32},{32,24},{40,48},{48,40},{56,64},{64,56},{72,... | collective-permute-start | bytes 3932168 | tf_op jit(solution)/shard_map/ppermute | solution.py:679
  26.9 17.1 %copy-start.1 = (f32[5,8,64,128]{3,2,1,0:T(8,128)}, f32[5,8,64,128]{3,2,1,0:T(8,128)S(1)}, u32[]{:S(2)}) copy-start(f32[5,8,64,128]{3,2,1,0:T(8,128)S(1)} %collective-permute-done.2.ev_ref) | copy-start | bytes 3932164
  62.5 3.6 %collective-permute-start.4 = (f32[41,72,128]{2,1,0:T(8,128)}, f32[41,72,128]{2,1,0:T(8,128)S(1)}, u32[]{:S(2)}, u32[]{:S(2)}) collective-permute-start(f32[41,72,128]{2,1,0:T(8,128)} %get-tuple-element.31), channel_id=1, source_target_pairs={{0,8},{8,0},{16,24},{24,16},{32,40},{40,32},{48,56},{56,48},{64,72... | collective-permute-start | bytes 4534280 | tf_op jit(solution)/shard_map/ppermute | solution.py:676
  62.6 23.6 %collective-permute-start.5 = (f32[41,72,128]{2,1,0:T(8,128)}, f32[41,72,128]{2,1,0:T(8,128)}, u32[]{:S(2)}, u32[]{:S(2)}) collective-permute-start(f32[41,72,128]{2,1,0:T(8,128)} %get-tuple-element.32), channel_id=1, source_target_pairs={{8,16},{16,8},{24,32},{32,24},{40,48},{48,40},{56,64},{64,56},{72,... | collective-permute-start | bytes 4534280 | tf_op jit(solution)/shard_map/ppermute | solution.py:679
  66.2 20.1 %copy-start = (f32[41,72,128]{2,1,0:T(8,128)}, f32[41,72,128]{2,1,0:T(8,128)S(1)}, u32[]{:S(2)}) copy-start(f32[41,72,128]{2,1,0:T(8,128)S(1)} %collective-permute-done.4.ev_any) | copy-start | bytes 4534276
  86.2 8.8 %copy-start.7 = (f32[3,9,32,4]{2,3,1,0:T(4,128)S(1)}, f32[3,9,32,4]{2,3,1,0:T(4,128)}, u32[]{:S(2)}) copy-start(f32[3,9,32,4]{2,3,1,0:T(4,128)} %param.22) | copy-start | bytes 41476
  88.6 15.2 %collective-permute-start.6 = (f32[9,72,128]{2,1,0:T(8,128)}, f32[9,72,128]{2,1,0:T(8,128)S(1)}, u32[]{:S(2)}, u32[]{:S(2)}) collective-permute-start(f32[9,72,128]{2,1,0:T(8,128)} %get-tuple-element.36), channel_id=1, source_target_pairs={{0,1},{1,0},{2,3},{3,2},{4,5},{5,4},{6,7},{7,6},{8,9},{9,8},{10,11... | collective-permute-start | bytes 995336 | tf_op jit(solution)/shard_map/ppermute | solution.py:682
  88.7 18.4 %collective-permute-start.7 = (f32[9,72,128]{2,1,0:T(8,128)}, f32[9,72,128]{2,1,0:T(8,128)S(1)}, u32[]{:S(2)}, u32[]{:S(2)}) collective-permute-start(f32[9,72,128]{2,1,0:T(8,128)} %get-tuple-element.37), channel_id=1, source_target_pairs={{1,2},{2,1},{3,4},{4,3},{5,6},{6,5},{9,10},{10,9},{11,12},{12,11},... | collective-permute-start | bytes 995336 | tf_op jit(solution)/shard_map/ppermute | solution.py:685
  103.8 3.3 %copy-start.2 = (f32[9,72,128]{2,1,0:T(8,128)}, f32[9,72,128]{2,1,0:T(8,128)S(1)}, u32[]{:S(2)}) copy-start(f32[9,72,128]{2,1,0:T(8,128)S(1)} %collective-permute-done.6.ce_ref) | copy-start | bytes 995332
  107.1 0.7 copy-start.3

commit v4 on v3

--- a/solution.py
+++ b/solution.py
@@ -15,8 +15,8 @@
 BAND = 144
 TILES = 5
 ROWS_KEPT = 140
-KDX = 48
-KTOT = 448
+ROWS_SET = 138
+KTOT = 240
 
 f32 = jnp.float32
 bf16 = jnp.bfloat16
@@ -351,23 +351,35 @@
     def exact(a, b):
         return jnp.dot(a, b, precision=lax.Precision.HIGHEST, preferred_element_type=f32)
 
-    place = hot(12, KTOT, lambda a, b: (b < 432) & (a == (b % 144) // 48 * 4 + b % 4))
-    row = lax.broadcasted_iota(jnp.int32, (256, KTOT), 0)
-    col = lax.broadcasted_iota(jnp.int32, (256, KTOT), 1)
-    shift = (col % 48) // 4 - row // 32
-    is_bias = (col == 432) | (col == 433)
-    use_low = ((col >= 288) & (col < 432)) | (col == 433)
-    hidden_hot = hot(256, 32, lambda a, b: a % 32 == b)
+    def column(b):
+        half = ((b >= 96) & (b < 144)) | ((b >= 192) & (b < 224))
+        line = jnp.where(half, b % 8, b % 16)
+        dx = jnp.where(half, (b - jnp.where(b < 144, 96, 192)) // 8 % 3, b // 16 % 3)
+        k = line // 4 + jnp.where(half, 4, 0)
+        return dx * 4 + line % 4, k, b < 216
+
+    def placed(a, b):
+        source, _, valid = column(b)
+        return valid & (a == source)
+
+    place = hot(12, KTOT, placed)
+    row = lax.broadcasted_iota(jnp.int32, (LANE, KTOT), 0)
+    col = lax.broadcasted_iota(jnp.int32, (LANE, KTOT), 1)
+    _, window_row, is_tap = column(col)
+    shift = window_row - row // 32
+    is_bias = (col == 224) | (col == 225)
+    use_low = ((col >= 144) & (col < 216)) | (col == 225)
+    hidden_hot = hot(LANE, 32, lambda a, b: a % 32 == b)
     channel_hot = hot(32, 4, lambda a, b: a % 4 == b)
     spread = hot(32, 256, lambda a, b: a == b % 32)
     same_row = hot(32, 256, lambda a, b: a // 4 == b // 32)
-    for layer, start in zip(range(3), (2, 2, 0)):
+    for layer in range(3):
         bias = jnp.sum(hidden_hot * bias_ref[layer : layer + 1, :], axis=1, keepdims=True)
         total = jnp.where(is_bias, bias, 0.0)
         for dy in range(3):
             part = exact(taps_ref[layer, dy], place)
-            whole = jnp.concatenate([part] * 8, axis=0)
-            total = total + jnp.where((shift == dy + start) & (col < 432), whole, 0.0)
+            whole = jnp.concatenate([part] * 4, axis=0)
+            total = total + jnp.where((shift == dy) & is_tap, whole, 0.0)
         high, low = split(total * 0.5)
         conv_out[layer] = jnp.where(use_low, low.astype(f32), high.astype(f32)).astype(bf16)
         wide = exact(exact(channel_hot, map_ref[layer]), spread) * same_row
@@ -397,8 +409,8 @@
 
     for t in range(TILES):
         for c in range(4):
-            low_st[t, pl.ds(c, ROWS_KEPT, stride=4), :] = combine(t, c)[3:143]
-            up_st[t, pl.ds(c, ROWS_KEPT, stride=4), :] = combine(t, 4 + c)[4:144]
+            low_st[t, pl.ds(c, ROWS_SET, stride=4), :] = combine(t, c)[5:143]
+            up_st[t, pl.ds(c, ROWS_SET, stride=4), :] = combine(t, 4 + c)[6:144]
 
 
 def denoise_kernel(
@@ -428,7 +440,7 @@
 
     def add_sides(c):
         store = low_st if c < 4 else up_st
-        skip = 3 if c < 4 else 4
+        skip = 5 if c < 4 else 6
         ce = ce_ref[c]
         co = co_ref[c]
         from_left = jnp.where(col_odd == 1, ce, co)
@@ -454,8 +466,8 @@
             ),
         }
         for t, both in pieces.items():
-            at = pl.ds(c % 4, ROWS_KEPT, stride=4)
-            whole = jnp.concatenate(both, axis=0)[skip : skip + ROWS_KEPT]
+            at = pl.ds(c % 4, ROWS_SET, stride=4)
+            whole = jnp.concatenate(both, axis=0)[skip : skip + ROWS_SET]
             store[t, at, :] = store[t, at, :] + whole
 
     low_copy.wait()
@@ -472,7 +484,7 @@
 
     def prepare(store, first_row):
         row_low = jnp.where(row_id == 0, -first_row * 4, 0)
-        row_high = jnp.where(row_id == last_row, (128 - first_row) * 4, 4 * ROWS_KEPT)
+        row_high = (jnp.where(row_id == last_row, 128, 131) - first_row) * 4
 
         def body(i, carry):
             at = pl.multiple_of(i * 16, 16)
@@ -482,27 +494,39 @@
             inside = (index >= row_low) & (index < row_high)
             inside = inside & ((column < right_off) | (column >= left_off))
             x = jnp.where(inside, x, 0.0)
+            heads = []
+            rests = []
             for dx in range(3):
                 y = x if dx == 1 else pltpu.roll(x, 1 if dx == 0 else 639, 1)
-                high, low = split(y)
+                high = y.astype(bf16)
+                rest = y - high.astype(f32)
                 cond_st[0, dx, pl.ds(at, 16), :] = high
-                cond_st[1, dx, pl.ds(at, 16), :] = low
+                cond_st[1, dx, pl.ds(at, 16), :] = rest.astype(bf16)
+                heads.append(y[:8])
+                rests.append(rest[:8])
+            for i in range(3):
+                both = jnp.concatenate((heads + rests)[2 * i : 2 * i + 2], axis=0)
+                cond_st[2, i, pl.ds(at, 16), :] = both.astype(bf16)
             return carry
 
-        lax.fori_loop(0, 4 * ROWS_KEPT // 16, body, 0, unroll=5)
+        lax.fori_loop(0, 4 * ROWS_KEPT // 16, body, 0, unroll=7)
 
     ones = jnp.ones((16, 640), bf16)
 
-    def layer_pass(layer, groups, read_at, store, write_at, width):
+    def layer_pass(layer, store, write_at, width):
+        groups = 17
         bias = bias_ref[layer]
 
         def first_map(g, slot):
-            src = pl.multiple_of(read_at + g * 32, 16)
-            pieces = [cond_st[part, dx, pl.ds(src, KDX), :width] for part in (0, 1) for dx in range(3)]
-            pieces = pieces + pieces[:3] + [ones[:, :width]]
-            half_sc[slot, :, :width] = jnp.dot(
-                conv_sc[layer], jnp.concatenate(pieces, axis=0), preferred_element_type=f32
-            )
+            for h in range(2):
+                here = pl.ds(pl.multiple_of(g * 32 + 16 * h, 16), 16)
+                below = pl.ds(pl.multiple_of(g * 32 + 16 * h + 16, 16), 16)
+                main = [cond_st[part, dx, here, :width] for part in (0, 1) for dx in range(3)]
+                half = [cond_st[2, i, below, :width] for i in range(3)]
+                pieces = main + half + main[:3] + half[:2] + [ones[:, :width]]
+                half_sc[slot, h * LANE : (h + 1) * LANE, :width] = jnp.dot(
+                    conv_sc[layer], jnp.concatenate(pieces, axis=0), preferred_element_type=f32
+                )
 
         def second_map(g, slot):
             dst = pl.multiple_of(write_at + g * 32, 8)
@@ -535,16 +559,16 @@
         else:
             second_map(done, 0)
 
-    prepare(low_st, -5)
-    layer_pass(0, 17, 0, up_st, 8, 640)
-    prepare(up_st, -4)
-    layer_pass(1, 17, 0, low_st, 16, 640)
-    prepare(low_st, -5)
-    layer_pass(2, 16, 16, up_st, 16, 512)
+    prepare(low_st, -3)
+    layer_pass(0, up_st, 0, 640)
+    prepare(up_st, -2)
+    layer_pass(1, low_st, 8, 640)
+    prepare(low_st, -3)
+    layer_pass(2, up_st, 0, 512)
     for t in range(4):
         for c in range(4):
-            out_ref[c, :, t * LANE : (t + 1) * LANE] = low_st[t, pl.ds(20 + c, 128, stride=4), :]
-            out_ref[4 + c, :, t * LANE : (t + 1) * LANE] = up_st[t, pl.ds(16 + c, 128, stride=4), :]
+            out_ref[c, :, t * LANE : (t + 1) * LANE] = low_st[t, pl.ds(12 + c, 128, stride=4), :]
+            out_ref[4 + c, :, t * LANE : (t + 1) * LANE] = up_st[t, pl.ds(8 + c, 128, stride=4), :]
 
 
 def dft_matrices():
@@ -608,7 +632,7 @@
     conv_parts, map_parts, out_bias = pl.pallas_call(
         weights_kernel,
         out_shape=[
-            jax.ShapeDtypeStruct((3, 256, KTOT), bf16),
+            jax.ShapeDtypeStruct((3, LANE, KTOT), bf16),
             jax.ShapeDtypeStruct((3, 64, 256), bf16),
             sds(3, 32, LANE),
         ],
@@ -641,7 +665,7 @@
         scratch_shapes=[
             pltpu.VMEM((TILES, 4 * ROWS_KEPT, LANE), f32),
             pltpu.VMEM((TILES, 4 * ROWS_KEPT, LANE), f32),
-            pltpu.VMEM((2, 3, 4 * ROWS_KEPT, 640), bf16),
+            pltpu.VMEM((3, 3, 4 * ROWS_KEPT, 640), bf16),
             pltpu.VMEM((2, 256, 640), f32),
             pltpu.SemaphoreType.DMA((2,)),
         ],

time: 136 us -> 132 us (0.971)
  Pallas kernels: 64.5 us -> 60 us
    pallas_call x1, Pallas kernels: 28 us -> 24 us  [denoise_call(): pl.pallas_call(denoise_kernel, out_shape=sds(8, 128, 512), in_specs=[anyw...]
where the time goes in v4:
time: 132 us
  Pallas kernels  60 us (45%)
  waiting for transfers between devices  48.1 us (36%)
  starting transfers between devices  19.8 us (15%)
  local copies, waits for them, and re-layouts  3.14 us (2%)
    ppermute x2, waiting for transfers between devices, row_od(): return lax.ppermute(x, 'row', pairs(rows, 1))  37.1 us
    pallas_call x1, Pallas kernels, denoise_call(): pl.pallas_call(denoise_kernel, out_shape=sds(8, 128, 512), in_specs=[anyw...  24 us
    pallas_call x1, Pallas kernels, slots_call(): pl.pallas_call(slots_kernel, out_shape=[sds(TILES, 8, BAND, LANE), sds(41...  18.6 us
    ppermute x2, starting transfers between devices, col_od(): return lax.ppermute(x, 'col', pairs(cols, 1))  12.6 us
    ppermute x2, waiting for transfers between devices, col_od(): return lax.ppermute(x, 'col', pairs(cols, 1))  10.2 us
    ppermute x2, starting transfers between devices, row_od(): return lax.ppermute(x, 'row', pairs(rows, 1))  5.44 us
    pallas_call x1, Pallas kernels, denoise_call(): pl.pallas_call(merge_kernel, out_shape=[lines] * 2, in_specs=[anywhere] *...  4.84 us
    pallas_call x1, Pallas kernels, per_device(): pl.pallas_call(strips_kernel, out_shape=[strip] * 2, in_specs=[vmem()], o...  3.23 us
  transfers between devices with their start and end apart: 8, of which 5 were waited for; matrix products, arithmetic and copies ran while one was open for 1% of the time, Pallas kernels for 8%

profile of v4, /device:TPU:23, one launch (start us, length us, event | category | flops | bytes accessed | tf_op | source)
XLA Modules:
  0.0 132.0 jit_solution(1947291801779780059)
XLA Ops:
  0.0 2.2 %pack.1 = (f32[8,64,128]{2,1,0:T(8,128)}, f32[8,64,128]{2,1,0:T(8,128)}) custom-call(f32[8,128,512]{2,1,0:T(8,128)} %bitcast.12, f32[8,128,512]{2,1,0:T(8,128)} %bitcast.13), custom_call_target="tpu_custom_call" | custom-call | tf_op jit(solution)/shard_map/pack/pallas_call | solution.py:718
  2.3 6.2 %collective-permute-start.1 = (f32[8,64,128]{2,1,0:T(8,128)}, f32[8,64,128]{2,1,0:T(8,128)S(1)}, u32[]{:S(2)}, u32[]{:S(2)}) collective-permute-start(f32[8,64,128]{2,1,0:T(8,128)} %get-tuple-element.24), channel_id=1, source_target_pairs={{1,2},{2,1},{3,4},{4,3},{5,6},{6,5},{9,10},{10,9},{11,12},{12,11},... | collective-permute-start | bytes 786440 | tf_op jit(solution)/shard_map/ppermute | solution.py:709
  8.4 3.2 %strips.1 = (f32[5,8,64,128]{3,2,1,0:T(8,128)}, f32[5,8,64,128]{3,2,1,0:T(8,128)}) custom-call(f32[8,128,512]{2,1,0:T(8,128)} %bitcast.14), custom_call_target="tpu_custom_call" | custom-call | bytes 4194304 | tf_op jit(solution)/shard_map/strips/pallas_call | solution.py:731
  11.7 6.4 %collective-permute-done.1.co_ref = f32[8,64,128]{2,1,0:T(8,128)S(1)} collective-permute-done((f32[8,64,128]{2,1,0:T(8,128)}, f32[8,64,128]{2,1,0:T(8,128)S(1)}, u32[]{:S(2)}, u32[]{:S(2)}) %collective-permute-start.1) | collective-permute-done | bytes 262176 | tf_op jit(solution)/shard_map/ppermute | solution.py:709
  18.1 0.7 copy-done.5
  18.8 2.2 %comb.1 = (f32[8,128,128]{2,1,0:T(8,128)}, f32[5,8,64,128]{3,2,1,0:T(8,128)}, f32[5,8,64,128]{3,2,1,0:T(8,128)}) custom-call(f32[8,64,128]{2,1,0:T(8,128)} %copy-done.4, f32[8,64,128]{2,1,0:T(8,128)} %copy-done.5, f32[5,8,64,128]{3,2,1,0:T(8,128)} %get-tuple-element.25.ev_in, ...), custom_call_target="tpu_custom_call", output_to_operand_aliasing={{1}: (2, {}), {2}: (3, {})} | custom-call | tf_op jit(solution)/shard_map/comb/pallas_call | solution.py:740
  21.0 1.6 %collective-permute-start.2 = (f32[5,8,64,128]{3,2,1,0:T(8,128)}, f32[5,8,64,128]{3,2,1,0:T(8,128)S(1)}, u32[]{:S(2)}, u32[]{:S(2)}) collective-permute-start(f32[5,8,64,128]{3,2,1,0:T(8,128)} %get-tuple-element.28), channel_id=1, source_target_pairs={{0,8},{8,0},{16,24},{24,16},{32,40},{40,32},{48,56},{56,48},{64,72... | collective-permute-start | bytes 3932168 | tf_op jit(solution)/shard_map/ppermute | solution.py:700
  22.6 2.7 %collective-permute-start.3 = (f32[5,8,64,128]{3,2,1,0:T(8,128)}, f32[5,8,64,128]{3,2,1,0:T(8,128)}, u32[]{:S(2)}, u32[]{:S(2)}) collective-permute-start(f32[5,8,64,128]{3,2,1,0:T(8,128)} %get-tuple-element.29), channel_id=1, source_target_pairs={{8,16},{16,8},{24,32},{32,24},{40,48},{48,40},{56,64},{64,56},{72,... | collective-permute-start | bytes 3932168 | tf_op jit(solution)/shard_map/ppermute | solution.py:703
  26.0 0.9 fusion
  26.9 17.1 %collective-permute-done.3.od_ref = f32[5,8,64,128]{3,2,1,0:T(8,128)} collective-permute-done((f32[5,8,64,128]{3,2,1,0:T(8,128)}, f32[5,8,64,128]{3,2,1,0:T(8,128)}, u32[]{:S(2)}, u32[]{:S(2)}) %collective-permute-start.3) | collective-permute-done | bytes 1310752 | tf_op jit(solution)/shard_map/ppermute | solution.py:703
  44.0 18.6 %slots.1 = (f32[5,8,144,128]{3,2,1,0:T(8,128)}, f32[41,72,128]{2,1,0:T(8,128)}, f32[41,72,128]{2,1,0:T(8,128)}, f32[9,144,128]{2,1,0:T(8,128)}) custom-call(s32[4]{0:T(128)} %bitcast.18, s32[4]{0:T(128)} %bitcast.19, s32[1]{0:T(128)} %bitcast.11.count_ref, f32[8,128,512]{2,1,0:T(8,128)} %bitcast.15, f32[8,128,128]{2,1,0:T(8,128)} %get-tuple-element.27.comb_ref, ...), custom_call_target="tpu_custom_call" | custom-call | tf_op jit(solution)/shard_map/slots/pallas_call | solution.py:601
  62.5 0.1 collective-permute-start.4
  62.6 2.7 %collective-permute-start.5 = (f32[41,72,128]{2,1,0:T(8,128)}, f32[41,72,128]{2,1,0:T(8,128)}, u32[]{:S(2)}, u32[]{:S(2)}) collective-permute-start(f32[41,72,128]{2,1,0:T(8,128)} %get-tuple-element.32), channel_id=1, source_target_pairs={{8,16},{16,8},{24,32},{32,24},{40,48},{48,40},{56,64},{64,56},{72,... | collective-permute-start | bytes 4534280 | tf_op jit(solution)/shard_map/ppermute | solution.py:703
  65.4 0.8 collective-permute-done.4.ev_any
  66.2 20.1 %collective-permute-done.5.od_any = f32[41,72,128]{2,1,0:T(8,128)} collective-permute-done((f32[41,72,128]{2,1,0:T(8,128)}, f32[41,72,128]{2,1,0:T(8,128)}, u32[]{:S(2)}, u32[]{:S(2)}) %collective-permute-start.5) | collective-permute-done | bytes 1511456 | tf_op jit(solution)/shard_map/ppermute | solution.py:703
  86.2 2.4 %sides.1 = (f32[9,72,128]{2,1,0:T(8,128)}, f32[9,72,128]{2,1,0:T(8,128)}) custom-call(f32[9,144,128]{2,1,0:T(8,128)} %get-tuple-element.35.own_any, f32[41,72,128]{2,1,0:T(8,128)} %copy-done, f32[41,72,128]{2,1,0:T(8,128)} %collective-permute-done.5.od_any), custom_call_target="tpu_custom_call" | custom-call | tf_op jit(solution)/shard_map/sides/pallas_call | solution.py:771
  88.6 0.1 collective-permute-start.6
  88.7 6.4 %collective-permute-start.7 = (f32[9,72,128]{2,1,0:T(8,128)}, f32[9,72,128]{2,1,0:T(8,128)S(1)}, u32[]{:S(2)}, u32[]{:S(2)}) collective-permute-start(f32[9,72,128]{2,1,0:T(8,128)} %get-tuple-element.37), channel_id=1, source_target_pairs={{1,2},{2,1},{3,4},{4,3},{5,6},{6,5},{9,10},{10,9},{11,12},{12,11},... | collective-permute-start | bytes 995336 | tf_op jit(solution)/shard_map/ppermute | solution.py:709
  95.1 0.8 copy.19.taps_ref
  95.9 2.6 %weights.1 = (bf16[3,128,240]{2,1,0:T(8,128)(2,1)}, bf16[3,64,256]{2,1,0:T(8,128)(2,1)}, f32[3,32,128]{2,1,0:T(8,128)}) custom-call(f32[3,3,32,12]{3,2,1,0:T(8,128)} %copy.19.taps_ref, f32[3,32]{1,0:T(4,128)} %bias_ref.1, f32[3,4,32]{2,1,0:T(4,128)} %map_ref.1, f32[3,4]{1,0:T(4,128)} %map_bias_ref.1), custom_call_target="tpu_custom_call" | custom-call | flops 1048576 | bytes 3145728 | tf_op jit(solution)/shard_map/weights/pallas_call | solution.py:632
  98.5 4.8 %merge.1 = (f32[5,560,128]{2,1,0:T(8,128)}, f32[5,560,128]{2,1,0:T(8,128)}) custom-call(f32[5,8,144,128]{3,2,1,0:T(8,128)} %get-tuple-element.30.u_any, f32[41,72,128]{2,1,0:T(8,128)} %copy-done, f32[41,72,128]{2,1,0:T(8,128)} %collective-permute-done.5.od_any), custom_call_target="tpu_custom_call" | custom-call | flops 1048576 | bytes 9437184 | tf_op jit(solution)/shard_map/merge/pallas_call | solution.py:645
  103.4 3.8 %collective-permute-done.7.co_ref = f32[9,72,128]{2,1,0:T(8,128)S(1)} collective-permute-done((f32[9,72,128]{2,1,0:T(8,128)}, f32[9,72,128]{2,1,0:T(8,128)S(1)}, u32[]{:S(2)}, u32[]{:S(2)}) %collective-permute-start.7) | collective-permute-done | bytes 331808 | tf_op jit(solution)/shard_map/ppermute | solution.py:709
  107.1 0.7 copy-done.3
  107.8 24.0 %denoise.1 = f32[8,128,512]{2,1,0:T(8,128)} custom-call(f32[5,560,128]{2,1,0:T(8,128)} %get-tuple-element.33.low_any, f32[5,560,128]{2,1,0:T(8,128)} %get-tuple-element.34.up_any, f32[9,72,128]{2,1,0:T(8,128)} %copy-done.2, f32[9,72,128]{2,1,0:T(8,128)} %copy-done.3, bf16[3,128,240]{2,1,0:T(8,128)(2,1)} %get-tuple-element.38.conv_sc, ...), custom_call_target="tpu_custom_call" | custom-call | tf_op jit(solution)/shard_map/denoise/pallas_call | solution.py:660
  (19 shorter events, 0.1 us)
Async XLA Ops:
  2.2 9.5 %collective-permute-start = (f32[8,64,128]{2,1,0:T(8,128)}, f32[8,64,128]{2,1,0:T(8,128)S(1)}, u32[]{:S(2)}, u32[]{:S(2)}) collective-permute-start(f32[8,64,128]{2,1,0:T(8,128)} %get-tuple-element.23), channel_id=1, source_target_pairs={{0,1},{1,0},{2,3},{3,2},{4,5},{5,4},{6,7},{7,6},{8,9},{9,8},{10,11... | collective-permute-start | bytes 786440 | tf_op jit(solution)/shard_map/ppermute | solution.py:706
  2.3 15.8 %collective-permute-start.1 = (f32[8,64,128]{2,1,0:T(8,128)}, f32[8,64,128]{2,1,0:T(8,128)S(1)}, u32[]{:S(2)}, u32[]{:S(2)}) collective-permute-start(f32[8,64,128]{2,1,0:T(8,128)} %get-tuple-element.24), channel_id=1, source_target_pairs={{1,2},{2,1},{3,4},{4,3},{5,6},{6,5},{9,10},{10,9},{11,12},{12,11},... | collective-permute-start | bytes 786440 | tf_op jit(solution)/shard_map/ppermute | solution.py:709
  11.7 6.4 %copy-start.4 = (f32[8,64,128]{2,1,0:T(8,128)}, f32[8,64,128]{2,1,0:T(8,128)S(1)}, u32[]{:S(2)}) copy-start(f32[8,64,128]{2,1,0:T(8,128)S(1)} %collective-permute-done.ce_ref) | copy-start | bytes 786436
  18.1 0.7 copy-start.5
  18.8 7.2 %copy-start.6 = (f32[128,128]{1,0:T(8,128)S(1)}, f32[128,128]{1,0:T(8,128)}, u32[]{:S(2)}) copy-start(f32[128,128]{1,0:T(8,128)} %param.17) | copy-start | bytes 196612
  21.0 5.9 %collective-permute-start.2 = (f32[5,8,64,128]{3,2,1,0:T(8,128)}, f32[5,8,64,128]{3,2,1,0:T(8,128)S(1)}, u32[]{:S(2)}, u32[]{:S(2)}) collective-permute-start(f32[5,8,64,128]{3,2,1,0:T(8,128)} %get-tuple-element.28), channel_id=1, source_target_pairs={{0,8},{8,0},{16,24},{24,16},{32,40},{40,32},{48,56},{56,48},{64,72... | collective-permute-start | bytes 3932168 | tf_op jit(solution)/shard_map/ppermute | solution.py:700
  22.6 21.3 %collective-permute-start.3 = (f32[5,8,64,128]{3,2,1,0:T(8,128)}, f32[5,8,64,128]{3,2,1,0:T(8,128)}, u32[]{:S(2)}, u32[]{:S(2)}) collective-permute-start(f32[5,8,64,128]{3,2,1,0:T(8,128)} %get-tuple-element.29), channel_id=1, source_target_pairs={{8,16},{16,8},{24,32},{32,24},{40,48},{48,40},{56,64},{64,56},{72,... | collective-permute-start | bytes 3932168 | tf_op jit(solution)/shard_map/ppermute | solution.py:703
  26.9 17.1 %copy-start.1 = (f32[5,8,64,128]{3,2,1,0:T(8,128)}, f32[5,8,64,128]{3,2,1,0:T(8,128)S(1)}, u32[]{:S(2)}) copy-start(f32[5,8,64,128]{3,2,1,0:T(8,128)S(1)} %collective-permute-done.2.ev_ref) | copy-start | bytes 3932164
  62.5 3.6 %collective-permute-start.4 = (f32[41,72,128]{2,1,0:T(8,128)}, f32[41,72,128]{2,1,0:T(8,128)S(1)}, u32[]{:S(2)}, u32[]{:S(2)}) collective-permute-start(f32[41,72,128]{2,1,0:T(8,128)} %get-tuple-element.31), channel_id=1, source_target_pairs={{0,8},{8,0},{16,24},{24,16},{32,40},{40,32},{48,56},{56,48},{64,72... | collective-permute-start | bytes 4534280 | tf_op jit(solution)/shard_map/ppermute | solution.py:700
  62.6 23.6 %collective-permute-start.5 = (f32[41,72,128]{2,1,0:T(8,128)}, f32[41,72,128]{2,1,0:T(8,128)}, u32[]{:S(2)}, u32[]{:S(2)}) collective-permute-start(f32[41,72,128]{2,1,0:T(8,128)} %get-tuple-element.32), channel_id=1, source_target_pairs={{8,16},{16,8},{24,32},{32,24},{40,48},{48,40},{56,64},{64,56},{72,... | collective-permute-start | bytes 4534280 | tf_op jit(solution)/shard_map/ppermute | solution.py:703
  66.2 20.1 %copy-start = (f32[41,72,128]{2,1,0:T(8,128)}, f32[41,72,128]{2,1,0:T(8,128)S(1)}, u32[]{:S(2)}) copy-start(f32[41,72,128]{2,1,0:T(8,128)S(1)} %collective-permute-done.4.ev_any) | copy-start | bytes 4534276
  86.2 8.9 %copy-start.7 = (f32[3,9,32,4]{2,3,1,0:T(4,128)S(1)}, f32[3,9,32,4]{2,3,1,0:T(4,128)}, u32[]{:S(2)}) copy-start(f32[3,9,32,4]{2,3,1,0:T(4,128)} %param.22) | copy-start | bytes 41476
  88.6 14.8 %collective-permute-start.6 = (f32[9,72,128]{2,1,0:T(8,128)}, f32[9,72,128]{2,1,0:T(8,128)S(1)}, u32[]{:S(2)}, u32[]{:S(2)}) collective-permute-start(f32[9,72,128]{2,1,0:T(8,128)} %get-tuple-element.36), channel_id=1, source_target_pairs={{0,1},{1,0},{2,3},{3,2},{4,5},{5,4},{6,7},{7,6},{8,9},{9,8},{10,11... | collective-permute-start | bytes 995336 | tf_op jit(solution)/shard_map/ppermute | solution.py:706
  88.7 18.4 %collective-permute-start.7 = (f32[9,72,128]{2,1,0:T(8,128)}, f32[9,72,128]{2,1,0:T(8,128)S(1)}, u32[]{:S(2)}, u32[]{:S(2)}) collective-permute-start(f32[9,72,128]{2,1,0:T(8,128)} %get-tuple-element.37), channel_id=1, source_target_pairs={{1,2},{2,1},{3,4},{4,3},{5,6},{6,5},{9,10},{10,9},{11,12},{12,11},... | collective-permute-start | bytes 995336 | tf_op jit(solution)/shard_map/ppermute | solution.py:709
  103.4 3.8 %copy-start.2 = (f32[9,72,128]{2,1,0:T(8,128)}, f32[9,72,128]{2,1,0:T(8,128)S(1)}, u32[]{:S(2)}) copy-start(f32[9,72,128]{2,1,0:T(8,128)S(1)} %collective-permute-done.6.ce_ref) | copy-start | bytes 995332
  107.1 0.7 copy-start.3

commit v5 on v4

--- a/solution.py
+++ b/solution.py
@@ -70,8 +70,16 @@
             od_ref[t, c] = obj_ref[c, pl.ds(od_start, HALF), t * LANE : (t + 1) * LANE]
 
 
-def comb_kernel(ce_ref, co_ref, ev_in, od_in, comb_ref, ev_ref, od_ref, comb_sc, sems):
+def comb_kernel(ce_any, co_any, ev_in, od_in, comb_ref, ev_ref, od_ref, comb_sc, ce_ref, co_ref, sems):
     del ev_in, od_in
+    fetched = [
+        pltpu.make_async_copy(ce_any, ce_ref, sems.at[3]),
+        pltpu.make_async_copy(co_any, co_ref, sems.at[4]),
+    ]
+    for item in fetched:
+        item.start()
+    for item in fetched:
+        item.wait()
     row_odd = lax.axis_index("row") % 2
     col_odd = lax.axis_index("col") % 2
     first = lanes_of((HALF, LANE)) < HALF
@@ -416,16 +424,20 @@
 def denoise_kernel(
     low_any,
     up_any,
-    ce_ref,
-    co_ref,
+    ce_any,
+    co_any,
     conv_sc,
     map_sc,
     bias_ref,
-    out_ref,
+    out_any,
     low_st,
     up_st,
-    cond_st,
+    cond_a,
+    cond_b,
     half_sc,
+    ce_ref,
+    co_ref,
+    out_ref,
     sems,
 ):
     row_id = lax.axis_index("row")
@@ -435,6 +447,12 @@
     first = lane < HALF
     low_copy = pltpu.make_async_copy(low_any, low_st, sems.at[0])
     up_copy = pltpu.make_async_copy(up_any, up_st, sems.at[1])
+    side_copies = [
+        pltpu.make_async_copy(ce_any, ce_ref, sems.at[2]),
+        pltpu.make_async_copy(co_any, co_ref, sems.at[3]),
+    ]
+    side_copies[0].start()
+    side_copies[1].start()
     low_copy.start()
     up_copy.start()
 
@@ -470,6 +488,8 @@
             whole = jnp.concatenate(both, axis=0)[skip : skip + ROWS_SET]
             store[t, at, :] = store[t, at, :] + whole
 
+    side_copies[0].wait()
+    side_copies[1].wait()
     low_copy.wait()
     for c in range(4):
         add_sides(c)
@@ -482,7 +502,7 @@
     right_off = jnp.where(col_id == last_col, 512, 576)
     left_off = jnp.where(col_id == 0, 640, 576)
 
-    def prepare(store, first_row):
+    def prepare(store, first_row, cond_st):
         row_low = jnp.where(row_id == 0, -first_row * 4, 0)
         row_high = (jnp.where(row_id == last_row, 128, 131) - first_row) * 4
 
@@ -509,11 +529,11 @@
                 cond_st[2, i, pl.ds(at, 16), :] = both.astype(bf16)
             return carry
 
-        lax.fori_loop(0, 4 * ROWS_KEPT // 16, body, 0, unroll=7)
+        return body
 
     ones = jnp.ones((16, 640), bf16)
 
-    def layer_pass(layer, store, write_at, width):
+    def layer_pass(layer, cond_st, store, write_at, width, coming=None):
         groups = 17
         bias = bias_ref[layer]
 
@@ -544,6 +564,9 @@
         pairs_whole = (groups - 1) // 2
 
         def body(i, carry):
+            if coming is not None:
+                for j in range(4):
+                    coming(jnp.maximum(4 * i - 4, 0) + j, 0)
             first_map(2 * i + 1, 1)
             second_map(2 * i, 0)
             first_map(2 * i + 2, 0)
@@ -551,24 +574,28 @@
             return carry
 
         lax.fori_loop(0, pairs_whole, body, 0)
-        done = 2 * pairs_whole
-        if groups - done == 2:
-            first_map(done + 1, 1)
-            second_map(done, 0)
-            second_map(done + 1, 1)
-        else:
-            second_map(done, 0)
-
-    prepare(low_st, -3)
-    layer_pass(0, up_st, 0, 640)
-    prepare(up_st, -2)
-    layer_pass(1, low_st, 8, 640)
-    prepare(low_st, -3)
-    layer_pass(2, up_st, 0, 512)
-    for t in range(4):
-        for c in range(4):
-            out_ref[c, :, t * LANE : (t + 1) * LANE] = low_st[t, pl.ds(12 + c, 128, stride=4), :]
-            out_ref[4 + c, :, t * LANE : (t + 1) * LANE] = up_st[t, pl.ds(8 + c, 128, stride=4), :]
+        second_map(2 * pairs_whole, 0)
+        if coming is not None:
+            for j in range(28, 35):
+                coming(j, 0)
+
+    def finish(store, skip, at, sem):
+        for t in range(4):
+            for c in range(4):
+                lines = store[t, pl.ds(skip + c, 128, stride=4), :]
+                out_ref[at + c, :, t * LANE : (t + 1) * LANE] = lines
+        copy = pltpu.make_async_copy(out_ref.at[at : at + 4], out_any.at[at : at + 4], sem)
+        copy.start()
+        return copy
+
+    lax.fori_loop(0, 35, prepare(low_st, -3, cond_a), 0, unroll=7)
+    layer_pass(0, cond_a, up_st, 0, 640, prepare(up_st, -2, cond_b))
+    layer_pass(1, cond_b, low_st, 8, 640, prepare(low_st, -3, cond_a))
+    low_out = finish(low_st, 12, 0, sems.at[4])
+    layer_pass(2, cond_a, up_st, 0, 512)
+    up_out = finish(up_st, 8, 4, sems.at[5])
+    low_out.wait()
+    up_out.wait()
 
 
 def dft_matrices():
@@ -660,14 +687,18 @@
     return pl.pallas_call(
         denoise_kernel,
         out_shape=sds(8, 128, 512),
-        in_specs=[anywhere] * 2 + [vmem()] * 5,
-        out_specs=vmem(),
+        in_specs=[anywhere] * 4 + [vmem()] * 3,
+        out_specs=anywhere,
         scratch_shapes=[
             pltpu.VMEM((TILES, 4 * ROWS_KEPT, LANE), f32),
             pltpu.VMEM((TILES, 4 * ROWS_KEPT, LANE), f32),
             pltpu.VMEM((3, 3, 4 * ROWS_KEPT, 640), bf16),
+            pltpu.VMEM((3, 3, 4 * ROWS_KEPT, 640), bf16),
             pltpu.VMEM((2, 256, 640), f32),
-            pltpu.SemaphoreType.DMA((2,)),
+            pltpu.VMEM((9, STRIP, LANE), f32),
+            pltpu.VMEM((9, STRIP, LANE), f32),
+            pltpu.VMEM((8, 128, 512), f32),
+            pltpu.SemaphoreType.DMA((6,)),
         ],
         compiler_params=params(62),
         name="denoise",
@@ -740,9 +771,14 @@
     comb, ev, od = pl.pallas_call(
         comb_kernel,
         out_shape=[sds(8, 128, LANE), strip, strip],
-        in_specs=[vmem()] * 2 + [anywhere] * 2,
+        in_specs=[anywhere] * 4,
         out_specs=[anywhere] * 3,
-        scratch_shapes=[pltpu.VMEM((8, 128, LANE), f32), pltpu.SemaphoreType.DMA((3,))],
+        scratch_shapes=[
+            pltpu.VMEM((8, 128, LANE), f32),
+            pltpu.VMEM((8, HALF, LANE), f32),
+            pltpu.VMEM((8, HALF, LANE), f32),
+            pltpu.SemaphoreType.DMA((5,)),
+        ],
         input_output_aliases={2: 1, 3: 2},
         compiler_params=params(62),
         name="comb",

time: 132 us -> 130 us (0.985)
  Pallas kernels: 60 us -> 57.6 us
    pallas_call x1, Pallas kernels: 24 us -> 21.6 us  [denoise_call(): pl.pallas_call(denoise_kernel, out_shape=sds(8, 128, 512), in_specs=[anyw...]
where the time goes in v5:
time: 130 us
  Pallas kernels  57.6 us (44%)
  waiting for transfers between devices  48.1 us (37%)
  starting transfers between devices  19.9 us (15%)
  local copies, waits for them, and re-layouts  3.14 us (2%)
    ppermute x2, waiting for transfers between devices, row_od(): return lax.ppermute(x, 'row', pairs(rows, 1))  37.1 us
    pallas_call x1, Pallas kernels, denoise_call(): pl.pallas_call(denoise_kernel, out_shape=sds(8, 128, 512), in_specs=[anyw...  21.6 us
    pallas_call x1, Pallas kernels, slots_call(): pl.pallas_call(slots_kernel, out_shape=[sds(TILES, 8, BAND, LANE), sds(41...  18.6 us
    ppermute x2, starting transfers between devices, col_od(): return lax.ppermute(x, 'col', pairs(cols, 1))  12.6 us
    ppermute x2, waiting for transfers between devices, col_od(): return lax.ppermute(x, 'col', pairs(cols, 1))  10.1 us
    ppermute x2, starting transfers between devices, row_od(): return lax.ppermute(x, 'row', pairs(rows, 1))  5.46 us
    pallas_call x1, Pallas kernels, denoise_call(): pl.pallas_call(merge_kernel, out_shape=[lines] * 2, in_specs=[anywhere] *...  4.84 us
    pallas_call x1, Pallas kernels, per_device(): pl.pallas_call(strips_kernel, out_shape=[strip] * 2, in_specs=[vmem()], o...  3.23 us
  transfers between devices with their start and end apart: 8, of which 5 were waited for; matrix products, arithmetic and copies ran while one was open for 1% of the time, Pallas kernels for 8%

profile of v5, /device:TPU:23, one launch (start us, length us, event | category | flops | bytes accessed | tf_op | source)
XLA Modules:
  0.0 129.6 jit_solution(3941431303216134818)
XLA Ops:
  0.0 2.2 %pack.1 = (f32[8,64,128]{2,1,0:T(8,128)}, f32[8,64,128]{2,1,0:T(8,128)}) custom-call(f32[8,128,512]{2,1,0:T(8,128)} %bitcast.12, f32[8,128,512]{2,1,0:T(8,128)} %bitcast.13), custom_call_target="tpu_custom_call" | custom-call | tf_op jit(solution)/shard_map/pack/pallas_call | solution.py:749
  2.3 6.2 %collective-permute-start.1 = (f32[8,64,128]{2,1,0:T(8,128)}, f32[8,64,128]{2,1,0:T(8,128)S(1)}, u32[]{:S(2)}, u32[]{:S(2)}) collective-permute-start(f32[8,64,128]{2,1,0:T(8,128)} %get-tuple-element.24), channel_id=1, source_target_pairs={{1,2},{2,1},{3,4},{4,3},{5,6},{6,5},{9,10},{10,9},{11,12},{12,11},... | collective-permute-start | bytes 786440 | tf_op jit(solution)/shard_map/ppermute | solution.py:740
  8.4 3.2 %strips.1 = (f32[5,8,64,128]{3,2,1,0:T(8,128)}, f32[5,8,64,128]{3,2,1,0:T(8,128)}) custom-call(f32[8,128,512]{2,1,0:T(8,128)} %bitcast.14), custom_call_target="tpu_custom_call" | custom-call | bytes 4194304 | tf_op jit(solution)/shard_map/strips/pallas_call | solution.py:762
  11.7 6.4 %collective-permute-done.1.co_any = f32[8,64,128]{2,1,0:T(8,128)S(1)} collective-permute-done((f32[8,64,128]{2,1,0:T(8,128)}, f32[8,64,128]{2,1,0:T(8,128)S(1)}, u32[]{:S(2)}, u32[]{:S(2)}) %collective-permute-start.1) | collective-permute-done | bytes 262176 | tf_op jit(solution)/shard_map/ppermute | solution.py:740
  18.1 0.7 copy-done.5
  18.8 2.2 %comb.1 = (f32[8,128,128]{2,1,0:T(8,128)}, f32[5,8,64,128]{3,2,1,0:T(8,128)}, f32[5,8,64,128]{3,2,1,0:T(8,128)}) custom-call(f32[8,64,128]{2,1,0:T(8,128)} %copy-done.4, f32[8,64,128]{2,1,0:T(8,128)} %copy-done.5, f32[5,8,64,128]{3,2,1,0:T(8,128)} %get-tuple-element.25.ev_in, ...), custom_call_target="tpu_custom_call", output_to_operand_aliasing={{1}: (2, {}), {2}: (3, {})} | custom-call | tf_op jit(solution)/shard_map/comb/pallas_call | solution.py:771
  21.0 1.6 %collective-permute-start.2 = (f32[5,8,64,128]{3,2,1,0:T(8,128)}, f32[5,8,64,128]{3,2,1,0:T(8,128)S(1)}, u32[]{:S(2)}, u32[]{:S(2)}) collective-permute-start(f32[5,8,64,128]{3,2,1,0:T(8,128)} %get-tuple-element.28), channel_id=1, source_target_pairs={{0,8},{8,0},{16,24},{24,16},{32,40},{40,32},{48,56},{56,48},{64,72... | collective-permute-start | bytes 3932168 | tf_op jit(solution)/shard_map/ppermute | solution.py:731
  22.6 2.7 %collective-permute-start.3 = (f32[5,8,64,128]{3,2,1,0:T(8,128)}, f32[5,8,64,128]{3,2,1,0:T(8,128)}, u32[]{:S(2)}, u32[]{:S(2)}) collective-permute-start(f32[5,8,64,128]{3,2,1,0:T(8,128)} %get-tuple-element.29), channel_id=1, source_target_pairs={{8,16},{16,8},{24,32},{32,24},{40,48},{48,40},{56,64},{64,56},{72,... | collective-permute-start | bytes 3932168 | tf_op jit(solution)/shard_map/ppermute | solution.py:734
  26.0 0.9 fusion
  26.9 17.1 %collective-permute-done.3.od_ref = f32[5,8,64,128]{3,2,1,0:T(8,128)} collective-permute-done((f32[5,8,64,128]{3,2,1,0:T(8,128)}, f32[5,8,64,128]{3,2,1,0:T(8,128)}, u32[]{:S(2)}, u32[]{:S(2)}) %collective-permute-start.3) | collective-permute-done | bytes 1310752 | tf_op jit(solution)/shard_map/ppermute | solution.py:734
  44.0 18.6 %slots.1 = (f32[5,8,144,128]{3,2,1,0:T(8,128)}, f32[41,72,128]{2,1,0:T(8,128)}, f32[41,72,128]{2,1,0:T(8,128)}, f32[9,144,128]{2,1,0:T(8,128)}) custom-call(s32[4]{0:T(128)} %bitcast.18, s32[4]{0:T(128)} %bitcast.19, s32[1]{0:T(128)} %bitcast.11.count_ref, f32[8,128,512]{2,1,0:T(8,128)} %bitcast.15, f32[8,128,128]{2,1,0:T(8,128)} %get-tuple-element.27.comb_ref, ...), custom_call_target="tpu_custom_call" | custom-call | tf_op jit(solution)/shard_map/slots/pallas_call | solution.py:628
  62.6 0.1 collective-permute-start.4
  62.6 2.7 %collective-permute-start.5 = (f32[41,72,128]{2,1,0:T(8,128)}, f32[41,72,128]{2,1,0:T(8,128)}, u32[]{:S(2)}, u32[]{:S(2)}) collective-permute-start(f32[41,72,128]{2,1,0:T(8,128)} %get-tuple-element.32), channel_id=1, source_target_pairs={{8,16},{16,8},{24,32},{32,24},{40,48},{48,40},{56,64},{64,56},{72,... | collective-permute-start | bytes 4534280 | tf_op jit(solution)/shard_map/ppermute | solution.py:734
  65.4 0.8 collective-permute-done.4.ev_any
  66.2 20.1 %collective-permute-done.5.od_any = f32[41,72,128]{2,1,0:T(8,128)} collective-permute-done((f32[41,72,128]{2,1,0:T(8,128)}, f32[41,72,128]{2,1,0:T(8,128)}, u32[]{:S(2)}, u32[]{:S(2)}) %collective-permute-start.5) | collective-permute-done | bytes 1511456 | tf_op jit(solution)/shard_map/ppermute | solution.py:734
  86.3 2.4 %sides.1 = (f32[9,72,128]{2,1,0:T(8,128)}, f32[9,72,128]{2,1,0:T(8,128)}) custom-call(f32[9,144,128]{2,1,0:T(8,128)} %get-tuple-element.35.own_any, f32[41,72,128]{2,1,0:T(8,128)} %copy-done, f32[41,72,128]{2,1,0:T(8,128)} %collective-permute-done.5.od_any), custom_call_target="tpu_custom_call" | custom-call | tf_op jit(solution)/shard_map/sides/pallas_call | solution.py:807
  88.6 0.1 collective-permute-start.6
  88.7 6.4 %collective-permute-start.7 = (f32[9,72,128]{2,1,0:T(8,128)}, f32[9,72,128]{2,1,0:T(8,128)S(1)}, u32[]{:S(2)}, u32[]{:S(2)}) collective-permute-start(f32[9,72,128]{2,1,0:T(8,128)} %get-tuple-element.37), channel_id=1, source_target_pairs={{1,2},{2,1},{3,4},{4,3},{5,6},{6,5},{9,10},{10,9},{11,12},{12,11},... | collective-permute-start | bytes 995336 | tf_op jit(solution)/shard_map/ppermute | solution.py:740
  95.2 0.8 copy.19.taps_ref
  96.0 2.6 %weights.1 = (bf16[3,128,240]{2,1,0:T(8,128)(2,1)}, bf16[3,64,256]{2,1,0:T(8,128)(2,1)}, f32[3,32,128]{2,1,0:T(8,128)}) custom-call(f32[3,3,32,12]{3,2,1,0:T(8,128)} %copy.19.taps_ref, f32[3,32]{1,0:T(4,128)} %bias_ref.1, f32[3,4,32]{2,1,0:T(4,128)} %map_ref.1, f32[3,4]{1,0:T(4,128)} %map_bias_ref.1), custom_call_target="tpu_custom_call" | custom-call | flops 1048576 | bytes 3145728 | tf_op jit(solution)/shard_map/weights/pallas_call | solution.py:659
  98.5 4.8 %merge.1 = (f32[5,560,128]{2,1,0:T(8,128)}, f32[5,560,128]{2,1,0:T(8,128)}) custom-call(f32[5,8,144,128]{3,2,1,0:T(8,128)} %get-tuple-element.30.u_any, f32[41,72,128]{2,1,0:T(8,128)} %copy-done, f32[41,72,128]{2,1,0:T(8,128)} %collective-permute-done.5.od_any), custom_call_target="tpu_custom_call" | custom-call | flops 1048576 | bytes 9437184 | tf_op jit(solution)/shard_map/merge/pallas_call | solution.py:672
  103.4 3.7 %collective-permute-done.7.co_any = f32[9,72,128]{2,1,0:T(8,128)S(1)} collective-permute-done((f32[9,72,128]{2,1,0:T(8,128)}, f32[9,72,128]{2,1,0:T(8,128)S(1)}, u32[]{:S(2)}, u32[]{:S(2)}) %collective-permute-start.7) | collective-permute-done | bytes 331808 | tf_op jit(solution)/shard_map/ppermute | solution.py:740
  107.2 0.7 copy-done.3
  107.9 21.6 %denoise.1 = f32[8,128,512]{2,1,0:T(8,128)} custom-call(f32[5,560,128]{2,1,0:T(8,128)} %get-tuple-element.33.low_any, f32[5,560,128]{2,1,0:T(8,128)} %get-tuple-element.34.up_any, f32[9,72,128]{2,1,0:T(8,128)} %copy-done.2, f32[9,72,128]{2,1,0:T(8,128)} %copy-done.3, bf16[3,128,240]{2,1,0:T(8,128)(2,1)} %get-tuple-element.38.conv_sc, ...), custom_call_target="tpu_custom_call" | custom-call | tf_op jit(solution)/shard_map/denoise/pallas_call | solution.py:687
  (19 shorter events, 0.1 us)
Async XLA Ops:
  2.2 9.5 %collective-permute-start = (f32[8,64,128]{2,1,0:T(8,128)}, f32[8,64,128]{2,1,0:T(8,128)S(1)}, u32[]{:S(2)}, u32[]{:S(2)}) collective-permute-start(f32[8,64,128]{2,1,0:T(8,128)} %get-tuple-element.23), channel_id=1, source_target_pairs={{0,1},{1,0},{2,3},{3,2},{4,5},{5,4},{6,7},{7,6},{8,9},{9,8},{10,11... | collective-permute-start | bytes 786440 | tf_op jit(solution)/shard_map/ppermute | solution.py:737
  2.3 15.8 %collective-permute-start.1 = (f32[8,64,128]{2,1,0:T(8,128)}, f32[8,64,128]{2,1,0:T(8,128)S(1)}, u32[]{:S(2)}, u32[]{:S(2)}) collective-permute-start(f32[8,64,128]{2,1,0:T(8,128)} %get-tuple-element.24), channel_id=1, source_target_pairs={{1,2},{2,1},{3,4},{4,3},{5,6},{6,5},{9,10},{10,9},{11,12},{12,11},... | collective-permute-start | bytes 786440 | tf_op jit(solution)/shard_map/ppermute | solution.py:740
  11.7 6.4 %copy-start.4 = (f32[8,64,128]{2,1,0:T(8,128)}, f32[8,64,128]{2,1,0:T(8,128)S(1)}, u32[]{:S(2)}) copy-start(f32[8,64,128]{2,1,0:T(8,128)S(1)} %collective-permute-done.ce_any) | copy-start | bytes 786436
  18.1 0.7 copy-start.5
  18.8 7.3 %copy-start.6 = (f32[128,128]{1,0:T(8,128)S(1)}, f32[128,128]{1,0:T(8,128)}, u32[]{:S(2)}) copy-start(f32[128,128]{1,0:T(8,128)} %param.17) | copy-start | bytes 196612
  21.0 5.9 %collective-permute-start.2 = (f32[5,8,64,128]{3,2,1,0:T(8,128)}, f32[5,8,64,128]{3,2,1,0:T(8,128)S(1)}, u32[]{:S(2)}, u32[]{:S(2)}) collective-permute-start(f32[5,8,64,128]{3,2,1,0:T(8,128)} %get-tuple-element.28), channel_id=1, source_target_pairs={{0,8},{8,0},{16,24},{24,16},{32,40},{40,32},{48,56},{56,48},{64,72... | collective-permute-start | bytes 3932168 | tf_op jit(solution)/shard_map/ppermute | solution.py:731
  22.6 21.3 %collective-permute-start.3 = (f32[5,8,64,128]{3,2,1,0:T(8,128)}, f32[5,8,64,128]{3,2,1,0:T(8,128)}, u32[]{:S(2)}, u32[]{:S(2)}) collective-permute-start(f32[5,8,64,128]{3,2,1,0:T(8,128)} %get-tuple-element.29), channel_id=1, source_target_pairs={{8,16},{16,8},{24,32},{32,24},{40,48},{48,40},{56,64},{64,56},{72,... | collective-permute-start | bytes 3932168 | tf_op jit(solution)/shard_map/ppermute | solution.py:734
  26.9 17.1 %copy-start.1 = (f32[5,8,64,128]{3,2,1,0:T(8,128)}, f32[5,8,64,128]{3,2,1,0:T(8,128)S(1)}, u32[]{:S(2)}) copy-start(f32[5,8,64,128]{3,2,1,0:T(8,128)S(1)} %collective-permute-done.2.ev_ref) | copy-start | bytes 3932164
  62.6 3.6 %collective-permute-start.4 = (f32[41,72,128]{2,1,0:T(8,128)}, f32[41,72,128]{2,1,0:T(8,128)S(1)}, u32[]{:S(2)}, u32[]{:S(2)}) collective-permute-start(f32[41,72,128]{2,1,0:T(8,128)} %get-tuple-element.31), channel_id=1, source_target_pairs={{0,8},{8,0},{16,24},{24,16},{32,40},{40,32},{48,56},{56,48},{64,72... | collective-permute-start | bytes 4534280 | tf_op jit(solution)/shard_map/ppermute | solution.py:731
  62.6 23.6 %collective-permute-start.5 = (f32[41,72,128]{2,1,0:T(8,128)}, f32[41,72,128]{2,1,0:T(8,128)}, u32[]{:S(2)}, u32[]{:S(2)}) collective-permute-start(f32[41,72,128]{2,1,0:T(8,128)} %get-tuple-element.32), channel_id=1, source_target_pairs={{8,16},{16,8},{24,32},{32,24},{40,48},{48,40},{56,64},{64,56},{72,... | collective-permute-start | bytes 4534280 | tf_op jit(solution)/shard_map/ppermute | solution.py:734
  66.2 20.1 %copy-start = (f32[41,72,128]{2,1,0:T(8,128)}, f32[41,72,128]{2,1,0:T(8,128)S(1)}, u32[]{:S(2)}) copy-start(f32[41,72,128]{2,1,0:T(8,128)S(1)} %collective-permute-done.4.ev_any) | copy-start | bytes 4534276
  86.3 8.9 %copy-start.7 = (f32[3,9,32,4]{2,3,1,0:T(4,128)S(1)}, f32[3,9,32,4]{2,3,1,0:T(4,128)}, u32[]{:S(2)}) copy-start(f32[3,9,32,4]{2,3,1,0:T(4,128)} %param.22) | copy-start | bytes 41476
  88.6 14.8 %collective-permute-start.6 = (f32[9,72,128]{2,1,0:T(8,128)}, f32[9,72,128]{2,1,0:T(8,128)S(1)}, u32[]{:S(2)}, u32[]{:S(2)}) collective-permute-start(f32[9,72,128]{2,1,0:T(8,128)} %get-tuple-element.36), channel_id=1, source_target_pairs={{0,1},{1,0},{2,3},{3,2},{4,5},{5,4},{6,7},{7,6},{8,9},{9,8},{10,11... | collective-permute-start | bytes 995336 | tf_op jit(solution)/shard_map/ppermute | solution.py:737
  88.7 18.4 %collective-permute-start.7 = (f32[9,72,128]{2,1,0:T(8,128)}, f32[9,72,128]{2,1,0:T(8,128)S(1)}, u32[]{:S(2)}, u32[]{:S(2)}) collective-permute-start(f32[9,72,128]{2,1,0:T(8,128)} %get-tuple-element.37), channel_id=1, source_target_pairs={{1,2},{2,1},{3,4},{4,3},{5,6},{6,5},{9,10},{10,9},{11,12},{12,11},... | collective-permute-start | bytes 995336 | tf_op jit(solution)/shard_map/ppermute | solution.py:740
  103.4 3.8 %copy-start.2 = (f32[9,72,128]{2,1,0:T(8,128)}, f32[9,72,128]{2,1,0:T(8,128)S(1)}, u32[]{:S(2)}) copy-start(f32[9,72,128]{2,1,0:T(8,128)S(1)} %collective-permute-done.6.ce_any) | copy-start | bytes 995332
  107.1 0.7 copy-start.3

commit v6 on v5

--- a/solution.py
+++ b/solution.py
@@ -121,7 +121,8 @@
     right_b_any,
     u_ref,
     out_ev,
-    out_od,
+    out_odc,
+    out_odm,
     own_ref,
     frame,
     accum,
@@ -303,11 +304,11 @@
     ev_from = pl.multiple_of((1 - row_odd) * 184, 8)
     od_from = pl.multiple_of(row_odd * 184, 8)
     moves = [
-        (accum.at[4, :, pl.ds(od_from, STRIP), :], out_od.at[0:8]),
-        (extra.at[pl.ds(od_from, STRIP), :], out_od.at[8]),
+        (accum.at[4, :, pl.ds(od_from, STRIP), :], out_odc.at[0:8]),
+        (extra.at[pl.ds(od_from, STRIP), :], out_odc.at[8]),
     ]
     for t in range(4):
-        moves.append((accum.at[t, :, pl.ds(od_from, STRIP), :], out_od.at[9 + 8 * t : 17 + 8 * t]))
+        moves.append((accum.at[t, :, pl.ds(od_from, STRIP), :], out_odm.at[8 * t : 8 * t + 8]))
     moves.append((accum.at[4, :, pl.ds(ev_from, STRIP), :], out_ev.at[0:8]))
     moves.append((extra.at[pl.ds(ev_from, STRIP), :], out_ev.at[8]))
     for t in range(4):
@@ -326,11 +327,11 @@
         item.wait()
 
 
-def sides_kernel(own_any, ev_any, od_any, ce_ref, co_ref, own_ref, evc_ref, odc_ref, sems):
+def sides_kernel(own_any, ev_any, odc_any, ce_ref, co_ref, own_ref, evc_ref, odc_ref, sems):
     started = [
         pltpu.make_async_copy(own_any, own_ref, sems.at[0]),
         pltpu.make_async_copy(ev_any.at[0:9], evc_ref, sems.at[1]),
-        pltpu.make_async_copy(od_any.at[0:9], odc_ref, sems.at[2]),
+        pltpu.make_async_copy(odc_any, odc_ref, sems.at[2]),
     ]
     for item in started:
         item.start()
@@ -398,8 +399,13 @@
         bias_out[layer] = jnp.broadcast_to(out_bias, (32, LANE))
 
 
-def merge_kernel(u_any, ev_any, od_any, low_st, up_st, u_ref, ev_ref, od_ref, sems):
-    pairs = ((u_any, u_ref), (ev_any, ev_ref), (od_any, od_ref))
+def merge_kernel(u_any, ev_any, odc_any, odm_any, low_st, up_st, u_ref, ev_ref, od_ref, sems):
+    pairs = (
+        (u_any, u_ref),
+        (ev_any, ev_ref),
+        (odc_any, od_ref.at[0:9]),
+        (odm_any, od_ref.at[9:41]),
+    )
     started = [pltpu.make_async_copy(a, b, sems.at[i]) for i, (a, b) in enumerate(pairs)]
     for item in started:
         item.start()
@@ -630,11 +636,12 @@
         out_shape=[
             sds(TILES, 8, BAND, LANE),
             sds(41, STRIP, LANE),
-            sds(41, STRIP, LANE),
+            sds(9, STRIP, LANE),
+            sds(32, STRIP, LANE),
             sds(9, BAND, LANE),
         ],
         in_specs=[smem()] * 3 + [anywhere] * 5 + [vmem()] * 3 + [anywhere] * 4,
-        out_specs=[anywhere] * 4,
+        out_specs=[anywhere] * 5,
         scratch_shapes=[
             pltpu.VMEM((TILES, 8, 256, LANE), f32),
             pltpu.VMEM((TILES, 8, 256, LANE), f32),
@@ -653,7 +660,7 @@
     )(*operands)
 
 
-def denoise_call(u, ev, od, ce, co, taps, conv_bias, output_weight, output_bias):
+def denoise_call(u, ev, odc, odm, ce, co, taps, conv_bias, output_weight, output_bias):
     anywhere = pl.BlockSpec(memory_space=pl.ANY)
     lines = sds(TILES, 4 * ROWS_KEPT, LANE)
     conv_parts, map_parts, out_bias = pl.pallas_call(
@@ -672,18 +679,18 @@
     low, up = pl.pallas_call(
         merge_kernel,
         out_shape=[lines] * 2,
-        in_specs=[anywhere] * 3,
+        in_specs=[anywhere] * 4,
         out_specs=[vmem()] * 2,
         scratch_shapes=[
             pltpu.VMEM((TILES, 8, BAND, LANE), f32),
             pltpu.VMEM((41, STRIP, LANE), f32),
             pltpu.VMEM((41, STRIP, LANE), f32),
-            pltpu.SemaphoreType.DMA((3,)),
+            pltpu.SemaphoreType.DMA((4,)),
         ],
         compiler_params=params(62),
         cost_estimate=pl.CostEstimate(flops=1 << 20, bytes_accessed=9 << 20, transcendentals=0),
         name="merge",
-    )(u, ev, od)
+    )(u, ev, odc, odm)
     return pl.pallas_call(
         denoise_kernel,
         out_shape=sds(8, 128, 512),
@@ -788,7 +795,7 @@
     phase_re = jnp.cos(propagator_phase)
     phase_im = jnp.sin(propagator_phase)
     tables = [jnp.asarray(m) for m in dft_matrices()]
-    u, ev, od, own = slots_call(
+    u, ev, odc, odm, own = slots_call(
         position_rows.reshape(-1),
         position_cols.reshape(-1),
         tile_counts.reshape(-1),
@@ -802,7 +809,9 @@
         phase_im,
         *tables,
     )
-    od = row_od(od)
+    odc = row_od(odc)
+    odm, odc = lax.optimization_barrier((odm, odc))
+    odm = row_od(odm)
     ev = row_ev(ev)
     ce, co = pl.pallas_call(
         sides_kernel,
@@ -817,11 +826,11 @@
         ],
         compiler_params=params(62),
         name="sides",
-    )(own, ev, od)
+    )(own, ev, odc)
     ce = col_ev(ce)
     co = col_od(co)
     taps = conv_weight.reshape(3, 3, 3, 32, 4).transpose(0, 1, 3, 2, 4).reshape(3, 3, 32, 12)
-    out = denoise_call(u, ev, od, ce, co, taps, conv_bias, output_weight, output_bias)
+    out = denoise_call(u, ev, odc, odm, ce, co, taps, conv_bias, output_weight, output_bias)
     return out.reshape(4, 2, 128, 512)
 
 

time: 130 us -> 125 us (0.962)
  the two profiles are of different devices: /device:TPU:23 before, /device:TPU:97 now
where the time goes in v6:
time: 125 us; the launch traced here: 124 us
  Pallas kernels  57.5 us (46%)
  waiting for transfers between devices  38.6 us (31%)
  starting transfers between devices  22.8 us (18%)
  local copies, waits for them, and re-layouts  4.27 us (3%)
    pallas_call x1, Pallas kernels, denoise_call(): pl.pallas_call(denoise_kernel, out_shape=sds(8, 128, 512), in_specs=[anyw...  21.6 us
    ppermute x3, waiting for transfers between devices, row_od(): return lax.ppermute(x, 'row', pairs(rows, 1))  21.5 us
    pallas_call x1, Pallas kernels, slots_call(): pl.pallas_call(slots_kernel, out_shape=[sds(TILES, 8, BAND, LANE), sds(41...  18.6 us
    ppermute x2, waiting for transfers between devices, col_od(): return lax.ppermute(x, 'col', pairs(cols, 1))  12.9 us
    ppermute x3, starting transfers between devices, row_od(): return lax.ppermute(x, 'row', pairs(rows, 1))  9.99 us
    ppermute x2, starting transfers between devices, col_od(): return lax.ppermute(x, 'col', pairs(cols, 1))  7.73 us
    pallas_call x1, Pallas kernels, denoise_call(): pl.pallas_call(merge_kernel, out_shape=[lines] * 2, in_specs=[anywhere] *...  4.79 us
    ppermute x2, waiting for transfers between devices, col_ev(): return lax.ppermute(x, 'col', pairs(cols, 0))  4.13 us
  transfers between devices with their start and end apart: 9, of which 7 were waited for; matrix products, arithmetic and copies ran while one was open for 1% of the time, Pallas kernels for 10%

profile of v6, /device:TPU:97, one launch (start us, length us, event | category | flops | bytes accessed | tf_op | source)
XLA Modules:
  0.0 124.0 jit_solution(9505170313422013960)
XLA Ops:
  0.0 2.2 %pack.1 = (f32[8,64,128]{2,1,0:T(8,128)}, f32[8,64,128]{2,1,0:T(8,128)}) custom-call(f32[8,128,512]{2,1,0:T(8,128)} %bitcast.12, f32[8,128,512]{2,1,0:T(8,128)} %bitcast.13), custom_call_target="tpu_custom_call" | custom-call | tf_op jit(solution)/shard_map/pack/pallas_call | solution.py:756
  2.2 2.9 %collective-permute-start = (f32[8,64,128]{2,1,0:T(8,128)}, f32[8,64,128]{2,1,0:T(8,128)S(1)}, u32[]{:S(2)}, u32[]{:S(2)}) collective-permute-start(f32[8,64,128]{2,1,0:T(8,128)} %get-tuple-element.26), channel_id=1, source_target_pairs={{0,1},{1,0},{2,3},{3,2},{4,5},{5,4},{6,7},{7,6},{8,9},{9,8},{10,11... | collective-permute-start | bytes 786440 | tf_op jit(solution)/shard_map/ppermute | solution.py:744
  5.1 1.9 %collective-permute-start.1 = (f32[8,64,128]{2,1,0:T(8,128)}, f32[8,64,128]{2,1,0:T(8,128)S(1)}, u32[]{:S(2)}, u32[]{:S(2)}) collective-permute-start(f32[8,64,128]{2,1,0:T(8,128)} %get-tuple-element.27), channel_id=1, source_target_pairs={{1,2},{2,1},{3,4},{4,3},{5,6},{6,5},{9,10},{10,9},{11,12},{12,11},... | collective-permute-start | bytes 786440 | tf_op jit(solution)/shard_map/ppermute | solution.py:747
  7.0 3.2 %strips.1 = (f32[5,8,64,128]{3,2,1,0:T(8,128)}, f32[5,8,64,128]{3,2,1,0:T(8,128)}) custom-call(f32[8,128,512]{2,1,0:T(8,128)} %bitcast.14), custom_call_target="tpu_custom_call" | custom-call | bytes 4194304 | tf_op jit(solution)/shard_map/strips/pallas_call | solution.py:769
  10.3 0.8 collective-permute-done.ce_any
  11.1 5.4 %collective-permute-done.1.co_any = f32[8,64,128]{2,1,0:T(8,128)S(1)} collective-permute-done((f32[8,64,128]{2,1,0:T(8,128)}, f32[8,64,128]{2,1,0:T(8,128)S(1)}, u32[]{:S(2)}, u32[]{:S(2)}) %collective-permute-start.1) | collective-permute-done | bytes 262176 | tf_op jit(solution)/shard_map/ppermute | solution.py:747
  17.2 2.2 %comb.1 = (f32[8,128,128]{2,1,0:T(8,128)}, f32[5,8,64,128]{3,2,1,0:T(8,128)}, f32[5,8,64,128]{3,2,1,0:T(8,128)}) custom-call(f32[8,64,128]{2,1,0:T(8,128)} %copy-done.5, f32[8,64,128]{2,1,0:T(8,128)} %copy-done.6, f32[5,8,64,128]{3,2,1,0:T(8,128)} %get-tuple-element.28.ev_in, ...), custom_call_target="tpu_custom_call", output_to_operand_aliasing={{1}: (2, {}), {2}: (3, {})} | custom-call | tf_op jit(solution)/shard_map/comb/pallas_call | solution.py:778
  19.4 1.9 %collective-permute-start.2 = (f32[5,8,64,128]{3,2,1,0:T(8,128)}, f32[5,8,64,128]{3,2,1,0:T(8,128)S(1)}, u32[]{:S(2)}, u32[]{:S(2)}) collective-permute-start(f32[5,8,64,128]{3,2,1,0:T(8,128)} %get-tuple-element.31), channel_id=1, source_target_pairs={{0,8},{8,0},{16,24},{24,16},{32,40},{40,32},{48,56},{56,48},{64,72... | collective-permute-start | bytes 3932168 | tf_op jit(solution)/shard_map/ppermute | solution.py:738
  21.3 3.0 %collective-permute-start.3 = (f32[5,8,64,128]{3,2,1,0:T(8,128)}, f32[5,8,64,128]{3,2,1,0:T(8,128)}, u32[]{:S(2)}, u32[]{:S(2)}) collective-permute-start(f32[5,8,64,128]{3,2,1,0:T(8,128)} %get-tuple-element.32), channel_id=1, source_target_pairs={{8,16},{16,8},{24,32},{32,24},{40,48},{48,40},{56,64},{64,56},{72,... | collective-permute-start | bytes 3932168 | tf_op jit(solution)/shard_map/ppermute | solution.py:741
  25.0 0.9 fusion
  25.9 14.6 %collective-permute-done.3.od_ref = f32[5,8,64,128]{3,2,1,0:T(8,128)} collective-permute-done((f32[5,8,64,128]{3,2,1,0:T(8,128)}, f32[5,8,64,128]{3,2,1,0:T(8,128)}, u32[]{:S(2)}, u32[]{:S(2)}) %collective-permute-start.3) | collective-permute-done | bytes 1310752 | tf_op jit(solution)/shard_map/ppermute | solution.py:741
  40.6 18.6 %slots.1 = (f32[5,8,144,128]{3,2,1,0:T(8,128)}, f32[41,72,128]{2,1,0:T(8,128)}, f32[9,72,128]{2,1,0:T(8,128)}, f32[32,72,128]{2,1,0:T(8,128)}, f32[9,144,128]{2,1,0:T(8,128)}) custom-call(s32[4]{0:T(128)} %bitcast.18, s32[4]{0:T(128)} %bitcast.19, s32[1]{0:T(128)} %bitcast.11.count_ref, f32[8,128,512]{2,1,0:T(8,128)} %bitcast.15, ...), custom_call_target="tpu_custom_call" | custom-call | tf_op jit(solution)/shard_map/slots/pallas_call | solution.py:634
  59.3 3.5 %collective-permute-start.5 = (f32[9,72,128]{2,1,0:T(8,128)}, f32[9,72,128]{2,1,0:T(8,128)S(1)}, u32[]{:S(2)}, u32[]{:S(2)}) collective-permute-start(f32[9,72,128]{2,1,0:T(8,128)} %get-tuple-element.36), channel_id=1, source_target_pairs={{8,16},{16,8},{24,32},{32,24},{40,48},{48,40},{56,64},{64,56},{72,... | collective-permute-start | bytes 995336 | tf_op jit(solution)/shard_map/ppermute | solution.py:741
  62.8 5.1 %collective-permute-done.5.odc_any = f32[9,72,128]{2,1,0:T(8,128)S(1)} collective-permute-done((f32[9,72,128]{2,1,0:T(8,128)}, f32[9,72,128]{2,1,0:T(8,128)S(1)}, u32[]{:S(2)}, u32[]{:S(2)}) %collective-permute-start.5) | collective-permute-done | bytes 331808 | tf_op jit(solution)/shard_map/ppermute | solution.py:741
  67.9 3.5 %collective-permute-start.6 = (f32[32,72,128]{2,1,0:T(8,128)}, f32[32,72,128]{2,1,0:T(8,128)}, u32[]{:S(2)}, u32[]{:S(2)}) collective-permute-start(f32[32,72,128]{2,1,0:T(8,128)} %get-tuple-element.38), channel_id=1, source_target_pairs={{8,16},{16,8},{24,32},{32,24},{40,48},{48,40},{56,64},{64,56},{72,... | collective-permute-start | bytes 3538952 | tf_op jit(solution)/shard_map/ppermute | solution.py:741
  71.4 1.1 copy-done
  72.5 2.3 %sides.1 = (f32[9,72,128]{2,1,0:T(8,128)}, f32[9,72,128]{2,1,0:T(8,128)}) custom-call(f32[9,144,128]{2,1,0:T(8,128)} %get-tuple-element.41.own_any, f32[41,72,128]{2,1,0:T(8,128)} %copy-done, f32[9,72,128]{2,1,0:T(8,128)} %copy-done.1), custom_call_target="tpu_custom_call" | custom-call | tf_op jit(solution)/shard_map/sides/pallas_call | solution.py:816
  75.0 5.8 %collective-permute-start.8 = (f32[9,72,128]{2,1,0:T(8,128)}, f32[9,72,128]{2,1,0:T(8,128)S(1)}, u32[]{:S(2)}, u32[]{:S(2)}) collective-permute-start(f32[9,72,128]{2,1,0:T(8,128)} %get-tuple-element.43), channel_id=1, source_target_pairs={{1,2},{2,1},{3,4},{4,3},{5,6},{6,5},{9,10},{10,9},{11,12},{12,11},... | collective-permute-start | bytes 995336 | tf_op jit(solution)/shard_map/ppermute | solution.py:747
  81.6 2.6 %weights.1 = (bf16[3,128,240]{2,1,0:T(8,128)(2,1)}, bf16[3,64,256]{2,1,0:T(8,128)(2,1)}, f32[3,32,128]{2,1,0:T(8,128)}) custom-call(f32[3,3,32,12]{3,2,1,0:T(8,128)} %copy.19.taps_ref, f32[3,32]{1,0:T(4,128)} %bias_ref.1, f32[3,4,32]{2,1,0:T(4,128)} %map_ref.1, f32[3,4]{1,0:T(4,128)} %map_bias_ref.1), custom_call_target="tpu_custom_call" | custom-call | flops 1048576 | bytes 3145728 | tf_op jit(solution)/shard_map/weights/pallas_call | solution.py:666
  84.2 1.7 %collective-permute-done.6.odm_any = f32[32,72,128]{2,1,0:T(8,128)} collective-permute-done((f32[32,72,128]{2,1,0:T(8,128)}, f32[32,72,128]{2,1,0:T(8,128)}, u32[]{:S(2)}, u32[]{:S(2)}) %collective-permute-start.6) | collective-permute-done | bytes 1179680 | tf_op jit(solution)/shard_map/ppermute | solution.py:741
  85.9 4.8 %merge.1 = (f32[5,560,128]{2,1,0:T(8,128)}, f32[5,560,128]{2,1,0:T(8,128)}) custom-call(f32[5,8,144,128]{3,2,1,0:T(8,128)} %get-tuple-element.33.u_any, f32[41,72,128]{2,1,0:T(8,128)} %copy-done, f32[9,72,128]{2,1,0:T(8,128)} %copy-done.1, f32[32,72,128]{2,1,0:T(8,128)} %collective-permute-done.6.odm_any), custom_call_target="tpu_custom_call" | custom-call | flops 1048576 | bytes 9437184 | tf_op jit(solution)/shard_map/merge/pallas_call | solution.py:679
  90.7 3.3 %collective-permute-done.7.ce_any = f32[9,72,128]{2,1,0:T(8,128)S(1)} collective-permute-done((f32[9,72,128]{2,1,0:T(8,128)}, f32[9,72,128]{2,1,0:T(8,128)S(1)}, u32[]{:S(2)}, u32[]{:S(2)}) %collective-permute-start.7) | collective-permute-done | bytes 331808 | tf_op jit(solution)/shard_map/ppermute | solution.py:744
  94.0 7.6 %collective-permute-done.8.co_any = f32[9,72,128]{2,1,0:T(8,128)S(1)} collective-permute-done((f32[9,72,128]{2,1,0:T(8,128)}, f32[9,72,128]{2,1,0:T(8,128)S(1)}, u32[]{:S(2)}, u32[]{:S(2)}) %collective-permute-start.8) | collective-permute-done | bytes 331808 | tf_op jit(solution)/shard_map/ppermute | solution.py:747
  102.3 21.6 %denoise.1 = f32[8,128,512]{2,1,0:T(8,128)} custom-call(f32[5,560,128]{2,1,0:T(8,128)} %get-tuple-element.39.low_any, f32[5,560,128]{2,1,0:T(8,128)} %get-tuple-element.40.up_any, f32[9,72,128]{2,1,0:T(8,128)} %copy-done.3, f32[9,72,128]{2,1,0:T(8,128)} %copy-done.4, bf16[3,128,240]{2,1,0:T(8,128)(2,1)} %get-tuple-element.44.conv_sc, ...), custom_call_target="tpu_custom_call" | custom-call | tf_op jit(solution)/shard_map/denoise/pallas_call | solution.py:694
  (23 shorter events, 2.4 us)
Async XLA Ops:
  2.2 8.9 %collective-permute-start = (f32[8,64,128]{2,1,0:T(8,128)}, f32[8,64,128]{2,1,0:T(8,128)S(1)}, u32[]{:S(2)}, u32[]{:S(2)}) collective-permute-start(f32[8,64,128]{2,1,0:T(8,128)} %get-tuple-element.26), channel_id=1, source_target_pairs={{0,1},{1,0},{2,3},{3,2},{4,5},{5,4},{6,7},{7,6},{8,9},{9,8},{10,11... | collective-permute-start | bytes 786440 | tf_op jit(solution)/shard_map/ppermute | solution.py:744
  5.1 11.4 %collective-permute-start.1 = (f32[8,64,128]{2,1,0:T(8,128)}, f32[8,64,128]{2,1,0:T(8,128)S(1)}, u32[]{:S(2)}, u32[]{:S(2)}) collective-permute-start(f32[8,64,128]{2,1,0:T(8,128)} %get-tuple-element.27), channel_id=1, source_target_pairs={{1,2},{2,1},{3,4},{4,3},{5,6},{6,5},{9,10},{10,9},{11,12},{12,11},... | collective-permute-start | bytes 786440 | tf_op jit(solution)/shard_map/ppermute | solution.py:747
  11.1 5.4 %copy-start.5 = (f32[8,64,128]{2,1,0:T(8,128)}, f32[8,64,128]{2,1,0:T(8,128)S(1)}, u32[]{:S(2)}) copy-start(f32[8,64,128]{2,1,0:T(8,128)S(1)} %collective-permute-done.ce_any) | copy-start | bytes 786436
  16.5 0.7 copy-start.6
  17.2 7.8 %copy-start.7 = (f32[128,128]{1,0:T(8,128)S(1)}, f32[128,128]{1,0:T(8,128)}, u32[]{:S(2)}) copy-start(f32[128,128]{1,0:T(8,128)} %param.17) | copy-start | bytes 196612
  19.4 6.5 %collective-permute-start.2 = (f32[5,8,64,128]{3,2,1,0:T(8,128)}, f32[5,8,64,128]{3,2,1,0:T(8,128)S(1)}, u32[]{:S(2)}, u32[]{:S(2)}) collective-permute-start(f32[5,8,64,128]{3,2,1,0:T(8,128)} %get-tuple-element.31), channel_id=1, source_target_pairs={{0,8},{8,0},{16,24},{24,16},{32,40},{40,32},{48,56},{56,48},{64,72... | collective-permute-start | bytes 3932168 | tf_op jit(solution)/shard_map/ppermute | solution.py:738
  21.3 19.2 %collective-permute-start.3 = (f32[5,8,64,128]{3,2,1,0:T(8,128)}, f32[5,8,64,128]{3,2,1,0:T(8,128)}, u32[]{:S(2)}, u32[]{:S(2)}) collective-permute-start(f32[5,8,64,128]{3,2,1,0:T(8,128)} %get-tuple-element.32), channel_id=1, source_target_pairs={{8,16},{16,8},{24,32},{32,24},{40,48},{48,40},{56,64},{64,56},{72,... | collective-permute-start | bytes 3932168 | tf_op jit(solution)/shard_map/ppermute | solution.py:741
  25.9 14.6 %copy-start.2 = (f32[5,8,64,128]{3,2,1,0:T(8,128)}, f32[5,8,64,128]{3,2,1,0:T(8,128)S(1)}, u32[]{:S(2)}) copy-start(f32[5,8,64,128]{3,2,1,0:T(8,128)S(1)} %collective-permute-done.2.ev_ref) | copy-start | bytes 3932164
  59.2 21.6 %copy-start.8 = (f32[3,9,32,4]{2,3,1,0:T(4,128)S(1)}, f32[3,9,32,4]{2,3,1,0:T(4,128)}, u32[]{:S(2)}) copy-start(f32[3,9,32,4]{2,3,1,0:T(4,128)} %param.22) | copy-start | bytes 41476
  59.2 12.2 %collective-permute-start.4 = (f32[41,72,128]{2,1,0:T(8,128)}, f32[41,72,128]{2,1,0:T(8,128)S(1)}, u32[]{:S(2)}, u32[]{:S(2)}) collective-permute-start(f32[41,72,128]{2,1,0:T(8,128)} %get-tuple-element.34), channel_id=1, source_target_pairs={{0,8},{8,0},{16,24},{24,16},{32,40},{40,32},{48,56},{56,48},{64,72... | collective-permute-start | bytes 4534280 | tf_op jit(solution)/shard_map/ppermute | solution.py:738
  59.3 8.6 %collective-permute-start.5 = (f32[9,72,128]{2,1,0:T(8,128)}, f32[9,72,128]{2,1,0:T(8,128)S(1)}, u32[]{:S(2)}, u32[]{:S(2)}) collective-permute-start(f32[9,72,128]{2,1,0:T(8,128)} %get-tuple-element.36), channel_id=1, source_target_pairs={{8,16},{16,8},{24,32},{32,24},{40,48},{48,40},{56,64},{64,56},{72,... | collective-permute-start | bytes 995336 | tf_op jit(solution)/shard_map/ppermute | solution.py:741
  67.9 3.5 %copy-start.1 = (f32[9,72,128]{2,1,0:T(8,128)}, f32[9,72,128]{2,1,0:T(8,128)S(1)}, u32[]{:S(2)}) copy-start(f32[9,72,128]{2,1,0:T(8,128)S(1)} %collective-permute-done.5.odc_any) | copy-start | bytes 995332
  67.9 18.0 %collective-permute-start.6 = (f32[32,72,128]{2,1,0:T(8,128)}, f32[32,72,128]{2,1,0:T(8,128)}, u32[]{:S(2)}, u32[]{:S(2)}) collective-permute-start(f32[32,72,128]{2,1,0:T(8,128)} %get-tuple-element.38), channel_id=1, source_target_pairs={{8,16},{16,8},{24,32},{32,24},{40,48},{48,40},{56,64},{64,56},{72,... | collective-permute-start | bytes 3538952 | tf_op jit(solution)/shard_map/ppermute | solution.py:741
  71.4 1.1 copy-start
  74.9 19.1 %collective-permute-start.7 = (f32[9,72,128]{2,1,0:T(8,128)}, f32[9,72,128]{2,1,0:T(8,128)S(1)}, u32[]{:S(2)}, u32[]{:S(2)}) collective-permute-start(f32[9,72,128]{2,1,0:T(8,128)} %get-tuple-element.42), channel_id=1, source_target_pairs={{0,1},{1,0},{2,3},{3,2},{4,5},{5,4},{6,7},{7,6},{8,9},{9,8},{10,11... | collective-permute-start | bytes 995336 | tf_op jit(solution)/shard_map/ppermute | solution.py:744
  75.0 26.6 %collective-permute-start.8 = (f32[9,72,128]{2,1,0:T(8,128)}, f32[9,72,128]{2,1,0:T(8,128)S(1)}, u32[]{:S(2)}, u32[]{:S(2)}) collective-permute-start(f32[9,72,128]{2,1,0:T(8,128)} %get-tuple-element.43), channel_id=1, source_target_pairs={{1,2},{2,1},{3,4},{4,3},{5,6},{6,5},{9,10},{10,9},{11,12},{12,11},... | collective-permute-start | bytes 995336 | tf_op jit(solution)/shard_map/ppermute | solution.py:747
  94.0 7.6 %copy-start.3 = (f32[9,72,128]{2,1,0:T(8,128)}, f32[9,72,128]{2,1,0:T(8,128)S(1)}, u32[]{:S(2)}) copy-start(f32[9,72,128]{2,1,0:T(8,128)S(1)} %collective-permute-done.7.ce_any) | copy-start | bytes 995332
  101.6 0.7 copy-start.4

commit v7 on v6

--- a/solution.py
+++ b/solution.py
@@ -70,8 +70,8 @@
             od_ref[t, c] = obj_ref[c, pl.ds(od_start, HALF), t * LANE : (t + 1) * LANE]
 
 
-def comb_kernel(ce_any, co_any, ev_in, od_in, comb_ref, ev_ref, od_ref, comb_sc, ce_ref, co_ref, sems):
-    del ev_in, od_in
+def comb_kernel(ce_any, co_any, ev_in, comb_ref, ev_ref, od_ref, comb_sc, ce_ref, co_ref, sems):
+    del ev_in
     fetched = [
         pltpu.make_async_copy(ce_any, ce_ref, sems.at[3]),
         pltpu.make_async_copy(co_any, co_ref, sems.at[4]),
@@ -93,7 +93,7 @@
     ev_start = pl.multiple_of((1 - row_odd) * HALF, HALF)
     od_start = pl.multiple_of(row_odd * HALF, HALF)
     started = [
-        pltpu.make_async_copy(comb_sc.at[:, pl.ds(od_start, HALF), :], od_ref.at[4], sems.at[0]),
+        pltpu.make_async_copy(comb_sc.at[:, pl.ds(od_start, HALF), :], od_ref, sems.at[0]),
         pltpu.make_async_copy(comb_sc.at[:, pl.ds(ev_start, HALF), :], ev_ref.at[4], sems.at[1]),
         pltpu.make_async_copy(comb_sc, comb_ref, sems.at[2]),
     ]
@@ -110,7 +110,8 @@
     obj_ref,
     comb_ref,
     ev_ref,
-    od_ref,
+    odc_ref,
+    odm_ref,
     meas_any,
     probe_ref,
     phase_re_ref,
@@ -144,7 +145,8 @@
         copies.append((obj_ref.at[:, :, t * LANE : (t + 1) * LANE], frame.at[t, :, HALF:192, :]))
     copies.append((comb_ref, frame.at[4, :, HALF:192, :]))
     copies.append((ev_ref, frame.at[:, :, pl.ds(ev_at, HALF), :]))
-    copies.append((od_ref, frame.at[:, :, pl.ds(od_at, HALF), :]))
+    copies.append((odc_ref, frame.at[4, :, pl.ds(od_at, HALF), :]))
+    copies.append((odm_ref, frame.at[0:4, :, pl.ds(od_at, HALF), :]))
     started = [pltpu.make_async_copy(src, dst, sems.at[i]) for i, (src, dst) in enumerate(copies)]
     late = [
         (left_f_any, left_f_ref),
@@ -153,7 +155,7 @@
         (left_b_any, left_b_ref),
         (meas_any, meas_ref),
     ]
-    later = [pltpu.make_async_copy(src, dst, sems.at[7 + i]) for i, (src, dst) in enumerate(late)]
+    later = [pltpu.make_async_copy(src, dst, sems.at[8 + i]) for i, (src, dst) in enumerate(late)]
     for item in started + later:
         item.start()
     accum[...] = jnp.zeros(accum.shape, f32)
@@ -315,12 +317,12 @@
         moves.append((accum.at[t, :, pl.ds(ev_from, STRIP), :], out_ev.at[9 + 8 * t : 17 + 8 * t]))
     moves.append((accum.at[4, :, 56:200, :], own_ref.at[0:8]))
     moves.append((extra.at[56:200, :], own_ref.at[8]))
-    sent = [pltpu.make_async_copy(src, dst, sems.at[12 + i]) for i, (src, dst) in enumerate(moves)]
+    sent = [pltpu.make_async_copy(src, dst, sems.at[13 + i]) for i, (src, dst) in enumerate(moves)]
     for item in sent:
         item.start()
     for t in range(TILES):
         frame[t, :, 56:200, :] = frame[t, :, 56:200, :] + accum[t, :, 56:200, :]
-        item = pltpu.make_async_copy(frame.at[t, :, 56:200, :], u_ref.at[t], sems.at[26 + t])
+        item = pltpu.make_async_copy(frame.at[t, :, 56:200, :], u_ref.at[t], sems.at[27 + t])
         item.start()
         sent.append(item)
     for item in sent:
@@ -640,7 +642,7 @@
             sds(32, STRIP, LANE),
             sds(9, BAND, LANE),
         ],
-        in_specs=[smem()] * 3 + [anywhere] * 5 + [vmem()] * 3 + [anywhere] * 4,
+        in_specs=[smem()] * 3 + [anywhere] * 6 + [vmem()] * 3 + [anywhere] * 4,
         out_specs=[anywhere] * 5,
         scratch_shapes=[
             pltpu.VMEM((TILES, 8, 256, LANE), f32),
@@ -653,7 +655,7 @@
             pltpu.VMEM((768, 256), bf16),
             pltpu.VMEM((768, 256), bf16),
             pltpu.VMEM((4, LANE, LANE), f32),
-            pltpu.SemaphoreType.DMA((31,)),
+            pltpu.SemaphoreType.DMA((32,)),
         ],
         compiler_params=params(62),
         name="slots",
@@ -766,19 +768,21 @@
     co = col_od(co)
     anywhere = pl.BlockSpec(memory_space=pl.ANY)
     strip = sds(TILES, 8, HALF, LANE)
-    ev, od = pl.pallas_call(
+    ev, odm = pl.pallas_call(
         strips_kernel,
-        out_shape=[strip] * 2,
+        out_shape=[strip, sds(4, 8, HALF, LANE)],
         in_specs=[vmem()],
         out_specs=[vmem()] * 2,
         compiler_params=params(62),
         cost_estimate=pl.CostEstimate(flops=0, bytes_accessed=4 << 20, transcendentals=0),
         name="strips",
     )(obj)
-    comb, ev, od = pl.pallas_call(
+    odm = row_od(odm)
+    ce, co, odm = lax.optimization_barrier((ce, co, odm))
+    comb, ev, odc = pl.pallas_call(
         comb_kernel,
-        out_shape=[sds(8, 128, LANE), strip, strip],
-        in_specs=[anywhere] * 4,
+        out_shape=[sds(8, 128, LANE), strip, sds(8, HALF, LANE)],
+        in_specs=[anywhere] * 3,
         out_specs=[anywhere] * 3,
         scratch_shapes=[
             pltpu.VMEM((8, 128, LANE), f32),
@@ -786,11 +790,11 @@
             pltpu.VMEM((8, HALF, LANE), f32),
             pltpu.SemaphoreType.DMA((5,)),
         ],
-        input_output_aliases={2: 1, 3: 2},
+        input_output_aliases={2: 1},
         compiler_params=params(62),
         name="comb",
-    )(ce, co, ev, od)
-    od = row_od(od)
+    )(ce, co, ev)
+    odc = row_od(odc)
     ev = row_ev(ev)
     phase_re = jnp.cos(propagator_phase)
     phase_im = jnp.sin(propagator_phase)
@@ -802,7 +806,8 @@
         obj,
         comb,
         ev,
-        od,
+        odc,
+        odm,
         intensities.reshape(4, LANE, LANE),
         probe_field,
         phase_re,

time: 125 us -> 127 us (1.016)
  the two profiles are of different devices: /device:TPU:97 before, /device:TPU:63 now
where the time goes in v7:
time: 127 us; the launch traced here: 126 us
  Pallas kernels  57.4 us (45%)
  waiting for transfers between devices  40.6 us (32%)
  starting transfers between devices  21.9 us (17%)
  local copies, waits for them, and re-layouts  5.35 us (4%)
    ppermute x2, waiting for transfers between devices, col_ev(): return lax.ppermute(x, 'col', pairs(cols, 0))  23.7 us
    pallas_call x1, Pallas kernels, denoise_call(): pl.pallas_call(denoise_kernel, out_shape=sds(8, 128, 512), in_specs=[anyw...  21.6 us
    pallas_call x1, Pallas kernels, slots_call(): pl.pallas_call(slots_kernel, out_shape=[sds(TILES, 8, BAND, LANE), sds(41...  18.6 us
    ppermute x2, waiting for transfers between devices, col_od(): return lax.ppermute(x, 'col', pairs(cols, 1))  15.4 us
    ppermute x2, starting transfers between devices, col_od(): return lax.ppermute(x, 'col', pairs(cols, 1))  11.3 us
    ppermute x2, starting transfers between devices, row_ev(): return lax.ppermute(x, 'row', pairs(rows, 0))  5.8 us
    pallas_call x1, Pallas kernels, denoise_call(): pl.pallas_call(merge_kernel, out_shape=[lines] * 2, in_specs=[anywhere] *...  4.79 us
    ppermute x4, starting transfers between devices, row_od(): return lax.ppermute(x, 'row', pairs(rows, 1))  3.75 us
  transfers between devices with their start and end apart: 10, of which 6 were waited for; matrix products, arithmetic and copies ran while one was open for 1% of the time, Pallas kernels for 9%

profile of v7, /device:TPU:63, one launch (start us, length us, event | category | flops | bytes accessed | tf_op | source)
XLA Modules:
  0.0 126.2 jit_solution(10707574727354876485)
XLA Ops:
  0.0 3.2 %strips.1 = (f32[5,8,64,128]{3,2,1,0:T(8,128)}, f32[4,8,64,128]{3,2,1,0:T(8,128)}) custom-call(f32[8,128,512]{2,1,0:T(8,128)} %bitcast.12), custom_call_target="tpu_custom_call" | custom-call | bytes 4194304 | tf_op jit(solution)/shard_map/strips/pallas_call | solution.py:771
  3.2 0.7 collective-permute-start.2
  3.9 2.2 %pack.1 = (f32[8,64,128]{2,1,0:T(8,128)}, f32[8,64,128]{2,1,0:T(8,128)}) custom-call(f32[8,128,512]{2,1,0:T(8,128)} %bitcast.13, f32[8,128,512]{2,1,0:T(8,128)} %bitcast.14), custom_call_target="tpu_custom_call" | custom-call | tf_op jit(solution)/shard_map/pack/pallas_call | solution.py:758
  6.1 1.0 collective-permute-start
  7.1 5.3 %collective-permute-start.1 = (f32[8,64,128]{2,1,0:T(8,128)}, f32[8,64,128]{2,1,0:T(8,128)S(1)}, u32[]{:S(2)}, u32[]{:S(2)}) collective-permute-start(f32[8,64,128]{2,1,0:T(8,128)} %get-tuple-element.30), channel_id=1, source_target_pairs={{1,2},{2,1},{3,4},{4,3},{5,6},{6,5},{9,10},{10,9},{11,12},{12,11},... | collective-permute-start | bytes 786440 | tf_op jit(solution)/shard_map/ppermute | solution.py:749
  12.3 14.7 %collective-permute-done.ce_any = f32[8,64,128]{2,1,0:T(8,128)S(1)} collective-permute-done((f32[8,64,128]{2,1,0:T(8,128)}, f32[8,64,128]{2,1,0:T(8,128)S(1)}, u32[]{:S(2)}, u32[]{:S(2)}) %collective-permute-start) | collective-permute-done | bytes 262176 | tf_op jit(solution)/shard_map/ppermute | solution.py:746
  27.1 7.0 %collective-permute-done.1.co_any = f32[8,64,128]{2,1,0:T(8,128)S(1)} collective-permute-done((f32[8,64,128]{2,1,0:T(8,128)}, f32[8,64,128]{2,1,0:T(8,128)S(1)}, u32[]{:S(2)}, u32[]{:S(2)}) %collective-permute-start.1) | collective-permute-done | bytes 262176 | tf_op jit(solution)/shard_map/ppermute | solution.py:749
  34.8 2.2 %comb.1 = (f32[8,128,128]{2,1,0:T(8,128)}, f32[5,8,64,128]{3,2,1,0:T(8,128)}, f32[8,64,128]{2,1,0:T(8,128)}) custom-call(f32[8,64,128]{2,1,0:T(8,128)} %copy-done.7, f32[8,64,128]{2,1,0:T(8,128)} %copy-done.8, f32[5,8,64,128]{3,2,1,0:T(8,128)} %get-tuple-element.34.ev_in), custom_call_target="tpu_custom_call", output_to_operand_aliasing={{1}: (2, {})} | custom-call | tf_op jit(solution)/shard_map/comb/pallas_call | solution.py:782
  38.9 0.9 fusion
  40.5 1.0 copy-done.2
  41.5 18.6 %slots.1 = (f32[5,8,144,128]{3,2,1,0:T(8,128)}, f32[41,72,128]{2,1,0:T(8,128)}, f32[9,72,128]{2,1,0:T(8,128)}, f32[32,72,128]{2,1,0:T(8,128)}, f32[9,144,128]{2,1,0:T(8,128)}) custom-call(s32[4]{0:T(128)} %bitcast.18, s32[4]{0:T(128)} %bitcast.19, s32[1]{0:T(128)} %bitcast.11.count_ref, f32[8,128,512]{2,1,0:T(8,128)} %bitcast.15, ...), custom_call_target="tpu_custom_call" | custom-call | tf_op jit(solution)/shard_map/slots/pallas_call | solution.py:636
  60.0 5.2 %collective-permute-start.5 = (f32[41,72,128]{2,1,0:T(8,128)}, f32[41,72,128]{2,1,0:T(8,128)S(1)}, u32[]{:S(2)}, u32[]{:S(2)}) collective-permute-start(f32[41,72,128]{2,1,0:T(8,128)} %get-tuple-element.40), channel_id=1, source_target_pairs={{0,8},{8,0},{16,24},{24,16},{32,40},{40,32},{48,56},{56,48},{64,72... | collective-permute-start | bytes 4534280 | tf_op jit(solution)/shard_map/ppermute | solution.py:740
  66.0 1.7 %collective-permute-start.7 = (f32[32,72,128]{2,1,0:T(8,128)}, f32[32,72,128]{2,1,0:T(8,128)}, u32[]{:S(2)}, u32[]{:S(2)}) collective-permute-start(f32[32,72,128]{2,1,0:T(8,128)} %get-tuple-element.44), channel_id=1, source_target_pairs={{8,16},{16,8},{24,32},{32,24},{40,48},{48,40},{56,64},{64,56},{72,... | collective-permute-start | bytes 3538952 | tf_op jit(solution)/shard_map/ppermute | solution.py:743
  67.7 0.8 collective-permute-done.5.ev_any
  68.4 1.1 copy-done
  69.5 2.3 %sides.1 = (f32[9,72,128]{2,1,0:T(8,128)}, f32[9,72,128]{2,1,0:T(8,128)}) custom-call(f32[9,144,128]{2,1,0:T(8,128)} %get-tuple-element.47.own_any, f32[41,72,128]{2,1,0:T(8,128)} %copy-done, f32[9,72,128]{2,1,0:T(8,128)} %copy-done.1), custom_call_target="tpu_custom_call" | custom-call | tf_op jit(solution)/shard_map/sides/pallas_call | solution.py:821
  72.0 6.1 %collective-permute-start.9 = (f32[9,72,128]{2,1,0:T(8,128)}, f32[9,72,128]{2,1,0:T(8,128)S(1)}, u32[]{:S(2)}, u32[]{:S(2)}) collective-permute-start(f32[9,72,128]{2,1,0:T(8,128)} %get-tuple-element.49), channel_id=1, source_target_pairs={{1,2},{2,1},{3,4},{4,3},{5,6},{6,5},{9,10},{10,9},{11,12},{12,11},... | collective-permute-start | bytes 995336 | tf_op jit(solution)/shard_map/ppermute | solution.py:749
  78.1 0.8 copy.18.taps_ref
  78.9 2.6 %weights.1 = (bf16[3,128,240]{2,1,0:T(8,128)(2,1)}, bf16[3,64,256]{2,1,0:T(8,128)(2,1)}, f32[3,32,128]{2,1,0:T(8,128)}) custom-call(f32[3,3,32,12]{3,2,1,0:T(8,128)} %copy.18.taps_ref, f32[3,32]{1,0:T(4,128)} %bias_ref.1, f32[3,4,32]{2,1,0:T(4,128)} %map_ref.1, f32[3,4]{1,0:T(4,128)} %map_bias_ref.1), custom_call_target="tpu_custom_call" | custom-call | flops 1048576 | bytes 3145728 | tf_op jit(solution)/shard_map/weights/pallas_call | solution.py:668
  81.5 4.8 %merge.1 = (f32[5,560,128]{2,1,0:T(8,128)}, f32[5,560,128]{2,1,0:T(8,128)}) custom-call(f32[5,8,144,128]{3,2,1,0:T(8,128)} %get-tuple-element.39.u_any, f32[41,72,128]{2,1,0:T(8,128)} %copy-done, f32[9,72,128]{2,1,0:T(8,128)} %copy-done.1, f32[32,72,128]{2,1,0:T(8,128)} %collective-permute-done.7.odm_any), custom_call_target="tpu_custom_call" | custom-call | flops 1048576 | bytes 9437184 | tf_op jit(solution)/shard_map/merge/pallas_call | solution.py:681
  86.3 9.0 %collective-permute-done.8.ce_any = f32[9,72,128]{2,1,0:T(8,128)S(1)} collective-permute-done((f32[9,72,128]{2,1,0:T(8,128)}, f32[9,72,128]{2,1,0:T(8,128)S(1)}, u32[]{:S(2)}, u32[]{:S(2)}) %collective-permute-start.8) | collective-permute-done | bytes 331808 | tf_op jit(solution)/shard_map/ppermute | solution.py:746
  95.3 8.4 %collective-permute-done.9.co_any = f32[9,72,128]{2,1,0:T(8,128)S(1)} collective-permute-done((f32[9,72,128]{2,1,0:T(8,128)}, f32[9,72,128]{2,1,0:T(8,128)S(1)}, u32[]{:S(2)}, u32[]{:S(2)}) %collective-permute-start.9) | collective-permute-done | bytes 331808 | tf_op jit(solution)/shard_map/ppermute | solution.py:749
  103.7 0.7 copy-done.5
  104.5 21.6 %denoise.1 = f32[8,128,512]{2,1,0:T(8,128)} custom-call(f32[5,560,128]{2,1,0:T(8,128)} %get-tuple-element.45.low_any, f32[5,560,128]{2,1,0:T(8,128)} %get-tuple-element.46.up_any, f32[9,72,128]{2,1,0:T(8,128)} %copy-done.4, f32[9,72,128]{2,1,0:T(8,128)} %copy-done.5, bf16[3,128,240]{2,1,0:T(8,128)(2,1)} %get-tuple-element.50.conv_sc, ...), custom_call_target="tpu_custom_call" | custom-call | tf_op jit(solution)/shard_map/denoise/pallas_call | solution.py:696
  (29 shorter events, 3.5 us)
Async XLA Ops:
  3.2 30.9 %collective-permute-start.2 = (f32[4,8,64,128]{3,2,1,0:T(8,128)}, f32[4,8,64,128]{3,2,1,0:T(8,128)S(1)}, u32[]{:S(2)}, u32[]{:S(2)}) collective-permute-start(f32[4,8,64,128]{3,2,1,0:T(8,128)} %get-tuple-element.31), channel_id=1, source_target_pairs={{8,16},{16,8},{24,32},{32,24},{40,48},{48,40},{56,64},{64,56},{72,... | collective-permute-start | bytes 3145736 | tf_op jit(solution)/shard_map/ppermute | solution.py:743
  6.1 32.8 %copy-start.9 = (f32[128,128]{1,0:T(8,128)S(1)}, f32[128,128]{1,0:T(8,128)}, u32[]{:S(2)}) copy-start(f32[128,128]{1,0:T(8,128)} %param.17) | copy-start | bytes 196612
  6.1 21.0 %collective-permute-start = (f32[8,64,128]{2,1,0:T(8,128)}, f32[8,64,128]{2,1,0:T(8,128)S(1)}, u32[]{:S(2)}, u32[]{:S(2)}) collective-permute-start(f32[8,64,128]{2,1,0:T(8,128)} %get-tuple-element.29), channel_id=1, source_target_pairs={{0,1},{1,0},{2,3},{3,2},{4,5},{5,4},{6,7},{7,6},{8,9},{9,8},{10,11... | collective-permute-start | bytes 786440 | tf_op jit(solution)/shard_map/ppermute | solution.py:746
  7.1 27.0 %collective-permute-start.1 = (f32[8,64,128]{2,1,0:T(8,128)}, f32[8,64,128]{2,1,0:T(8,128)S(1)}, u32[]{:S(2)}, u32[]{:S(2)}) collective-permute-start(f32[8,64,128]{2,1,0:T(8,128)} %get-tuple-element.30), channel_id=1, source_target_pairs={{1,2},{2,1},{3,4},{4,3},{5,6},{6,5},{9,10},{10,9},{11,12},{12,11},... | collective-permute-start | bytes 786440 | tf_op jit(solution)/shard_map/ppermute | solution.py:749
  27.1 7.0 %copy-start.7 = (f32[8,64,128]{2,1,0:T(8,128)}, f32[8,64,128]{2,1,0:T(8,128)S(1)}, u32[]{:S(2)}) copy-start(f32[8,64,128]{2,1,0:T(8,128)S(1)} %collective-permute-done.ce_any) | copy-start | bytes 786436
  34.0 0.7 copy-start.8
  34.0 2.9 %copy-start.3 = (f32[4,8,64,128]{3,2,1,0:T(8,128)}, f32[4,8,64,128]{3,2,1,0:T(8,128)S(1)}, u32[]{:S(2)}) copy-start(f32[4,8,64,128]{3,2,1,0:T(8,128)S(1)} %collective-permute-done.2.odm_ref) | copy-start | bytes 3145732
  37.0 3.4 %collective-permute-start.3 = (f32[5,8,64,128]{3,2,1,0:T(8,128)}, f32[5,8,64,128]{3,2,1,0:T(8,128)S(1)}, u32[]{:S(2)}, u32[]{:S(2)}) collective-permute-start(f32[5,8,64,128]{3,2,1,0:T(8,128)} %get-tuple-element.36), channel_id=1, source_target_pairs={{0,8},{8,0},{16,24},{24,16},{32,40},{40,32},{48,56},{56,48},{64,72... | collective-permute-start | bytes 3932168 | tf_op jit(solution)/shard_map/ppermute | solution.py:740
  37.5 2.2 %collective-permute-start.4 = (f32[8,64,128]{2,1,0:T(8,128)}, f32[8,64,128]{2,1,0:T(8,128)S(1)}, u32[]{:S(2)}, u32[]{:S(2)}) collective-permute-start(f32[8,64,128]{2,1,0:T(8,128)} %get-tuple-element.37), channel_id=1, source_target_pairs={{8,16},{16,8},{24,32},{32,24},{40,48},{48,40},{56,64},{64,56},{72,... | collective-permute-start | bytes 786440 | tf_op jit(solution)/shard_map/ppermute | solution.py:743
  39.8 0.7 copy-start.6
  40.4 1.1 copy-start.2
  60.0 18.0 %copy-start.10 = (f32[3,9,32,4]{2,3,1,0:T(4,128)S(1)}, f32[3,9,32,4]{2,3,1,0:T(4,128)}, u32[]{:S(2)}) copy-start(f32[3,9,32,4]{2,3,1,0:T(4,128)} %param.22) | copy-start | bytes 41476
  60.0 8.4 %collective-permute-start.5 = (f32[41,72,128]{2,1,0:T(8,128)}, f32[41,72,128]{2,1,0:T(8,128)S(1)}, u32[]{:S(2)}, u32[]{:S(2)}) collective-permute-start(f32[41,72,128]{2,1,0:T(8,128)} %get-tuple-element.40), channel_id=1, source_target_pairs={{0,8},{8,0},{16,24},{24,16},{32,40},{40,32},{48,56},{56,48},{64,72... | collective-permute-start | bytes 4534280 | tf_op jit(solution)/shard_map/ppermute | solution.py:740
  65.3 0.7 collective-permute-start.6
  66.0 2.5 %copy-start.1 = (f32[9,72,128]{2,1,0:T(8,128)}, f32[9,72,128]{2,1,0:T(8,128)S(1)}, u32[]{:S(2)}) copy-start(f32[9,72,128]{2,1,0:T(8,128)S(1)} %collective-permute-done.6.odc_any) | copy-start | bytes 995332
  66.0 15.5 %collective-permute-start.7 = (f32[32,72,128]{2,1,0:T(8,128)}, f32[32,72,128]{2,1,0:T(8,128)}, u32[]{:S(2)}, u32[]{:S(2)}) collective-permute-start(f32[32,72,128]{2,1,0:T(8,128)} %get-tuple-element.44), channel_id=1, source_target_pairs={{8,16},{16,8},{24,32},{32,24},{40,48},{48,40},{56,64},{64,56},{72,... | collective-permute-start | bytes 3538952 | tf_op jit(solution)/shard_map/ppermute | solution.py:743
  68.4 1.1 copy-start
  71.9 23.4 %collective-permute-start.8 = (f32[9,72,128]{2,1,0:T(8,128)}, f32[9,72,128]{2,1,0:T(8,128)S(1)}, u32[]{:S(2)}, u32[]{:S(2)}) collective-permute-start(f32[9,72,128]{2,1,0:T(8,128)} %get-tuple-element.48), channel_id=1, source_target_pairs={{0,1},{1,0},{2,3},{3,2},{4,5},{5,4},{6,7},{7,6},{8,9},{9,8},{10,11... | collective-permute-start | bytes 995336 | tf_op jit(solution)/shard_map/ppermute | solution.py:746
  72.0 31.7 %collective-permute-start.9 = (f32[9,72,128]{2,1,0:T(8,128)}, f32[9,72,128]{2,1,0:T(8,128)S(1)}, u32[]{:S(2)}, u32[]{:S(2)}) collective-permute-start(f32[9,72,128]{2,1,0:T(8,128)} %get-tuple-element.49), channel_id=1, source_target_pairs={{1,2},{2,1},{3,4},{4,3},{5,6},{6,5},{9,10},{10,9},{11,12},{12,11},... | collective-permute-start | bytes 995336 | tf_op jit(solution)/shard_map/ppermute | solution.py:749
  95.3 8.5 %copy-start.4 = (f32[9,72,128]{2,1,0:T(8,128)}, f32[9,72,128]{2,1,0:T(8,128)S(1)}, u32[]{:S(2)}) copy-start(f32[9,72,128]{2,1,0:T(8,128)S(1)} %collective-permute-done.8.ce_any) | copy-start | bytes 995332
  103.7 0.7 copy-start.5

commit v8 on v6

--- a/solution.py
+++ b/solution.py
@@ -120,7 +120,8 @@
     right_f_any,
     right_b_any,
     u_ref,
-    out_ev,
+    out_evc,
+    out_evm,
     out_odc,
     out_odm,
     own_ref,
@@ -309,10 +310,10 @@
     ]
     for t in range(4):
         moves.append((accum.at[t, :, pl.ds(od_from, STRIP), :], out_odm.at[8 * t : 8 * t + 8]))
-    moves.append((accum.at[4, :, pl.ds(ev_from, STRIP), :], out_ev.at[0:8]))
-    moves.append((extra.at[pl.ds(ev_from, STRIP), :], out_ev.at[8]))
+    moves.append((accum.at[4, :, pl.ds(ev_from, STRIP), :], out_evc.at[0:8]))
+    moves.append((extra.at[pl.ds(ev_from, STRIP), :], out_evc.at[8]))
     for t in range(4):
-        moves.append((accum.at[t, :, pl.ds(ev_from, STRIP), :], out_ev.at[9 + 8 * t : 17 + 8 * t]))
+        moves.append((accum.at[t, :, pl.ds(ev_from, STRIP), :], out_evm.at[8 * t : 8 * t + 8]))
     moves.append((accum.at[4, :, 56:200, :], own_ref.at[0:8]))
     moves.append((extra.at[56:200, :], own_ref.at[8]))
     sent = [pltpu.make_async_copy(src, dst, sems.at[12 + i]) for i, (src, dst) in enumerate(moves)]
@@ -327,10 +328,10 @@
         item.wait()
 
 
-def sides_kernel(own_any, ev_any, odc_any, ce_ref, co_ref, own_ref, evc_ref, odc_ref, sems):
+def sides_kernel(own_any, evc_any, odc_any, ce_ref, co_ref, own_ref, evc_ref, odc_ref, sems):
     started = [
         pltpu.make_async_copy(own_any, own_ref, sems.at[0]),
-        pltpu.make_async_copy(ev_any.at[0:9], evc_ref, sems.at[1]),
+        pltpu.make_async_copy(evc_any, evc_ref, sems.at[1]),
         pltpu.make_async_copy(odc_any, odc_ref, sems.at[2]),
     ]
     for item in started:
@@ -399,10 +400,11 @@
         bias_out[layer] = jnp.broadcast_to(out_bias, (32, LANE))
 
 
-def merge_kernel(u_any, ev_any, odc_any, odm_any, low_st, up_st, u_ref, ev_ref, od_ref, sems):
+def merge_kernel(u_any, evc_any, evm_any, odc_any, odm_any, low_st, up_st, u_ref, ev_ref, od_ref, sems):
     pairs = (
         (u_any, u_ref),
-        (ev_any, ev_ref),
+        (evc_any, ev_ref.at[0:9]),
+        (evm_any, ev_ref.at[9:41]),
         (odc_any, od_ref.at[0:9]),
         (odm_any, od_ref.at[9:41]),
     )
@@ -635,13 +637,14 @@
         slots_kernel,
         out_shape=[
             sds(TILES, 8, BAND, LANE),
-            sds(41, STRIP, LANE),
+            sds(9, STRIP, LANE),
+            sds(32, STRIP, LANE),
             sds(9, STRIP, LANE),
             sds(32, STRIP, LANE),
             sds(9, BAND, LANE),
         ],
         in_specs=[smem()] * 3 + [anywhere] * 5 + [vmem()] * 3 + [anywhere] * 4,
-        out_specs=[anywhere] * 5,
+        out_specs=[anywhere] * 6,
         scratch_shapes=[
             pltpu.VMEM((TILES, 8, 256, LANE), f32),
             pltpu.VMEM((TILES, 8, 256, LANE), f32),
@@ -660,7 +663,7 @@
     )(*operands)
 
 
-def denoise_call(u, ev, odc, odm, ce, co, taps, conv_bias, output_weight, output_bias):
+def denoise_call(u, evc, evm, odc, odm, ce, co, taps, conv_bias, output_weight, output_bias):
     anywhere = pl.BlockSpec(memory_space=pl.ANY)
     lines = sds(TILES, 4 * ROWS_KEPT, LANE)
     conv_parts, map_parts, out_bias = pl.pallas_call(
@@ -679,18 +682,18 @@
     low, up = pl.pallas_call(
         merge_kernel,
         out_shape=[lines] * 2,
-        in_specs=[anywhere] * 4,
+        in_specs=[anywhere] * 5,
         out_specs=[vmem()] * 2,
         scratch_shapes=[
             pltpu.VMEM((TILES, 8, BAND, LANE), f32),
             pltpu.VMEM((41, STRIP, LANE), f32),
             pltpu.VMEM((41, STRIP, LANE), f32),
-            pltpu.SemaphoreType.DMA((4,)),
+            pltpu.SemaphoreType.DMA((5,)),
         ],
         compiler_params=params(62),
         cost_estimate=pl.CostEstimate(flops=1 << 20, bytes_accessed=9 << 20, transcendentals=0),
         name="merge",
-    )(u, ev, odc, odm)
+    )(u, evc, evm, odc, odm)
     return pl.pallas_call(
         denoise_kernel,
         out_shape=sds(8, 128, 512),
@@ -795,7 +798,7 @@
     phase_re = jnp.cos(propagator_phase)
     phase_im = jnp.sin(propagator_phase)
     tables = [jnp.asarray(m) for m in dft_matrices()]
-    u, ev, odc, odm, own = slots_call(
+    u, evc, evm, odc, odm, own = slots_call(
         position_rows.reshape(-1),
         position_cols.reshape(-1),
         tile_counts.reshape(-1),
@@ -812,7 +815,8 @@
     odc = row_od(odc)
     odm, odc = lax.optimization_barrier((odm, odc))
     odm = row_od(odm)
-    ev = row_ev(ev)
+    evc = row_ev(evc)
+    evm = row_ev(evm)
     ce, co = pl.pallas_call(
         sides_kernel,
         out_shape=[sds(9, STRIP, LANE)] * 2,
@@ -826,11 +830,11 @@
         ],
         compiler_params=params(62),
         name="sides",
-    )(own, ev, odc)
+    )(own, evc, odc)
     ce = col_ev(ce)
     co = col_od(co)
     taps = conv_weight.reshape(3, 3, 3, 32, 4).transpose(0, 1, 3, 2, 4).reshape(3, 3, 32, 12)
-    out = denoise_call(u, ev, odc, odm, ce, co, taps, conv_bias, output_weight, output_bias)
+    out = denoise_call(u, evc, evm, odc, odm, ce, co, taps, conv_bias, output_weight, output_bias)
     return out.reshape(4, 2, 128, 512)
 
 

time: 125 us -> 131 us (1.048)
  the two profiles are of different devices: /device:TPU:97 before, /device:TPU:96 now
where the time goes in v8:
time: 131 us; the launch traced here: 130 us
  Pallas kernels  57.5 us (44%)
  starting transfers between devices  40.5 us (31%)
  waiting for transfers between devices  25.4 us (19%)
  local copies, waits for them, and re-layouts  5.94 us (5%)
    ppermute x3, starting transfers between devices, row_ev(): return lax.ppermute(x, 'row', pairs(rows, 0))  24.9 us
    pallas_call x1, Pallas kernels, denoise_call(): pl.pallas_call(denoise_kernel, out_shape=sds(8, 128, 512), in_specs=[anyw...  21.6 us
    pallas_call x1, Pallas kernels, slots_call(): pl.pallas_call(slots_kernel, out_shape=[sds(TILES, 8, BAND, LANE), sds(9,...  18.5 us
    ppermute x2, waiting for transfers between devices, col_od(): return lax.ppermute(x, 'col', pairs(cols, 1))  16.4 us
    ppermute x2, starting transfers between devices, col_od(): return lax.ppermute(x, 'col', pairs(cols, 1))  8.19 us
    ppermute x2, waiting for transfers between devices, col_ev(): return lax.ppermute(x, 'col', pairs(cols, 0))  7.49 us
    pallas_call x1, Pallas kernels, denoise_call(): pl.pallas_call(merge_kernel, out_shape=[lines] * 2, in_specs=[anywhere] *...  4.8 us
    unnamed x20, local copies, waits for them, and re-layouts  4.23 us
  transfers between devices with their start and end apart: 10, of which 5 were waited for; matrix products, arithmetic and copies ran while one was open for 1% of the time, Pallas kernels for 10%

profile of v8, /device:TPU:96, one launch (start us, length us, event | category | flops | bytes accessed | tf_op | source)
XLA Modules:
  0.0 130.3 jit_solution(2055556793869205447)
XLA Ops:
  0.0 2.2 %pack.1 = (f32[8,64,128]{2,1,0:T(8,128)}, f32[8,64,128]{2,1,0:T(8,128)}) custom-call(f32[8,128,512]{2,1,0:T(8,128)} %bitcast.12, f32[8,128,512]{2,1,0:T(8,128)} %bitcast.13), custom_call_target="tpu_custom_call" | custom-call | tf_op jit(solution)/shard_map/pack/pallas_call | solution.py:759
  2.2 3.2 %collective-permute-start = (f32[8,64,128]{2,1,0:T(8,128)}, f32[8,64,128]{2,1,0:T(8,128)S(1)}, u32[]{:S(2)}, u32[]{:S(2)}) collective-permute-start(f32[8,64,128]{2,1,0:T(8,128)} %get-tuple-element.27), channel_id=1, source_target_pairs={{0,1},{1,0},{2,3},{3,2},{4,5},{5,4},{6,7},{7,6},{8,9},{9,8},{10,11... | collective-permute-start | bytes 786440 | tf_op jit(solution)/shard_map/ppermute | solution.py:747
  5.4 2.1 %collective-permute-start.1 = (f32[8,64,128]{2,1,0:T(8,128)}, f32[8,64,128]{2,1,0:T(8,128)S(1)}, u32[]{:S(2)}, u32[]{:S(2)}) collective-permute-start(f32[8,64,128]{2,1,0:T(8,128)} %get-tuple-element.28), channel_id=1, source_target_pairs={{1,2},{2,1},{3,4},{4,3},{5,6},{6,5},{9,10},{10,9},{11,12},{12,11},... | collective-permute-start | bytes 786440 | tf_op jit(solution)/shard_map/ppermute | solution.py:750
  7.5 3.2 %strips.1 = (f32[5,8,64,128]{3,2,1,0:T(8,128)}, f32[5,8,64,128]{3,2,1,0:T(8,128)}) custom-call(f32[8,128,512]{2,1,0:T(8,128)} %bitcast.14), custom_call_target="tpu_custom_call" | custom-call | bytes 4194304 | tf_op jit(solution)/shard_map/strips/pallas_call | solution.py:772
  10.7 1.7 %collective-permute-done.ce_any = f32[8,64,128]{2,1,0:T(8,128)S(1)} collective-permute-done((f32[8,64,128]{2,1,0:T(8,128)}, f32[8,64,128]{2,1,0:T(8,128)S(1)}, u32[]{:S(2)}, u32[]{:S(2)}) %collective-permute-start) | collective-permute-done | bytes 262176 | tf_op jit(solution)/shard_map/ppermute | solution.py:747
  12.4 5.2 %collective-permute-done.1.co_any = f32[8,64,128]{2,1,0:T(8,128)S(1)} collective-permute-done((f32[8,64,128]{2,1,0:T(8,128)}, f32[8,64,128]{2,1,0:T(8,128)S(1)}, u32[]{:S(2)}, u32[]{:S(2)}) %collective-permute-start.1) | collective-permute-done | bytes 262176 | tf_op jit(solution)/shard_map/ppermute | solution.py:750
  18.4 2.2 %comb.1 = (f32[8,128,128]{2,1,0:T(8,128)}, f32[5,8,64,128]{3,2,1,0:T(8,128)}, f32[5,8,64,128]{3,2,1,0:T(8,128)}) custom-call(f32[8,64,128]{2,1,0:T(8,128)} %copy-done.6, f32[8,64,128]{2,1,0:T(8,128)} %copy-done.7, f32[5,8,64,128]{3,2,1,0:T(8,128)} %get-tuple-element.29.ev_in, ...), custom_call_target="tpu_custom_call", output_to_operand_aliasing={{1}: (2, {}), {2}: (3, {})} | custom-call | tf_op jit(solution)/shard_map/comb/pallas_call | solution.py:781
  20.7 1.7 %collective-permute-start.3 = (f32[5,8,64,128]{3,2,1,0:T(8,128)}, f32[5,8,64,128]{3,2,1,0:T(8,128)}, u32[]{:S(2)}, u32[]{:S(2)}) collective-permute-start(f32[5,8,64,128]{3,2,1,0:T(8,128)} %get-tuple-element.33), channel_id=1, source_target_pairs={{8,16},{16,8},{24,32},{32,24},{40,48},{48,40},{56,64},{64,56},{72,... | collective-permute-start | bytes 3932168 | tf_op jit(solution)/shard_map/ppermute | solution.py:744
  23.1 0.9 fusion
  24.0 1.0 copy-done.2
  25.0 18.5 %slots.1 = (f32[5,8,144,128]{3,2,1,0:T(8,128)}, f32[9,72,128]{2,1,0:T(8,128)}, f32[32,72,128]{2,1,0:T(8,128)}, f32[9,72,128]{2,1,0:T(8,128)}, f32[32,72,128]{2,1,0:T(8,128)}, /*index=5*/f32[9,144,128]{2,1,0:T(8,128)}) custom-call(s32[4]{0:T(128)} %bitcast.18, s32[4]{0:T(128)} %bitcast.19, s32[1]{0:T(128)} %bitcast.11.count_ref, f32[8,128,512]{2,1,0:T(8,128)} %bitcast.15, ...), custom_call_target="tpu_custom_call" | custom-call | tf_op jit(solution)/shard_map/slots/pallas_call | solution.py:636
  43.6 0.8 collective-permute-start.6
  44.4 17.8 %collective-permute-start.5 = (f32[32,72,128]{2,1,0:T(8,128)}, f32[32,72,128]{2,1,0:T(8,128)S(1)}, u32[]{:S(2)}, u32[]{:S(2)}) collective-permute-start(f32[32,72,128]{2,1,0:T(8,128)} %get-tuple-element.36), channel_id=1, source_target_pairs={{0,8},{8,0},{16,24},{24,16},{32,40},{40,32},{48,56},{56,48},{64,72... | collective-permute-start | bytes 3538952 | tf_op jit(solution)/shard_map/ppermute | solution.py:741
  62.2 1.7 %collective-permute-start.7 = (f32[32,72,128]{2,1,0:T(8,128)}, f32[32,72,128]{2,1,0:T(8,128)}, u32[]{:S(2)}, u32[]{:S(2)}) collective-permute-start(f32[32,72,128]{2,1,0:T(8,128)} %get-tuple-element.40), channel_id=1, source_target_pairs={{8,16},{16,8},{24,32},{32,24},{40,48},{48,40},{56,64},{64,56},{72,... | collective-permute-start | bytes 3538952 | tf_op jit(solution)/shard_map/ppermute | solution.py:744
  63.9 7.0 %collective-permute-start.4 = (f32[9,72,128]{2,1,0:T(8,128)}, f32[9,72,128]{2,1,0:T(8,128)S(1)}, u32[]{:S(2)}, u32[]{:S(2)}) collective-permute-start(f32[9,72,128]{2,1,0:T(8,128)} %get-tuple-element.35), channel_id=1, source_target_pairs={{0,8},{8,0},{16,24},{24,16},{32,40},{40,32},{48,56},{56,48},{64,72... | collective-permute-start | bytes 995336 | tf_op jit(solution)/shard_map/ppermute | solution.py:741
  70.8 1.5 %collective-permute-done.4.evc_any = f32[9,72,128]{2,1,0:T(8,128)S(1)} collective-permute-done((f32[9,72,128]{2,1,0:T(8,128)}, f32[9,72,128]{2,1,0:T(8,128)S(1)}, u32[]{:S(2)}, u32[]{:S(2)}) %collective-permute-start.4) | collective-permute-done | bytes 331808 | tf_op jit(solution)/shard_map/ppermute | solution.py:741
  73.0 2.3 %sides.1 = (f32[9,72,128]{2,1,0:T(8,128)}, f32[9,72,128]{2,1,0:T(8,128)}) custom-call(f32[9,144,128]{2,1,0:T(8,128)} %get-tuple-element.43.own_any, f32[9,72,128]{2,1,0:T(8,128)} %copy-done.1, f32[9,72,128]{2,1,0:T(8,128)} %copy-done), custom_call_target="tpu_custom_call" | custom-call | tf_op jit(solution)/shard_map/sides/pallas_call | solution.py:820
  75.5 6.1 %collective-permute-start.9 = (f32[9,72,128]{2,1,0:T(8,128)}, f32[9,72,128]{2,1,0:T(8,128)S(1)}, u32[]{:S(2)}, u32[]{:S(2)}) collective-permute-start(f32[9,72,128]{2,1,0:T(8,128)} %get-tuple-element.45), channel_id=1, source_target_pairs={{1,2},{2,1},{3,4},{4,3},{5,6},{6,5},{9,10},{10,9},{11,12},{12,11},... | collective-permute-start | bytes 995336 | tf_op jit(solution)/shard_map/ppermute | solution.py:750
  82.4 2.6 %weights.1 = (bf16[3,128,240]{2,1,0:T(8,128)(2,1)}, bf16[3,64,256]{2,1,0:T(8,128)(2,1)}, f32[3,32,128]{2,1,0:T(8,128)}) custom-call(f32[3,3,32,12]{3,2,1,0:T(8,128)} %copy.19.taps_ref, f32[3,32]{1,0:T(4,128)} %bias_ref.1, f32[3,4,32]{2,1,0:T(4,128)} %map_ref.1, f32[3,4]{1,0:T(4,128)} %map_bias_ref.1), custom_call_target="tpu_custom_call" | custom-call | flops 1048576 | bytes 3145728 | tf_op jit(solution)/shard_map/weights/pallas_call | solution.py:669
  85.0 1.0 copy-done.3
  86.0 4.8 %merge.1 = (f32[5,560,128]{2,1,0:T(8,128)}, f32[5,560,128]{2,1,0:T(8,128)}) custom-call(f32[5,8,144,128]{3,2,1,0:T(8,128)} %get-tuple-element.34.u_any, f32[9,72,128]{2,1,0:T(8,128)} %copy-done.1, f32[32,72,128]{2,1,0:T(8,128)} %copy-done.3, f32[9,72,128]{2,1,0:T(8,128)} %copy-done, f32[32,72,128]{2,1,0:T(8,128)} %collective-permute-done.7.odm_any), custom_call_target="tpu_custom_call" | custom-call | flops 1048576 | bytes 9437184 | tf_op jit(solution)/shard_map/merge/pallas_call | solution.py:682
  90.8 5.8 %collective-permute-done.8.ce_any = f32[9,72,128]{2,1,0:T(8,128)S(1)} collective-permute-done((f32[9,72,128]{2,1,0:T(8,128)}, f32[9,72,128]{2,1,0:T(8,128)S(1)}, u32[]{:S(2)}, u32[]{:S(2)}) %collective-permute-start.8) | collective-permute-done | bytes 331808 | tf_op jit(solution)/shard_map/ppermute | solution.py:747
  96.6 11.2 %collective-permute-done.9.co_any = f32[9,72,128]{2,1,0:T(8,128)S(1)} collective-permute-done((f32[9,72,128]{2,1,0:T(8,128)}, f32[9,72,128]{2,1,0:T(8,128)S(1)}, u32[]{:S(2)}, u32[]{:S(2)}) %collective-permute-start.9) | collective-permute-done | bytes 331808 | tf_op jit(solution)/shard_map/ppermute | solution.py:750
  108.5 21.6 %denoise.1 = f32[8,128,512]{2,1,0:T(8,128)} custom-call(f32[5,560,128]{2,1,0:T(8,128)} %get-tuple-element.41.low_any, f32[5,560,128]{2,1,0:T(8,128)} %get-tuple-element.42.up_any, f32[9,72,128]{2,1,0:T(8,128)} %copy-done.4, f32[9,72,128]{2,1,0:T(8,128)} %copy-done.5, bf16[3,128,240]{2,1,0:T(8,128)(2,1)} %get-tuple-element.46.conv_sc, ...), custom_call_target="tpu_custom_call" | custom-call | tf_op jit(solution)/shard_map/denoise/pallas_call | solution.py:697
  (27 shorter events, 3.2 us)
Async XLA Ops:
  2.2 10.2 %collective-permute-start = (f32[8,64,128]{2,1,0:T(8,128)}, f32[8,64,128]{2,1,0:T(8,128)S(1)}, u32[]{:S(2)}, u32[]{:S(2)}) collective-permute-start(f32[8,64,128]{2,1,0:T(8,128)} %get-tuple-element.27), channel_id=1, source_target_pairs={{0,1},{1,0},{2,3},{3,2},{4,5},{5,4},{6,7},{7,6},{8,9},{9,8},{10,11... | collective-permute-start | bytes 786440 | tf_op jit(solution)/shard_map/ppermute | solution.py:747
  5.4 12.3 %collective-permute-start.1 = (f32[8,64,128]{2,1,0:T(8,128)}, f32[8,64,128]{2,1,0:T(8,128)S(1)}, u32[]{:S(2)}, u32[]{:S(2)}) collective-permute-start(f32[8,64,128]{2,1,0:T(8,128)} %get-tuple-element.28), channel_id=1, source_target_pairs={{1,2},{2,1},{3,4},{4,3},{5,6},{6,5},{9,10},{10,9},{11,12},{12,11},... | collective-permute-start | bytes 786440 | tf_op jit(solution)/shard_map/ppermute | solution.py:750
  12.4 5.2 %copy-start.6 = (f32[8,64,128]{2,1,0:T(8,128)}, f32[8,64,128]{2,1,0:T(8,128)S(1)}, u32[]{:S(2)}) copy-start(f32[8,64,128]{2,1,0:T(8,128)S(1)} %collective-permute-done.ce_any) | copy-start | bytes 786436
  17.7 0.7 copy-start.7
  18.4 4.7 %copy-start.8 = (f32[128,128]{1,0:T(8,128)S(1)}, f32[128,128]{1,0:T(8,128)}, u32[]{:S(2)}) copy-start(f32[128,128]{1,0:T(8,128)} %param.17) | copy-start | bytes 196612
  20.6 3.4 %collective-permute-start.2 = (f32[5,8,64,128]{3,2,1,0:T(8,128)}, f32[5,8,64,128]{3,2,1,0:T(8,128)S(1)}, u32[]{:S(2)}, u32[]{:S(2)}) collective-permute-start(f32[5,8,64,128]{3,2,1,0:T(8,128)} %get-tuple-element.32), channel_id=1, source_target_pairs={{0,8},{8,0},{16,24},{24,16},{32,40},{40,32},{48,56},{56,48},{64,72... | collective-permute-start | bytes 3932168 | tf_op jit(solution)/shard_map/ppermute | solution.py:741
  20.7 3.3 %collective-permute-start.3 = (f32[5,8,64,128]{3,2,1,0:T(8,128)}, f32[5,8,64,128]{3,2,1,0:T(8,128)}, u32[]{:S(2)}, u32[]{:S(2)}) collective-permute-start(f32[5,8,64,128]{3,2,1,0:T(8,128)} %get-tuple-element.33), channel_id=1, source_target_pairs={{8,16},{16,8},{24,32},{32,24},{40,48},{48,40},{56,64},{64,56},{72,... | collective-permute-start | bytes 3932168 | tf_op jit(solution)/shard_map/ppermute | solution.py:744
  24.0 1.1 copy-start.2
  43.5 38.1 %copy-start.9 = (f32[3,9,32,4]{2,3,1,0:T(4,128)S(1)}, f32[3,9,32,4]{2,3,1,0:T(4,128)}, u32[]{:S(2)}) copy-start(f32[3,9,32,4]{2,3,1,0:T(4,128)} %param.22) | copy-start | bytes 41476
  43.6 18.7 %collective-permute-start.6 = (f32[9,72,128]{2,1,0:T(8,128)}, f32[9,72,128]{2,1,0:T(8,128)S(1)}, u32[]{:S(2)}, u32[]{:S(2)}) collective-permute-start(f32[9,72,128]{2,1,0:T(8,128)} %get-tuple-element.38), channel_id=1, source_target_pairs={{8,16},{16,8},{24,32},{32,24},{40,48},{48,40},{56,64},{64,56},{72,... | collective-permute-start | bytes 995336 | tf_op jit(solution)/shard_map/ppermute | solution.py:744
  44.4 40.6 %collective-permute-start.5 = (f32[32,72,128]{2,1,0:T(8,128)}, f32[32,72,128]{2,1,0:T(8,128)S(1)}, u32[]{:S(2)}, u32[]{:S(2)}) collective-permute-start(f32[32,72,128]{2,1,0:T(8,128)} %get-tuple-element.36), channel_id=1, source_target_pairs={{0,8},{8,0},{16,24},{24,16},{32,40},{40,32},{48,56},{56,48},{64,72... | collective-permute-start | bytes 3538952 | tf_op jit(solution)/shard_map/ppermute | solution.py:741
  62.2 10.1 %copy-start = (f32[9,72,128]{2,1,0:T(8,128)}, f32[9,72,128]{2,1,0:T(8,128)S(1)}, u32[]{:S(2)}) copy-start(f32[9,72,128]{2,1,0:T(8,128)S(1)} %collective-permute-done.6.odc_any) | copy-start | bytes 995332
  62.2 22.8 %collective-permute-start.7 = (f32[32,72,128]{2,1,0:T(8,128)}, f32[32,72,128]{2,1,0:T(8,128)}, u32[]{:S(2)}, u32[]{:S(2)}) collective-permute-start(f32[32,72,128]{2,1,0:T(8,128)} %get-tuple-element.40), channel_id=1, source_target_pairs={{8,16},{16,8},{24,32},{32,24},{40,48},{48,40},{56,64},{64,56},{72,... | collective-permute-start | bytes 3538952 | tf_op jit(solution)/shard_map/ppermute | solution.py:744
  63.9 8.4 %collective-permute-start.4 = (f32[9,72,128]{2,1,0:T(8,128)}, f32[9,72,128]{2,1,0:T(8,128)S(1)}, u32[]{:S(2)}, u32[]{:S(2)}) collective-permute-start(f32[9,72,128]{2,1,0:T(8,128)} %get-tuple-element.35), channel_id=1, source_target_pairs={{0,8},{8,0},{16,24},{24,16},{32,40},{40,32},{48,56},{56,48},{64,72... | collective-permute-start | bytes 995336 | tf_op jit(solution)/shard_map/ppermute | solution.py:741
  72.3 0.7 copy-start.1
  75.4 21.2 %collective-permute-start.8 = (f32[9,72,128]{2,1,0:T(8,128)}, f32[9,72,128]{2,1,0:T(8,128)S(1)}, u32[]{:S(2)}, u32[]{:S(2)}) collective-permute-start(f32[9,72,128]{2,1,0:T(8,128)} %get-tuple-element.44), channel_id=1, source_target_pairs={{0,1},{1,0},{2,3},{3,2},{4,5},{5,4},{6,7},{7,6},{8,9},{9,8},{10,11... | collective-permute-start | bytes 995336 | tf_op jit(solution)/shard_map/ppermute | solution.py:747
  75.5 32.3 %collective-permute-start.9 = (f32[9,72,128]{2,1,0:T(8,128)}, f32[9,72,128]{2,1,0:T(8,128)S(1)}, u32[]{:S(2)}, u32[]{:S(2)}) collective-permute-start(f32[9,72,128]{2,1,0:T(8,128)} %get-tuple-element.45), channel_id=1, source_target_pairs={{1,2},{2,1},{3,4},{4,3},{5,6},{6,5},{9,10},{10,9},{11,12},{12,11},... | collective-permute-start | bytes 995336 | tf_op jit(solution)/shard_map/ppermute | solution.py:750
  85.0 1.0 copy-start.3
  96.6 11.2 %copy-start.4 = (f32[9,72,128]{2,1,0:T(8,128)}, f32[9,72,128]{2,1,0:T(8,128)S(1)}, u32[]{:S(2)}) copy-start(f32[9,72,128]{2,1,0:T(8,128)S(1)} %collective-permute-done.8.ce_any) | copy-start | bytes 995332
  107.8 0.7 copy-start.5
